TPU v7x, 128 devices: a whole 4x4x4 slice. The times are simulated.
128 devices in a mesh: dp: 16 (over x_hi, z, core), space: 8 (over x_lo, y).
Axes of the slice: x: 4 (x_hi: 2, x_lo: 2; x = x_hi * 2 + x_lo), y: 4, z: 4, core: 2. Of those that a mesh axis runs over, the one named last changes fastest.
Arguments:
- query: bfloat16 [16, 3072, 1536], P('dp', 'space'), may hold values from -8 to 8
- key_in: bfloat16 [16, 3072, 1536], P('dp', 'space'), may hold values from -8 to 8
- value_in: bfloat16 [16, 3072, 1536], P('dp', 'space'), may hold values from -6 to 6
- out_weight: bfloat16 [1536, 3072], P('dp'), may hold values from -0.15625 to 0.15625
- grad_out: bfloat16 [16, 3072, 3072], P('dp', 'space'), may hold values from -6 to 6
- neighbours: int32 [8, 3], replicated, may hold values from -1 to 7, as said below
Outputs:
- mixed: bfloat16 [16, 3072, 3072], P('dp', 'space')
- grad_query: bfloat16 [16, 3072, 1536], P('dp', 'space')
- grad_key: bfloat16 [16, 3072, 1536], P('dp', 'space')
- grad_value: bfloat16 [16, 3072, 1536], P('dp', 'space')
- grad_weight: float32 [1536, 3072], P('dp')
Inputs may be any that keep to these rules, and one draw needn't show every extreme that they name: `neighbours`: entry 0 of row t is t; entry 1 is t - 1 or -1; entry 2 is t + 1 or -1.
All inputs are finite; a program needn't handle non-finite values.
Results may differ from a plain program's by a relative error of at most 0.034.
Values may be sent and summed in bfloat16 or wider, within the bound.
No kernel may reach another device: no remote copies, remote signals or barrier semaphores. Data moves between devices by JAX's collectives and lax.ppermute only.
A program may use at most 192 MiB of HBM per device.

v0:
```python
import math

import jax
import jax.numpy as jnp
from jax import lax
from jax.sharding import PartitionSpec as P

HEAD = 128


masked_score = -1e30


def padded(x, sides, width):
    for axis, dim in sides:
        size, length = (lax.axis_size(axis), x.shape[dim])
        up = [(i, (i + 1) % size) for i in range(size - 1)]
        down = [(j, i) for i, j in up]
        last = lax.slice_in_dim(x, length - width, length, axis=dim)
        initial = lax.slice_in_dim(x, 0, width, axis=dim)
        before = lax.ppermute(last, axis, up)
        after = lax.ppermute(initial, axis, down)
        x = jnp.concatenate([before, x, after], axis=dim)
    return x


def on_device(query, key_in, value_in, out_weight, grad_out, neighbours):
    query_rows = query[0]
    key_rows = key_in[0]
    value_rows = value_in[0]
    upstream = grad_out[0]
    tile_rows, model_cols = query_rows.shape
    head_count = model_cols // HEAD
    score_scale = 1.0 / math.sqrt(HEAD)
    tile_total = neighbours.shape[0]
    device_tile = lax.axis_index("space")
    window_tiles = device_tile - 1 + jnp.arange(3, dtype=jnp.int32)
    own_list = neighbours[device_tile]
    key_live = jnp.any(
        (own_list[None, :] == window_tiles[:, None]) & (own_list[None, :] >= 0), axis=1
    )
    inside = (window_tiles >= 0) & (window_tiles < tile_total)
    their_lists = neighbours[jnp.clip(window_tiles, 0, tile_total - 1)]
    query_live = inside & jnp.any(their_lists == device_tile, axis=1)
    key_mask = jnp.repeat(key_live, tile_rows)
    query_mask = jnp.repeat(query_live, tile_rows)
    key_value = jnp.stack([key_rows, value_rows])
    kv_near = padded(key_value, (("space", 1),), tile_rows)
    key_heads = kv_near[0].reshape(3 * tile_rows, head_count, HEAD)
    value_heads = kv_near[1].reshape(3 * tile_rows, head_count, HEAD)
    query_heads = query_rows.reshape(tile_rows, head_count, HEAD)
    scores = (
        jnp.einsum("ihd,jhd->hij", query_heads, key_heads, preferred_element_type=jnp.float32)
        * score_scale
    )
    scores = jnp.where(key_mask[None, None, :], scores, masked_score)
    row_max = jnp.max(scores, axis=2, keepdims=True)
    log_total = (row_max + jnp.log(jnp.sum(jnp.exp(scores - row_max), axis=2, keepdims=True)))[
        ..., 0
    ]
    weights = jnp.exp(scores - log_total[..., None])
    weights_bf = weights.astype(jnp.bfloat16)
    attn = (
        jnp.einsum("hij,jhd->ihd", weights_bf, value_heads, preferred_element_type=jnp.float32)
        .reshape(tile_rows, model_cols)
        .astype(jnp.bfloat16)
    )
    shard_piece = lax.all_gather(out_weight, "dp", axis=0, tiled=True)
    attn_cols = attn
    mixed_sum = jnp.dot(attn_cols, shard_piece, preferred_element_type=jnp.float32)
    new_cols = lax.dot_general(
        upstream, shard_piece, (((1,), (1,)), ((), ())), preferred_element_type=jnp.float32
    )
    back_cols = new_cols
    mixed_sum, back_cols = (mixed_sum, back_cols)
    mixed = mixed_sum.astype(jnp.bfloat16)
    grad_attn = back_cols.astype(jnp.bfloat16)
    grad_heads = grad_attn.reshape(tile_rows, head_count, HEAD)
    deltas = jnp.sum(
        grad_heads.astype(jnp.float32)
        * attn.reshape(tile_rows, head_count, HEAD).astype(jnp.float32),
        axis=2,
    ).T
    dprob = jnp.einsum("ihd,jhd->hij", grad_heads, value_heads, preferred_element_type=jnp.float32)
    dscore = (weights * (dprob - deltas[:, :, None]) * score_scale).astype(jnp.bfloat16)
    grad_query = (
        jnp.einsum("hij,jhd->ihd", dscore, key_heads, preferred_element_type=jnp.float32)
        .reshape(tile_rows, model_cols)
        .astype(jnp.bfloat16)
    )
    stat_pair = jnp.stack([log_total, deltas])
    stat_near = padded(stat_pair, (("space", 2),), tile_rows)
    query_grad = jnp.stack([query_rows, grad_attn])
    query_near = padded(query_grad, (("space", 1),), tile_rows)
    far_queries = query_near[0].reshape(3 * tile_rows, head_count, HEAD)
    far_grads = query_near[1].reshape(3 * tile_rows, head_count, HEAD)
    own_keys = key_rows.reshape(tile_rows, head_count, HEAD)
    own_values = value_rows.reshape(tile_rows, head_count, HEAD)
    back_scores = (
        jnp.einsum("jhd,ihd->hji", far_queries, own_keys, preferred_element_type=jnp.float32)
        * score_scale
    )
    back_weights = jnp.where(
        query_mask[None, :, None], jnp.exp(back_scores - stat_near[0][:, :, None]), 0.0
    )
    back_bf = back_weights.astype(jnp.bfloat16)
    grad_value = (
        jnp.einsum("hji,jhd->ihd", back_bf, far_grads, preferred_element_type=jnp.float32)
        .reshape(tile_rows, model_cols)
        .astype(jnp.bfloat16)
    )
    back_dprob = jnp.einsum(
        "jhd,ihd->hji", far_grads, own_values, preferred_element_type=jnp.float32
    )
    back_dscore = (back_weights * (back_dprob - stat_near[1][:, :, None]) * score_scale).astype(
        jnp.bfloat16
    )
    grad_key = (
        jnp.einsum("hji,jhd->ihd", back_dscore, far_queries, preferred_element_type=jnp.float32)
        .reshape(tile_rows, model_cols)
        .astype(jnp.bfloat16)
    )
    attn_cols = attn
    partial_rows = lax.psum_scatter(
        lax.dot_general(
            attn_cols, upstream, (((0,), (0,)), ((), ())), preferred_element_type=jnp.float32
        ),
        ("dp", "space"),
        scatter_dimension=0,
        tiled=True,
    )
    grad_weight = lax.all_gather(partial_rows, "space", axis=0, tiled=True)
    return (mixed[None], grad_query[None], grad_key[None], grad_value[None], grad_weight)


def solution(mesh):
    return jax.shard_map(
        on_device,
        mesh=mesh,
        in_specs=(
            P("dp", "space", None),
            P("dp", "space", None),
            P("dp", "space", None),
            P("dp", None),
            P("dp", "space", None),
            P(),
        ),
        out_specs=(
            P("dp", "space", None),
            P("dp", "space", None),
            P("dp", "space", None),
            P("dp", "space", None),
            P("dp", None),
        ),
        check_vma=False,
    )
```

profile of v0, /device:TPU:0, one launch (start us, length us, event | category | flops | bytes accessed | tf_op | source)
XLA Modules:
  0.0 960.4 jit_solution(17843270505314857095)
XLA Ops:
  8.0 2.4 copy.67
  12.1 2.9 pad_maximum_fusion.2
  16.3 6.0 collective-permute-start
  22.3 2.4 copy.68
  25.4 44.8 %collective-permute-done.1 = bf16[2,384,1536]{1,2,0:T(8,128)(2,1)} collective-permute-done((bf16[2,384,1536]{1,2,0:T(8,128)(2,1)}, bf16[2,384,1536]{1,2,0:T(8,128)(2,1)}, u32[]{:S(2)}, u32[]{:S(2)}) %collective-permute-start.1) | collective-permute-done | bytes 2359328 | tf_op jit(solution)/shard_map/ppermute | solution.py:22
  71.3 3.6 pad_maximum_fusion
  74.9 2.3 fusion.36
  77.2 9.5 bitcast_reduce_fusion
  86.7 9.2 fusion.2
  96.6 7.5 convolution_convert_fusion.1
  104.1 2.4 copy.72
  106.5 12.5 %multiply_reduce_fusion = (f32[384,12]{0,1:T(8,128)}, bf16[12,128,384]{2,1,0:T(8,128)(2,1)S(1)}) fusion(bf16[384,12,128]{0,2,1:T(8,128)(2,1)} %bitcast.92, bf16[1152,12,128]{0,2,1:T(8,128)(2,1)} %bitcast.85, f32[12,1152,384]{2,1,0:T(8,128)} %get-tuple-element.32, f32[12,384]{1,0:T(8,128)} %log_add_fusion), kind=kOutput, calls=%fused_computation.31 | convolution fusion | flops 1372515840 | bytes 27168768 | tf_op jit(solution)/shard_map/hij,jhd->ihd/dot_general | solution.py:64
  120.0 9.1 fusion.18
  129.1 439.3 %fusion = f32[16,3072]{1,0:T(8,128)} fusion(f32[1536,3072]{1,0:T(8,128)} %fusion.18), kind=kCustom, calls=%all-reduce-scatter | all-reduce-scatter fusion | flops 6291457 | bytes 19070976
  568.5 2.0 collective-permute-start.36
  572.7 2.0 collective-permute-start.35
  574.7 2.0 collective-permute-start.34
  576.6 2.0 collective-permute-start.33
  579.3 2.0 collective-permute-start.32
  581.3 12.0 %collective-permute-start.31 = (f32[16,3072]{1,0:T(8,128)}, f32[16,3072]{1,0:T(8,128)}, u32[]{:S(2)}, u32[]{:S(2)}) collective-permute-start(f32[16,3072]{1,0:T(8,128)} %fusion), channel_id=1, source_target_pairs={{0,26},{1,27},{2,28},{3,29},{4,30},{5,31},{6,32},{7,33},{8,34},{9,... | collective-permute-start | bytes 589832
  593.2 2.0 collective-permute-start.30
  595.2 2.0 collective-permute-start.29
  597.2 8.7 collective-permute-start.28
  605.9 6.9 collective-permute-start.27
  612.8 2.4 collective-permute-start.26
  615.2 4.0 collective-permute-start.25
  619.2 17.2 %collective-permute-start.24 = (f32[16,3072]{1,0:T(8,128)}, f32[16,3072]{1,0:T(8,128)}, u32[]{:S(2)}, u32[]{:S(2)}) collective-permute-start(f32[16,3072]{1,0:T(8,128)} %fusion), channel_id=1, source_target_pairs={{0,19},{1,20},{2,21},{3,22},{4,23},{5,24},{6,25},{7,26},{8,27},{9,... | collective-permute-start | bytes 589832
  636.4 3.0 collective-permute-start.23
  639.3 2.8 collective-permute-start.22
  642.1 2.6 collective-permute-start.21
  644.8 9.2 collective-permute-start.20
  654.0 2.3 collective-permute-start.19
  656.3 2.2 collective-permute-start.18
  658.5 2.0 collective-permute-start.17
  660.4 15.2 %collective-permute-done.21 = f32[16,3072]{1,0:T(8,128)} collective-permute-done((f32[16,3072]{1,0:T(8,128)}, f32[16,3072]{1,0:T(8,128)}, u32[]{:S(2)}, u32[]{:S(2)}) %collective-permute-start.21) | collective-permute-done | bytes 196640
  675.6 1.9 collective-permute-start.16
  678.3 2.0 collective-permute-start.15
  680.2 2.1 collective-permute-start.14
  682.3 2.5 collective-permute-start.13
  684.9 8.5 collective-permute-start.12
  693.4 3.2 collective-permute-start.11
  696.7 4.1 collective-permute-start.10
  700.8 6.2 collective-permute-start.9
  707.0 3.1 collective-permute-start.8
  710.0 4.6 collective-permute-start.7
  714.6 2.0 collective-permute-start.6
  716.6 1.7 pad_maximum_fusion.3
  720.3 5.9 collective-permute-start.2
  727.5 5.2 collective-permute-start.4
  732.7 86.0 %concatenate.12 = f32[524,3072]{1,0:T(8,128)} concatenate(f32[12,3072]{1,0:T(8,128)} %copy-done.11, f32[16,3072]{1,0:T(8,128)} %collective-permute-done.36, f32[16,3072]{1,0:T(8,128)} %collective-permute-done.35, f32[16,3072]{1,0:T(8,128)} %collective-permute-done.34, f32[16,3072]{1,0:T(8,128)} %collective-permute-done.33, f32[16,3072]{1,0:T(8,128)} %collective-permute-done.32, ...), dimensions={0} | concatenate | bytes 12877824
  820.4 14.2 %fusion.21 = bf16[12,128,384]{2,1,0:T(8,128)(2,1)} fusion(bf16[1152,12,128]{0,2,1:T(8,128)(2,1)} %bitcast.84, bf16[384,12,128]{0,2,1:T(8,128)(2,1)} %bitcast.93, bf16[1152,12,128]{0,2,1:T(8,128)(2,1)} %bitcast.86, f32[12,1152,384]{2,1,0:T(8,128)} %get-tuple-element.32, f32[12,384]{1,0:T(8,128)} %bitcast.102, f32[12,384]{1,0:T(8,128)} %log_add_fusion), kind=kOutput, calls=%fused_computation.32 | convolution fusion | flops 2745040896 | bytes 30707712 | tf_op jit(solution)/shard_map/hij,jhd->ihd/dot_general | solution.py:87
  834.5 9.4 fusion.16
  843.9 2.4 copy.86
  847.8 40.7 %all-gather.6.cloned.1.call-done = f32[8,12,3072]{2,1,0:T(8,128)} async-done(((f32[1,12,3072]{2,1,0:T(8,128)}), f32[8,12,3072]{2,1,0:T(8,128)}) %all-gather.6.cloned.1.call-update) | async-done | bytes 1179664 | tf_op jit(solution)/shard_map/all_gather | solution.py:132
  888.5 2.6 reshape.114
  891.1 3.4 pad_maximum_fusion.1
  894.5 3.3 fusion.35
  897.8 5.8 copy.77
  903.6 5.8 copy.82
  909.3 12.2 %fusion.37 = f32[12,1152,384]{2,1,0:T(8,128)} fusion(bf16[1152,12,128]{0,2,1:T(8,128)(2,1)} %bitcast.81, bf16[384,12,128]{0,2,1:T(8,128)(2,1)S(1)} %bitcast.80), kind=kOutput, calls=%fused_computation.58 | convolution fusion | flops 1358954496 | bytes 25952256 | tf_op jit(solution)/shard_map/jhd,ihd->hji/dot_general | solution.py:100
  921.5 10.5 %fusion.23 = bf16[12,128,384]{2,1,0:T(8,128)(2,1)} fusion(bf16[1152,12,128]{0,2,1:T(8,128)(2,1)S(1)} %bitcast.96, f32[12,1152,384]{2,1,0:T(8,128)} %fusion.37, f32[12,1152]{1,0:T(8,128)S(1)} %copy-done.12, pred[1152]{0:T(1024)(128)(4,1)S(1)} %broadcast_in_dim.51), kind=kOutput, calls=%fused_computation.34 | convolution fusion | flops 1380777984 | bytes 26008704 | tf_op jit(solution)/shard_map/hji,jhd->ihd/dot_general | solution.py:108
  932.0 16.4 %fusion.22 = bf16[12,128,384]{2,1,0:T(8,128)(2,1)} fusion(bf16[1152,12,128]{0,2,1:T(8,128)(2,1)} %bitcast.82, f32[12,1152,384]{2,1,0:T(8,128)} %fusion.37, f32[12,1152]{1,0:T(8,128)} %get-tuple-element.30, f32[12,1152]{1,0:T(8,128)} %get-tuple-element.29, pred[1152]{0:T(1024)(128)(4,1)S(1)} %broadcast_in_dim.51, bf16[1152,12,128]{0,2,1:T(8,128)(2,1)} %bitcast.95, ...), kind=kOutput, calls=%fused_computation.33 | convolution fusion | flops 2755657728 | bytes 30782592 | tf_op jit(solution)/shard_map/hji,jhd->ihd/dot_general | solution.py:119
  948.5 2.4 copy.87
  950.8 2.4 copy.88
  (94 shorter events, 17.5 us)
Async XLA Ops:
  7.2 89.4 %copy-start = (bf16[1,384,3072]{2,1,0:T(8,128)(2,1)S(1)}, bf16[1,384,3072]{2,1,0:T(8,128)(2,1)}, u32[]{:S(2)}) copy-start(bf16[1,384,3072]{2,1,0:T(8,128)(2,1)} %param.10) | copy-start | bytes 7077892
  7.2 89.4 %all-gather.4.cloned.1.call-start = ((), (), s32[]{:S(2)}) async-start(), calls=%async_computation | async-start | bytes 10027008 | tf_op jit(solution)/shard_map/all_gather | solution.py:68
  7.9 880.6 %all-gather.6.cloned.1.call-start = ((), (), s32[]{:S(2)}) async-start(), calls=%async_computation.1 | async-start | bytes 1769472 | tf_op jit(solution)/shard_map/all_gather | solution.py:132
  12.0 12.7 %copy-start.13 = (s32[8,3]{0,1:T(4,128)S(1)}, s32[8,3]{0,1:T(4,128)}, u32[]{:S(2)}) copy-start(s32[8,3]{0,1:T(4,128)} %param.11) | copy-start | bytes 292
  15.0 55.1 %collective-permute-start.1 = (bf16[2,384,1536]{1,2,0:T(8,128)(2,1)}, bf16[2,384,1536]{1,2,0:T(8,128)(2,1)}, u32[]{:S(2)}, u32[]{:S(2)}) collective-permute-start(bf16[2,384,1536]{1,2,0:T(8,128)(2,1)} %pad_maximum_fusion.2), channel_id=1, source_target_pairs={{1,0},{2,1},{3,2},{4,3},{5,4},{6,5},{7,6},{9,8},{10,9},{11,10},{12... | collective-permute-start | bytes 7077896 | tf_op jit(solution)/shard_map/ppermute | solution.py:22
  16.3 55.0 %collective-permute-start = (bf16[2,384,1536]{1,2,0:T(8,128)(2,1)}, bf16[2,384,1536]{1,2,0:T(8,128)(2,1)}, u32[]{:S(2)}, u32[]{:S(2)}) collective-permute-start(bf16[2,384,1536]{1,2,0:T(8,128)(2,1)} %pad_maximum_fusion.2), channel_id=1, source_target_pairs={{0,1},{1,2},{2,3},{3,4},{4,5},{5,6},{6,7},{8,9},{9,10},{10,11},{11... | collective-permute-start | bytes 7077896 | tf_op jit(solution)/shard_map/ppermute | solution.py:21
  74.9 2.3 copy-start.7
  77.2 9.5 copy-start.2
  119.0 1.0 copy-start.6
  129.1 587.5 %copy-start.3 = (bf16[1,384,1536]{2,1,0:T(8,128)(2,1)S(1)}, bf16[1,384,1536]{2,1,0:T(8,128)(2,1)}, u32[]{:S(2)}) copy-start(bf16[1,384,1536]{2,1,0:T(8,128)(2,1)} %param.6) | copy-start | bytes 3538948
  129.1 587.5 %copy-start.5 = (bf16[384,1536]{1,0:T(8,128)(2,1)S(1)}, bf16[384,1536]{1,0:T(8,128)(2,1)}, u32[]{:S(2)}) copy-start(bf16[384,1536]{1,0:T(8,128)(2,1)} %convolution_convert_fusion.1) | copy-start | bytes 3538948
  568.5 12.8 %collective-permute-start.36 = (f32[16,3072]{1,0:T(8,128)}, f32[16,3072]{1,0:T(8,128)}, u32[]{:S(2)}, u32[]{:S(2)}) collective-permute-start(f32[16,3072]{1,0:T(8,128)} %fusion), channel_id=1, source_target_pairs={{0,31},{1,32},{2,33},{3,34},{4,35},{5,36},{6,37},{7,38},{8,39},{9,... | collective-permute-start | bytes 589832
  571.4 7.2 collective-permute-start.37
  572.7 20.5 %collective-permute-start.35 = (f32[16,3072]{1,0:T(8,128)}, f32[16,3072]{1,0:T(8,128)}, u32[]{:S(2)}, u32[]{:S(2)}) collective-permute-start(f32[16,3072]{1,0:T(8,128)} %fusion), channel_id=1, source_target_pairs={{0,30},{1,31},{2,32},{3,33},{4,34},{5,35},{6,36},{7,37},{8,38},{9,... | collective-permute-start | bytes 589832
  574.7 20.5 %collective-permute-start.34 = (f32[16,3072]{1,0:T(8,128)}, f32[16,3072]{1,0:T(8,128)}, u32[]{:S(2)}, u32[]{:S(2)}) collective-permute-start(f32[16,3072]{1,0:T(8,128)} %fusion), channel_id=1, source_target_pairs={{0,29},{1,30},{2,31},{3,32},{4,33},{5,34},{6,35},{7,36},{8,37},{9,... | collective-permute-start | bytes 589832
  576.6 20.5 %collective-permute-start.33 = (f32[16,3072]{1,0:T(8,128)}, f32[16,3072]{1,0:T(8,128)}, u32[]{:S(2)}, u32[]{:S(2)}) collective-permute-start(f32[16,3072]{1,0:T(8,128)} %fusion), channel_id=1, source_target_pairs={{0,28},{1,29},{2,30},{3,31},{4,32},{5,33},{6,34},{7,35},{8,36},{9,... | collective-permute-start | bytes 589832
  578.6 0.7 copy-start.11
  579.3 26.6 %collective-permute-start.32 = (f32[16,3072]{1,0:T(8,128)}, f32[16,3072]{1,0:T(8,128)}, u32[]{:S(2)}, u32[]{:S(2)}) collective-permute-start(f32[16,3072]{1,0:T(8,128)} %fusion), channel_id=1, source_target_pairs={{0,27},{1,28},{2,29},{3,30},{4,31},{5,32},{6,33},{7,34},{8,35},{9,... | collective-permute-start | bytes 589832
  581.3 31.6 %collective-permute-start.31 = (f32[16,3072]{1,0:T(8,128)}, f32[16,3072]{1,0:T(8,128)}, u32[]{:S(2)}, u32[]{:S(2)}) collective-permute-start(f32[16,3072]{1,0:T(8,128)} %fusion), channel_id=1, source_target_pairs={{0,26},{1,27},{2,28},{3,29},{4,30},{5,31},{6,32},{7,33},{8,34},{9,... | collective-permute-start | bytes 589832
  593.2 22.0 %collective-permute-start.30 = (f32[16,3072]{1,0:T(8,128)}, f32[16,3072]{1,0:T(8,128)}, u32[]{:S(2)}, u32[]{:S(2)}) collective-permute-start(f32[16,3072]{1,0:T(8,128)} %fusion), channel_id=1, source_target_pairs={{0,25},{1,26},{2,27},{3,28},{4,29},{5,30},{6,31},{7,32},{8,33},{9,... | collective-permute-start | bytes 589832
  595.2 24.0 %collective-permute-start.29 = (f32[16,3072]{1,0:T(8,128)}, f32[16,3072]{1,0:T(8,128)}, u32[]{:S(2)}, u32[]{:S(2)}) collective-permute-start(f32[16,3072]{1,0:T(8,128)} %fusion), channel_id=1, source_target_pairs={{0,24},{1,25},{2,26},{3,27},{4,28},{5,29},{6,30},{7,31},{8,32},{9,... | collective-permute-start | bytes 589832
  597.2 39.2 %collective-permute-start.28 = (f32[16,3072]{1,0:T(8,128)}, f32[16,3072]{1,0:T(8,128)}, u32[]{:S(2)}, u32[]{:S(2)}) collective-permute-start(f32[16,3072]{1,0:T(8,128)} %fusion), channel_id=1, source_target_pairs={{0,23},{1,24},{2,25},{3,26},{4,27},{5,28},{6,29},{7,30},{8,31},{9,... | collective-permute-start | bytes 589832
  605.9 33.4 %collective-permute-start.27 = (f32[16,3072]{1,0:T(8,128)}, f32[16,3072]{1,0:T(8,128)}, u32[]{:S(2)}, u32[]{:S(2)}) collective-permute-start(f32[16,3072]{1,0:T(8,128)} %fusion), channel_id=1, source_target_pairs={{0,22},{1,23},{2,24},{3,25},{4,26},{5,27},{6,28},{7,29},{8,30},{9,... | collective-permute-start | bytes 589832
  612.8 29.3 %collective-permute-start.26 = (f32[16,3072]{1,0:T(8,128)}, f32[16,3072]{1,0:T(8,128)}, u32[]{:S(2)}, u32[]{:S(2)}) collective-permute-start(f32[16,3072]{1,0:T(8,128)} %fusion), channel_id=1, source_target_pairs={{0,21},{1,22},{2,23},{3,24},{4,25},{5,26},{6,27},{7,28},{8,29},{9,... | collective-permute-start | bytes 589832
  615.2 29.6 %collective-permute-start.25 = (f32[16,3072]{1,0:T(8,128)}, f32[16,3072]{1,0:T(8,128)}, u32[]{:S(2)}, u32[]{:S(2)}) collective-permute-start(f32[16,3072]{1,0:T(8,128)} %fusion), channel_id=1, source_target_pairs={{0,20},{1,21},{2,22},{3,23},{4,24},{5,25},{6,26},{7,27},{8,28},{9,... | collective-permute-start | bytes 589832
  619.2 34.8 %collective-permute-start.24 = (f32[16,3072]{1,0:T(8,128)}, f32[16,3072]{1,0:T(8,128)}, u32[]{:S(2)}, u32[]{:S(2)}) collective-permute-start(f32[16,3072]{1,0:T(8,128)} %fusion), channel_id=1, source_target_pairs={{0,19},{1,20},{2,21},{3,22},{4,23},{5,24},{6,25},{7,26},{8,27},{9,... | collective-permute-start | bytes 589832
  636.4 19.9 %collective-permute-start.23 = (f32[16,3072]{1,0:T(8,128)}, f32[16,3072]{1,0:T(8,128)}, u32[]{:S(2)}, u32[]{:S(2)}) collective-permute-start(f32[16,3072]{1,0:T(8,128)} %fusion), channel_id=1, source_target_pairs={{0,18},{1,19},{2,20},{3,21},{4,22},{5,23},{6,24},{7,25},{8,26},{9,... | collective-permute-start | bytes 589832
  639.3 19.1 %collective-permute-start.22 = (f32[16,3072]{1,0:T(8,128)}, f32[16,3072]{1,0:T(8,128)}, u32[]{:S(2)}, u32[]{:S(2)}) collective-permute-start(f32[16,3072]{1,0:T(8,128)} %fusion), channel_id=1, source_target_pairs={{0,17},{1,18},{2,19},{3,20},{4,21},{5,22},{6,23},{7,24},{8,25},{9,... | collective-permute-start | bytes 589832
  642.1 33.5 %collective-permute-start.21 = (f32[16,3072]{1,0:T(8,128)}, f32[16,3072]{1,0:T(8,128)}, u32[]{:S(2)}, u32[]{:S(2)}) collective-permute-start(f32[16,3072]{1,0:T(8,128)} %fusion), channel_id=1, source_target_pairs={{0,16},{1,17},{2,18},{3,19},{4,20},{5,21},{6,22},{7,23},{8,24},{9,... | collective-permute-start | bytes 589832
  644.8 33.5 %collective-permute-start.20 = (f32[16,3072]{1,0:T(8,128)}, f32[16,3072]{1,0:T(8,128)}, u32[]{:S(2)}, u32[]{:S(2)}) collective-permute-start(f32[16,3072]{1,0:T(8,128)} %fusion), channel_id=1, source_target_pairs={{0,15},{1,16},{2,17},{3,18},{4,19},{5,20},{6,21},{7,22},{8,23},{9,... | collective-permute-start | bytes 589832
  654.0 26.2 %collective-permute-start.19 = (f32[16,3072]{1,0:T(8,128)}, f32[16,3072]{1,0:T(8,128)}, u32[]{:S(2)}, u32[]{:S(2)}) collective-permute-start(f32[16,3072]{1,0:T(8,128)} %fusion), channel_id=1, source_target_pairs={{0,14},{1,15},{2,16},{3,17},{4,18},{5,19},{6,20},{7,21},{8,22},{9,... | collective-permute-start | bytes 589832
  656.3 26.1 %collective-permute-start.18 = (f32[16,3072]{1,0:T(8,128)}, f32[16,3072]{1,0:T(8,128)}, u32[]{:S(2)}, u32[]{:S(2)}) collective-permute-start(f32[16,3072]{1,0:T(8,128)} %fusion), channel_id=1, source_target_pairs={{0,13},{1,14},{2,15},{3,16},{4,17},{5,18},{6,19},{7,20},{8,21},{9,... | collective-permute-start | bytes 589832
  658.5 26.4 %collective-permute-start.17 = (f32[16,3072]{1,0:T(8,128)}, f32[16,3072]{1,0:T(8,128)}, u32[]{:S(2)}, u32[]{:S(2)}) collective-permute-start(f32[16,3072]{1,0:T(8,128)} %fusion), channel_id=1, source_target_pairs={{0,12},{1,13},{2,14},{3,15},{4,16},{5,17},{6,18},{7,19},{8,20},{9,... | collective-permute-start | bytes 589832
  675.6 17.8 %collective-permute-start.16 = (f32[16,3072]{1,0:T(8,128)}, f32[16,3072]{1,0:T(8,128)}, u32[]{:S(2)}, u32[]{:S(2)}) collective-permute-start(f32[16,3072]{1,0:T(8,128)} %fusion), channel_id=1, source_target_pairs={{0,11},{1,12},{2,13},{3,14},{4,15},{5,16},{6,17},{7,18},{8,19},{9,... | collective-permute-start | bytes 589832
  678.3 18.4 %collective-permute-start.15 = (f32[16,3072]{1,0:T(8,128)}, f32[16,3072]{1,0:T(8,128)}, u32[]{:S(2)}, u32[]{:S(2)}) collective-permute-start(f32[16,3072]{1,0:T(8,128)} %fusion), channel_id=1, source_target_pairs={{0,10},{1,11},{2,12},{3,13},{4,14},{5,15},{6,16},{7,17},{8,18},{9,... | collective-permute-start | bytes 589832
  680.2 20.5 %collective-permute-start.14 = (f32[16,3072]{1,0:T(8,128)}, f32[16,3072]{1,0:T(8,128)}, u32[]{:S(2)}, u32[]{:S(2)}) collective-permute-start(f32[16,3072]{1,0:T(8,128)} %fusion), channel_id=1, source_target_pairs={{0,9},{1,10},{2,11},{3,12},{4,13},{5,14},{6,15},{7,16},{8,17},{9,1... | collective-permute-start | bytes 589832
  682.3 24.6 %collective-permute-start.13 = (f32[16,3072]{1,0:T(8,128)}, f32[16,3072]{1,0:T(8,128)}, u32[]{:S(2)}, u32[]{:S(2)}) collective-permute-start(f32[16,3072]{1,0:T(8,128)} %fusion), channel_id=1, source_target_pairs={{0,8},{1,9},{2,10},{3,11},{4,12},{5,13},{6,14},{7,15},{8,16},{9,17... | collective-permute-start | bytes 589832
  684.9 25.2 %collective-permute-start.12 = (f32[16,3072]{1,0:T(8,128)}, f32[16,3072]{1,0:T(8,128)}, u32[]{:S(2)}, u32[]{:S(2)}) collective-permute-start(f32[16,3072]{1,0:T(8,128)} %fusion), channel_id=1, source_target_pairs={{0,7},{1,8},{2,9},{3,10},{4,11},{5,12},{6,13},{7,14},{8,15},{9,16}... | collective-permute-start | bytes 589832
  693.4 21.3 %collective-permute-start.11 = (f32[16,3072]{1,0:T(8,128)}, f32[16,3072]{1,0:T(8,128)}, u32[]{:S(2)}, u32[]{:S(2)}) collective-permute-start(f32[16,3072]{1,0:T(8,128)} %fusion), channel_id=1, source_target_pairs={{0,6},{1,7},{2,8},{3,9},{4,10},{5,11},{6,12},{7,13},{8,14},{9,15},... | collective-permute-start | bytes 589832
  696.6 21.7 %copy-start.9 = (f32[12,384]{1,0:T(8,128)S(1)}, f32[12,384]{1,0:T(8,128)}, u32[]{:S(2)}) copy-start(f32[12,384]{1,0:T(8,128)} %log_add_fusion) | copy-start | bytes 55300
  696.6 21.7 %copy-start.10 = (f32[384,12]{0,1:T(8,128)S(1)}, f32[384,12]{0,1:T(8,128)}, u32[]{:S(2)}) copy-start(f32[384,12]{0,1:T(8,128)} %get-tuple-element.33) | copy-start | bytes 55300
  696.7 22.3 %collective-permute-start.10 = (f32[16,3072]{1,0:T(8,128)}, f32[16,3072]{1,0:T(8,128)}, u32[]{:S(2)}, u32[]{:S(2)}) collective-permute-start(f32[16,3072]{1,0:T(8,128)} %fusion), channel_id=1, source_target_pairs={{0,5},{1,6},{2,7},{3,8},{4,9},{5,10},{6,11},{7,12},{8,13},{9,14},{... | collective-permute-start | bytes 589832
  700.8 19.5 %collective-permute-start.9 = (f32[16,3072]{1,0:T(8,128)}, f32[16,3072]{1,0:T(8,128)}, u32[]{:S(2)}, u32[]{:S(2)}) collective-permute-start(f32[16,3072]{1,0:T(8,128)} %fusion), channel_id=1, source_target_pairs={{0,4},{1,5},{2,6},{3,7},{4,8},{5,9},{6,10},{7,11},{8,12},{9,13},{1... | collective-permute-start | bytes 589832
  707.0 19.2 %collective-permute-start.8 = (f32[16,3072]{1,0:T(8,128)}, f32[16,3072]{1,0:T(8,128)}, u32[]{:S(2)}, u32[]{:S(2)}) collective-permute-start(f32[16,3072]{1,0:T(8,128)} %fusion), channel_id=1, source_target_pairs={{0,3},{1,4},{2,5},{3,6},{4,7},{5,8},{6,9},{7,10},{8,11},{9,12},{10... | collective-permute-start | bytes 589832
  710.0 17.5 %collective-permute-start.7 = (f32[16,3072]{1,0:T(8,128)}, f32[16,3072]{1,0:T(8,128)}, u32[]{:S(2)}, u32[]{:S(2)}) collective-permute-start(f32[16,3072]{1,0:T(8,128)} %fusion), channel_id=1, source_target_pairs={{0,2},{1,3},{2,4},{3,5},{4,6},{5,7},{6,8},{7,9},{8,10},{9,11},{10,... | collective-permute-start | bytes 589832
  714.6 18.0 %collective-permute-start.6 = (f32[16,3072]{1,0:T(8,128)}, f32[16,3072]{1,0:T(8,128)}, u32[]{:S(2)}, u32[]{:S(2)}) collective-permute-start(f32[16,3072]{1,0:T(8,128)} %fusion), channel_id=1, source_target_pairs={{0,1},{1,2},{2,3},{3,4},{4,5},{5,6},{6,7},{7,8},{8,9},{9,10},{10,1... | collective-permute-start | bytes 589832
  719.0 172.1 %collective-permute-start.3 = (bf16[2,384,1536]{2,1,0:T(8,128)(2,1)}, bf16[2,384,1536]{2,1,0:T(8,128)(2,1)}, u32[]{:S(2)}, u32[]{:S(2)}) collective-permute-start(bf16[2,384,1536]{2,1,0:T(8,128)(2,1)} %pad_maximum_fusion.3), channel_id=1, source_target_pairs={{1,0},{2,1},{3,2},{4,3},{5,4},{6,5},{7,6},{9,8},{10,9},{11,10},{12... | collective-permute-start | bytes 7077896 | tf_op jit(solution)/shard_map/ppermute | solution.py:22
  720.3 170.8 %collective-permute-start.2 = (bf16[2,384,1536]{2,1,0:T(8,128)(2,1)}, bf16[2,384,1536]{2,1,0:T(8,128)(2,1)}, u32[]{:S(2)}, u32[]{:S(2)}) collective-permute-start(bf16[2,384,1536]{2,1,0:T(8,128)(2,1)} %pad_maximum_fusion.3), channel_id=1, source_target_pairs={{0,1},{1,2},{2,3},{3,4},{4,5},{5,6},{6,7},{8,9},{9,10},{10,11},{11... | collective-permute-start | bytes 7077896 | tf_op jit(solution)/shard_map/ppermute | solution.py:21
  726.2 120.1 %collective-permute-start.5 = (f32[2,12,384]{2,1,0:T(8,128)}, f32[2,12,384]{2,1,0:T(8,128)}, u32[]{:S(2)}, u32[]{:S(2)}) collective-permute-start(f32[2,12,384]{2,1,0:T(8,128)} %pad_maximum_fusion.5), channel_id=1, source_target_pairs={{1,0},{2,1},{3,2},{4,3},{5,4},{6,5},{7,6},{9,8},{10,9},{11,10},{12... | collective-permute-start | bytes 110600 | tf_op jit(solution)/shard_map/ppermute | solution.py:22
  727.5 118.8 %collective-permute-start.4 = (f32[2,12,384]{2,1,0:T(8,128)}, f32[2,12,384]{2,1,0:T(8,128)}, u32[]{:S(2)}, u32[]{:S(2)}) collective-permute-start(f32[2,12,384]{2,1,0:T(8,128)} %pad_maximum_fusion.5), channel_id=1, source_target_pairs={{0,1},{1,2},{2,3},{3,4},{4,5},{5,6},{6,7},{8,9},{9,10},{10,11},{11... | collective-permute-start | bytes 110600 | tf_op jit(solution)/shard_map/ppermute | solution.py:21
  909.3 12.2 %copy-start.8 = (bf16[1,1152,1536]{1,2,0:T(8,128)(2,1)S(1)}, bf16[1,1152,1536]{1,2,0:T(8,128)(2,1)}, u32[]{:S(2)}) copy-start(bf16[1,1152,1536]{1,2,0:T(8,128)(2,1)} %copy.82) | copy-start | bytes 10616836
  909.3 12.2 %copy-start.12 = (f32[12,1152]{1,0:T(8,128)S(1)}, f32[12,1152]{1,0:T(8,128)}, u32[]{:S(2)}) copy-start(f32[12,1152]{1,0:T(8,128)} %get-tuple-element.29) | copy-start | bytes 165892
  921.5 10.5 %copy-start.4 = (bf16[1,384,1536]{1,2,0:T(8,128)(2,1)S(1)}, bf16[1,384,1536]{1,2,0:T(8,128)(2,1)}, u32[]{:S(2)}) copy-start(bf16[1,384,1536]{1,2,0:T(8,128)(2,1)} %copy.67) | copy-start | bytes 3538948
  932.0 21.2 %copy-start.1 = (bf16[1,384,3072]{2,1,0:T(8,128)(2,1)S(1)}, bf16[1,384,3072]{2,1,0:T(8,128)(2,1)}, u32[]{:S(2)}) copy-start(bf16[1,384,3072]{2,1,0:T(8,128)(2,1)} %param.10) | copy-start | bytes 7077892
Sparse Core Ops, SparseCore 0:
  10.5 85.0 all-gather.3
  820.5 67.9 all-gather.5
where the time goes:
time: 974 us; the launch traced here: 960 us
  blocking collectives  439 us (45%)
  starting transfers between devices  151 us (16%)
  local copies, waits for them, and re-layouts  128 us (13%)
  waiting for transfers between devices  103 us (11%)
  matrix products  101 us (10%)
  other arithmetic  23.5 us (2%)
  between operations  14.6 us (1%)
    unnamed x1, blocking collectives  439 us
    unnamed x32, starting transfers between devices  130 us
    unnamed x39, local copies, waits for them, and re-layouts  107 us
    ppermute x3, waiting for transfers between devices, padded(): after = lax.ppermute(initial, axis, down)  44.8 us
    all_gather x1, waiting for transfers between devices, on_device(): grad_weight = lax.all_gather(partial_rows, 'space', axis=0, tiled=True)  40.7 us
  transfers between devices with their start and end apart: 40, of which 4 were waited for; matrix products, arithmetic and copies ran while one was open for 16% of the time, Pallas kernels for 0%

commit v1 on v0

v1 whole, which is shorter than its diff:
```python
import functools
import math

import jax
import jax.numpy as jnp
from jax import lax
from jax.experimental import pallas as pl
from jax.experimental.pallas import tpu as pltpu
from jax.sharding import PartitionSpec as P

HEAD = 128
SCALE = 1.0 / math.sqrt(HEAD)
LOG2_SCALE = SCALE * math.log2(math.e)
FAR = 1e30
BF = jnp.bfloat16
F32 = jnp.float32
VMEM_LIMIT = 56 * 1024 * 1024

NX, NZ, NC, NL, NY = 2, 4, 2, 2, 4
NS = NL * NY


def moves(change):
    pairs = []
    for a in range(NX):
        for z in range(NZ):
            for c in range(NC):
                for l in range(NL):
                    for y in range(NY):
                        b, w, d, m, v = change(a, z, c, l, y)
                        src = ((a * NZ + z) * NC + c) * NS + l * NY + y
                        dst = ((b * NZ + w) * NC + d) * NS + m * NY + v
                        pairs.append((src, dst))
    return pairs


def move(x, change):
    return lax.ppermute(x, ("dp", "space"), moves(change))


def move_core(x):
    return move(x, lambda a, z, c, l, y: (a, z, 1 - c, l, y))


def move_lo(x):
    return move(x, lambda a, z, c, l, y: (a, z, c, 1 - l, y))


def move_lo_core(x):
    return move(x, lambda a, z, c, l, y: (a, z, 1 - c, 1 - l, y))


def move_hi(x):
    return move(x, lambda a, z, c, l, y: (1 - a, z, c, l, y))


def move_cross(x):
    return move(x, lambda a, z, c, l, y: (1 - a, z, c, 1 - l, y))


def move_z(x, k):
    return move(x, lambda a, z, c, l, y: (a, (z + k) % NZ, c, l, y))


def move_y(x, k):
    return move(x, lambda a, z, c, l, y: (a, z, c, l, (y + k) % NY))


def to_next(x):
    return lax.ppermute(x, "space", [(i, i + 1) for i in range(NS - 1)])


def to_previous(x):
    return lax.ppermute(x, "space", [(i + 1, i) for i in range(NS - 1)])


def nt(a, b):
    return lax.dot_general(a, b, (((1,), (1,)), ((), ())), preferred_element_type=F32)


def tn(a, b):
    return lax.dot_general(a, b, (((0,), (0,)), ((), ())), preferred_element_type=F32)


def nn(a, b):
    return lax.dot_general(a, b, (((1,), (0,)), ((), ())), preferred_element_type=F32)


def forward_kernel(info, q_ref, k_ref, v_ref, left_ref, right_ref, attn_ref, total_ref):
    q = q_ref[...]
    tiles = ((left_ref[0], left_ref[1]), (k_ref[...], v_ref[...]), (right_ref[0], right_ref[1]))
    live = (info[1] > 0, None, info[2] > 0)
    scores = [nt(k, q) for k, _ in tiles]
    tops = [jnp.max(s, axis=0, keepdims=True) for s in scores]
    top = tops[1]
    for j in (0, 2):
        top = jnp.maximum(top, jnp.where(live[j], tops[j], -FAR))
    top = top * LOG2_SCALE
    total = jnp.zeros_like(top)
    acc = jnp.zeros((HEAD, q.shape[0]), F32)
    for j in range(3):
        if live[j] is None:
            factor, shift = LOG2_SCALE, top
        else:
            factor = jnp.where(live[j], LOG2_SCALE, 0.0)
            shift = jnp.where(live[j], top, FAR)
        p = jnp.exp2(scores[j] * factor - shift)
        total = total + jnp.sum(p, axis=0, keepdims=True)
        acc = acc + tn(tiles[j][1], p.astype(BF))
    attn_ref[...] = (acc / total).astype(BF)
    total_ref[0] = top + jnp.log2(total)


def attend(info, q, k, v, left, right, heads):
    rows = q.shape[0]
    own = pl.BlockSpec((rows, HEAD), lambda h, info: (0, info[0] + h))
    side = pl.BlockSpec((2, rows, HEAD), lambda h, info: (0, 0, h))
    return pl.pallas_call(
        forward_kernel,
        out_shape=(
            jax.ShapeDtypeStruct((heads * HEAD, rows), BF),
            jax.ShapeDtypeStruct((heads, 1, rows), F32),
        ),
        grid_spec=pltpu.PrefetchScalarGridSpec(
            num_scalar_prefetch=1,
            grid=(heads,),
            in_specs=[own, own, own, side, side],
            out_specs=(
                pl.BlockSpec((HEAD, rows), lambda h, info: (h, 0)),
                pl.BlockSpec((1, 1, rows), lambda h, info: (h, 0, 0)),
            ),
        ),
        compiler_params=pltpu.CompilerParams(vmem_limit_bytes=VMEM_LIMIT),
        cost_estimate=pl.CostEstimate(
            flops=heads * 16 * rows * rows * HEAD,
            bytes_accessed=heads * rows * HEAD * 2 * 8,
            transcendentals=heads * 3 * rows * rows,
        ),
        name="attend",
    )(info, q, k, v, left, right)


def backward_kernel(first, info, q_ref, k_ref, v_ref, left_ref, right_ref, grad_ref, attn_ref, total_ref, *rest):
    dq_ref, own_ref, to_left_ref, to_right_ref = rest if first else rest[1:]
    q = q_ref[...]
    g = grad_ref[...]
    total = total_ref[0]
    delta = jnp.sum(g.astype(F32) * attn_ref[...].astype(F32), axis=0, keepdims=True)
    tiles = ((left_ref[0], left_ref[1]), (k_ref[...], v_ref[...]), (right_ref[0], right_ref[1]))
    live = (info[1] > 0, None, info[2] > 0)
    outs = (to_left_ref, own_ref, to_right_ref)
    dq = jnp.zeros((HEAD, q.shape[0]), F32)
    for j in range(3):
        k, v = tiles[j]
        if live[j] is None:
            factor, shift = LOG2_SCALE, total
        else:
            factor = jnp.where(live[j], LOG2_SCALE, 0.0)
            shift = jnp.where(live[j], total, FAR)
        w = jnp.exp2(nt(k, q) * factor - shift)
        outs[j][1] = nt(w.astype(BF), g).astype(outs[j].dtype)
        ds = (w * (nn(v, g) - delta)).astype(BF)
        outs[j][0] = (nn(ds, q) * SCALE).astype(outs[j].dtype)
        dq = dq + tn(k, ds)
    dq_ref[...] = (dq * SCALE).T.astype(BF)


def attend_back(info, q, k, v, left, right, grad, attn, total, heads, before):
    rows, cols = q.shape
    own = pl.BlockSpec((rows, HEAD), lambda h, info: (0, info[0] + h))
    side = pl.BlockSpec((2, rows, HEAD), lambda h, info: (0, 0, h))
    turned = pl.BlockSpec((HEAD, rows), lambda h, info: (h, 0))
    first = before is None
    return pl.pallas_call(
        functools.partial(backward_kernel, first),
        out_shape=(
            jax.ShapeDtypeStruct((rows, cols), BF),
            jax.ShapeDtypeStruct((2, rows, heads * HEAD), F32),
            jax.ShapeDtypeStruct((2, rows, heads * HEAD), BF),
            jax.ShapeDtypeStruct((2, rows, heads * HEAD), BF),
        ),
        grid_spec=pltpu.PrefetchScalarGridSpec(
            num_scalar_prefetch=1,
            grid=(heads,),
            in_specs=[own, own, own, side, side, turned, turned,
                      pl.BlockSpec((1, 1, rows), lambda h, info: (h, 0, 0))]
            + ([] if first else [pl.BlockSpec(memory_space=pl.ANY)]),
            out_specs=(own, side, side, side),
        ),
        input_output_aliases={} if first else {9: 0},
        compiler_params=pltpu.CompilerParams(vmem_limit_bytes=VMEM_LIMIT),
        cost_estimate=pl.CostEstimate(
            flops=heads * 40 * rows * rows * HEAD,
            bytes_accessed=heads * rows * HEAD * 2 * 16,
            transcendentals=heads * 3 * rows * rows,
        ),
        name="attend_back",
    )(info, q, k, v, left, right, grad, attn, total, *(() if first else (before,)))


def join_kernel(first, info, own_ref, a_ref, b_ref, *rest):
    dk_ref, dv_ref = rest if first else rest[2:]
    for i, out in enumerate((dk_ref, dv_ref)):
        out[...] = (own_ref[i] + a_ref[i].astype(F32) + b_ref[i].astype(F32)).astype(BF)


def join(info, own, a, b, heads, cols, before):
    rows = own.shape[1]
    side = pl.BlockSpec((2, rows, HEAD), lambda h, info: (0, 0, h))
    out = pl.BlockSpec((rows, HEAD), lambda h, info: (0, info[0] + h))
    first = before is None
    return pl.pallas_call(
        functools.partial(join_kernel, first),
        out_shape=(jax.ShapeDtypeStruct((rows, cols), BF),) * 2,
        grid_spec=pltpu.PrefetchScalarGridSpec(
            num_scalar_prefetch=1,
            grid=(heads,),
            in_specs=[side] * 3 + ([] if first else [pl.BlockSpec(memory_space=pl.ANY)] * 2),
            out_specs=(out, out),
        ),
        input_output_aliases={} if first else {4: 0, 5: 1},
        compiler_params=pltpu.CompilerParams(vmem_limit_bytes=VMEM_LIMIT),
        cost_estimate=pl.CostEstimate(
            flops=heads * 4 * rows * HEAD, bytes_accessed=heads * rows * HEAD * 20, transcendentals=0
        ),
        name="join",
    )(info, own, a, b, *(() if first else before))


def project_back_kernel(place, *refs):
    pieces, (u_ref, w_ref, g_ref, sems) = refs[:8], refs[8:]
    rows = pieces[0].shape[0]
    copies = []
    for i in range(8):
        spot = pl.multiple_of(place[i] * rows, rows)
        copies.append(pltpu.make_async_copy(pieces[i], w_ref.at[pl.ds(spot, rows)], sems.at[i]))
        copies[-1].start()
    for copy in copies:
        copy.wait()
    u = u_ref[...]

    def step(i, carry):
        spot = pl.ds(pl.multiple_of(i * 2 * rows, 2 * rows), 2 * rows)
        g_ref[spot, :] = nt(w_ref[spot, :], u).astype(BF)
        return carry

    lax.fori_loop(0, 4, step, 0)


def project_back(place, pieces, u):
    rows, wide = pieces[0].shape
    tokens = u.shape[0]
    whole = pl.BlockSpec(memory_space=pltpu.VMEM)
    return pl.pallas_call(
        project_back_kernel,
        out_shape=(
            jax.ShapeDtypeStruct((8 * rows, wide), BF),
            jax.ShapeDtypeStruct((8 * rows, tokens), BF),
        ),
        in_specs=[pl.BlockSpec(memory_space=pltpu.SMEM)] + [pl.BlockSpec(memory_space=pl.ANY)] * 8 + [whole],
        out_specs=(whole, whole),
        scratch_shapes=[pltpu.SemaphoreType.DMA((8,))],
        compiler_params=pltpu.CompilerParams(vmem_limit_bytes=VMEM_LIMIT),
        cost_estimate=pl.CostEstimate(
            flops=16 * rows * wide * tokens, bytes_accessed=40 * rows * wide, transcendentals=0
        ),
        name="project_back",
    )(place, *pieces, u)


def project_kernel(a_ref, b_ref, wa_ref, wb_ref, out_ref, turned):
    half = a_ref.shape[0]

    @pl.when(pl.program_id(0) == 0)
    def _():
        turned[:, :half] = a_ref[...].T
        turned[:, half:] = b_ref[...].T

    out_ref[...] = (nn(turned[:, :half], wa_ref[...]) + nn(turned[:, half:], wb_ref[...])).astype(BF)


def project(a, b, wa, wb):
    half, tokens = a.shape
    wide = wa.shape[1]
    block = 512
    side = pl.BlockSpec((half, tokens), lambda i: (0, 0))
    weight = pl.BlockSpec((half, block), lambda i: (0, i))
    return pl.pallas_call(
        project_kernel,
        out_shape=jax.ShapeDtypeStruct((tokens, wide), BF),
        grid=(wide // block,),
        in_specs=[side, side, weight, weight],
        out_specs=pl.BlockSpec((tokens, block), lambda i: (0, i)),
        scratch_shapes=[pltpu.VMEM((tokens, 2 * half), BF)],
        compiler_params=pltpu.CompilerParams(vmem_limit_bytes=VMEM_LIMIT),
        cost_estimate=pl.CostEstimate(
            flops=4 * half * wide * tokens, bytes_accessed=4 * half * wide + 2 * tokens * wide, transcendentals=0
        ),
        name="project",
    )(a, b, wa, wb)


def weight_grad_kernel(place, *refs):
    a_refs, u_refs, out_refs, total = refs[:4], refs[4:8], refs[8:12], refs[12]
    total[...] = sum(nn(a[...], u[...]) for a, u in zip(a_refs, u_refs)).astype(BF)
    rows = out_refs[0].shape[0]
    for i, out in enumerate(out_refs):
        out[...] = total[pl.ds(pl.multiple_of(place[i] * rows, rows), rows), :]


def weight_grad(place, a_list, u_list):
    rows, tokens = a_list[0].shape
    wide = u_list[0].shape[1]
    block = 512
    return pl.pallas_call(
        weight_grad_kernel,
        out_shape=(jax.ShapeDtypeStruct((rows // NZ, wide), BF),) * NZ,
        grid_spec=pltpu.PrefetchScalarGridSpec(
            num_scalar_prefetch=1,
            grid=(wide // block,),
            in_specs=[pl.BlockSpec((rows, tokens), lambda i, p: (0, 0))] * 4
            + [pl.BlockSpec((tokens, block), lambda i, p: (0, i))] * 4,
            out_specs=(pl.BlockSpec((rows // NZ, block), lambda i, p: (0, i)),) * NZ,
            scratch_shapes=[pltpu.VMEM((rows, block), BF)],
        ),
        compiler_params=pltpu.CompilerParams(vmem_limit_bytes=VMEM_LIMIT),
        cost_estimate=pl.CostEstimate(
            flops=8 * rows * wide * tokens, bytes_accessed=10 * tokens * wide, transcendentals=0
        ),
        name="weight_grad",
    )(place, *a_list, *u_list)


def place_kernel(spots, mine_ref, other_ref, out_ref):
    _, rows, cols = mine_ref.shape
    for j, ref in enumerate((mine_ref, other_ref)):
        top = pl.multiple_of(spots[4 + j] * rows, rows)
        for i in range(NY):
            start = pl.multiple_of(spots[i] * cols, cols)
            out_ref[pl.ds(top, rows), pl.ds(start, cols)] = ref[i].astype(F32)


def place_pieces(spots, mine, other):
    _, rows, cols = mine.shape
    whole = pl.BlockSpec(memory_space=pltpu.VMEM)
    return pl.pallas_call(
        place_kernel,
        out_shape=jax.ShapeDtypeStruct((2 * rows, NY * cols), F32),
        in_specs=[pl.BlockSpec(memory_space=pltpu.SMEM), whole, whole],
        out_specs=whole,
        name="place_pieces",
    )(spots, mine, other)


def add(*terms):
    return functools.reduce(lambda s, t: s + t.astype(F32), terms[1:], terms[0].astype(F32))


def on_device(query, key_in, value_in, out_weight, grad_out, neighbours):
    q, k, v, upstream = query[0], key_in[0], value_in[0], grad_out[0]
    rows, cols = q.shape
    half = cols // 2
    heads = half // HEAD
    dp = lax.axis_index("dp")
    tile = lax.axis_index("space")
    a, z, c = dp // (NZ * NC), (dp // NC) % NZ, dp % NC
    lo, y = tile // NY, tile % NY

    own_list = neighbours[tile]
    live_left = jnp.any((own_list == tile - 1) & (own_list >= 0)).astype(jnp.int32)
    live_right = jnp.any(own_list == tile + 1).astype(jnp.int32)
    infos = [
        jnp.stack([part * heads, live_left, live_right]).astype(jnp.int32) for part in (a, 1 - a)
    ]

    near = []
    for part in (a, 1 - a):
        pair = jnp.stack(
            [lax.dynamic_slice_in_dim(t, part * half, half, axis=1) for t in (k, v)]
        )
        near.append((to_next(pair), to_previous(pair)))

    w0 = [out_weight] + [move_z(out_weight, i) for i in (1, 3, 2)]
    cross = move_cross(out_weight)
    w1 = [cross] + [move_z(cross, i) for i in (1, 3)] + [move_cross(w0[3])]
    z_of = [z, (z + 3) % NZ, (z + 1) % NZ, (z + 2) % NZ]
    place = jnp.stack([2 * i + c for i in z_of] + [2 * i + 1 - c for i in z_of]).astype(jnp.int32)

    up_core = move_core(upstream)
    up_lo = move_lo(upstream)
    up_both = move_core(up_lo)

    attns, owns, back_sends, weights = [], [], [], []
    dq = None
    for part, w, info, (left, right) in zip((0, 1), (w0, w1), infos, near):
        attn, total = attend(info, q, k, v, left, right, heads)
        w_full, grad = project_back(place, w + [move_core(t) for t in w], upstream)
        dq, own, to_left, to_right = attend_back(
            info, q, k, v, left, right, grad, attn, total, heads, dq
        )
        back_sends.append((to_next(to_right), to_previous(to_left)))
        attns.append(attn)
        owns.append(own)
        weights.append(w_full)

    mixed = project(attns[0], attns[1], weights[0], weights[1])

    z_place = jnp.stack([(z + i) % NZ for i in range(NZ)]).astype(jnp.int32)
    u_list = [upstream, up_core, up_lo, up_both]
    sums = []
    for attn in attns:
        parts = attn.reshape(NZ, NC, NL, -1, rows)
        sub = parts.shape[3]

        def pick(core, low):
            return lax.dynamic_slice(
                parts, (0, core, low, 0, 0), (NZ, 1, 1, sub, rows)
            ).reshape(NZ * sub, rows)

        a_list = [
            pick(c, lo),
            move_core(pick(1 - c, lo)),
            move_lo(pick(c, 1 - lo)),
            move_lo_core(pick(1 - c, 1 - lo)),
        ]
        pieces = weight_grad(z_place, a_list, u_list)
        sums.append(add(pieces[0], *[move_z(pieces[i], i) for i in (1, 3, 2)]))
    both = sums[0] + move_hi(sums[1].astype(BF)).astype(F32)
    quarter = both.shape[1] // NY
    both = both.astype(BF)

    def column(i):
        return lax.dynamic_slice_in_dim(both, ((y + i) % NY) * quarter, quarter, axis=1)

    mine = add(column(0), *[move_y(column(i), i) for i in (1, 3, 2)]).astype(BF)
    mine = jnp.stack([mine] + [move_y(mine, i) for i in (1, 2, 3)])
    other = move_lo(mine)
    spots = jnp.stack([(y - i) % NY for i in range(NY)] + [lo, 1 - lo]).astype(jnp.int32)
    grad_weight = place_pieces(spots, mine, other)

    done = None
    for own, (from_left, from_right), info in zip(owns, back_sends, infos):
        done = join(info, own, from_left, from_right, heads, cols, done)
    dk, dv = done
    return (mixed[None], dq[None], dk[None], dv[None], grad_weight)


def solution(mesh):
    return jax.shard_map(
        on_device,
        mesh=mesh,
        in_specs=(
            P("dp", "space", None),
            P("dp", "space", None),
            P("dp", "space", None),
            P("dp", None),
            P("dp", "space", None),
            P(),
        ),
        out_specs=(
            P("dp", "space", None),
            P("dp", "space", None),
            P("dp", "space", None),
            P("dp", "space", None),
            P("dp", None),
        ),
        check_vma=False,
    )
```

time: 974 us -> 327 us (0.34); the launches traced: 960 us -> 326 us
  blocking collectives: 439 us -> 0 us
  local copies, waits for them, and re-layouts: 128 us -> 10.4 us
  Pallas kernels: 0 us -> 105 us
  matrix products: 101 us -> 0 us
  starting transfers between devices: 151 us -> 94.1 us
  other arithmetic: 23.5 us -> 6.9 us
  between operations: 14.6 us -> 2.42 us
    unnamed x1 -> x0, blocking collectives: 439 us -> none
    unnamed x32 -> x0, starting transfers between devices: 130 us -> none
    pallas_call x0 -> x12, Pallas kernels: none -> 105 us  [the longest x2 26.6 us: attend_back(): pl.pallas_call(functools.partial(backward_kernel, first), out_shape=(jax....]
    unnamed x39 -> x56, local copies, waits for them, and re-layouts: 107 us -> 4.14 us
    dot_general x9 -> x0, matrix products: 101 us -> none  [the longest x1 16.4 us: on_device(): jnp.einsum('hji,jhd->ihd', back_dscore, far_queries, preferred_element_ty...]
    ppermute x6 -> x46, starting transfers between devices: 20.9 us -> 94.1 us  [the longest x38 72.9 us: move(): return lax.ppermute(x, ('dp', 'space'), moves(change))]
    ppermute x6 -> x46, waiting for transfers between devices: 45.9 us -> 107 us  [the longest x38 70.3 us: move(): return lax.ppermute(x, ('dp', 'space'), moves(change))]
    all_gather x2 -> x0, waiting for transfers between devices: 40.7 us -> none  [the longest x1 40.7 us: on_device(): grad_weight = lax.all_gather(partial_rows, 'space', axis=0, tiled=True)]
  transfers between devices with their start and end apart: 40 -> 46, of which waited for: 4 -> 12; matrix products, arithmetic and copies ran while one was open for 16% -> 4% of each run, Pallas kernels for 0% -> 32%
where the time goes in v1:
time: 327 us; the launch traced here: 326 us
  waiting for transfers between devices  107 us (33%)
  Pallas kernels  105 us (32%)
  starting transfers between devices  94.1 us (29%)
  local copies, waits for them, and re-layouts  10.4 us (3%)
  other arithmetic  6.9 us (2%)
    ppermute x38, starting transfers between devices, move(): return lax.ppermute(x, ('dp', 'space'), moves(change))  72.9 us
    ppermute x38, waiting for transfers between devices, move(): return lax.ppermute(x, ('dp', 'space'), moves(change))  70.3 us
    ppermute x4, waiting for transfers between devices, to_next(): return lax.ppermute(x, 'space', [(i, i + 1) for i in range(NS - 1)])  34.6 us
    pallas_call x2, Pallas kernels, attend_back(): pl.pallas_call(functools.partial(backward_kernel, first), out_shape=(jax....  26.6 us
    pallas_call x2, Pallas kernels, project_back(): pl.pallas_call(project_back_kernel, out_shape=(jax.ShapeDtypeStruct((8 *...  19.2 us
    pallas_call x2, Pallas kernels, attend(): pl.pallas_call(forward_kernel, out_shape=(jax.ShapeDtypeStruct((heads * H...  18.9 us
    pallas_call x2, Pallas kernels, weight_grad(): pl.pallas_call(weight_grad_kernel, out_shape=(jax.ShapeDtypeStruct((rows...  17.1 us
    ppermute x4, starting transfers between devices, to_next(): return lax.ppermute(x, 'space', [(i, i + 1) for i in range(NS - 1)])  16.1 us
  transfers between devices with their start and end apart: 46, of which 12 were waited for; matrix products, arithmetic and copies ran while one was open for 4% of the time, Pallas kernels for 32%

profile of v1, /device:TPU:0, one launch (start us, length us, event | category | flops | bytes accessed | tf_op | source)
XLA Modules:
  0.0 325.6 jit_solution(2187387366555929758)
XLA Ops:
  0.6 1.7 collective-permute-start.27
  2.3 3.9 %collective-permute-start.6 = (bf16[96,3072]{1,0:T(8,128)(2,1)}, bf16[96,3072]{1,0:T(8,128)(2,1)}, u32[]{:S(2)}, u32[]{:S(2)}) collective-permute-start(bf16[96,3072]{1,0:T(8,128)(2,1)} %refs_0_.1), channel_id=1, source_target_pairs={{0,32},{1,33},{2,34},{3,35},{4,36},{5,37},{6,38},{7,39},{8,40},{9,... | collective-permute-start | bytes 1769480 | tf_op jit(solution)/shard_map/ppermute | solution.py:38
  6.2 0.7 collective-permute-start.5
  6.9 1.3 collective-permute-start.4
  8.2 1.8 constant_dynamic-slice_fusion.11
  10.0 2.2 collective-permute-start.11
  12.3 8.4 %collective-permute-done.6.refs_3_ = bf16[96,3072]{1,0:T(8,128)(2,1)} collective-permute-done((bf16[96,3072]{1,0:T(8,128)(2,1)}, bf16[96,3072]{1,0:T(8,128)(2,1)}, u32[]{:S(2)}, u32[]{:S(2)}) %collective-permute-start.6) | collective-permute-done | bytes 589856 | tf_op jit(solution)/shard_map/ppermute | solution.py:38
  20.7 1.3 collective-permute-start.1
  22.0 11.9 %collective-permute-done.5.refs_2_ = bf16[96,3072]{1,0:T(8,128)(2,1)} collective-permute-done((bf16[96,3072]{1,0:T(8,128)(2,1)}, bf16[96,3072]{1,0:T(8,128)(2,1)}, u32[]{:S(2)}, u32[]{:S(2)}) %collective-permute-start.5) | collective-permute-done | bytes 589856 | tf_op jit(solution)/shard_map/ppermute | solution.py:38
  33.9 2.1 collective-permute-start.14
  36.5 13.8 %collective-permute-done.14.refs_3_ = bf16[96,3072]{1,0:T(8,128)(2,1)S(1)} collective-permute-done((bf16[96,3072]{1,0:T(8,128)(2,1)}, bf16[96,3072]{1,0:T(8,128)(2,1)S(1)}, u32[]{:S(2)}, u32[]{:S(2)}) %collective-permute-start.14) | collective-permute-done | bytes 589856 | tf_op jit(solution)/shard_map/ppermute | solution.py:38
  50.3 1.2 pad_maximum_fusion.1
  51.5 4.5 %collective-permute-start = (bf16[2,384,768]{2,1,0:T(8,128)(2,1)S(1)}, bf16[2,384,768]{2,1,0:T(8,128)(2,1)}, u32[]{:S(2)}, u32[]{:S(2)}) collective-permute-start(bf16[2,384,768]{2,1,0:T(8,128)(2,1)S(1)} %pad_maximum_fusion), channel_id=1, source_target_pairs={{0,1},{1,2},{2,3},{3,4},{4,5},{5,6},{6,7},{8,9},{9,10},{10,11},{11... | collective-permute-start | bytes 3538952 | tf_op jit(solution)/shard_map/ppermute | solution.py:70
  56.1 1.3 collective-permute-start.3
  57.4 5.6 %collective-permute-start.2 = (bf16[2,384,768]{2,1,0:T(8,128)(2,1)}, bf16[2,384,768]{2,1,0:T(8,128)(2,1)}, u32[]{:S(2)}, u32[]{:S(2)}) collective-permute-start(bf16[2,384,768]{2,1,0:T(8,128)(2,1)} %pad_maximum_fusion.1), channel_id=1, source_target_pairs={{0,1},{1,2},{2,3},{3,4},{4,5},{5,6},{6,7},{8,9},{9,10},{10,11},{11... | collective-permute-start | bytes 3538952 | tf_op jit(solution)/shard_map/ppermute | solution.py:70
  63.1 0.8 and_reduce_fusion
  65.8 15.5 %collective-permute-done.left_ref = bf16[2,384,768]{2,1,0:T(8,128)(2,1)} collective-permute-done((bf16[2,384,768]{2,1,0:T(8,128)(2,1)S(1)}, bf16[2,384,768]{2,1,0:T(8,128)(2,1)}, u32[]{:S(2)}, u32[]{:S(2)}) %collective-permute-start) | collective-permute-done | bytes 1179680 | tf_op jit(solution)/shard_map/ppermute | solution.py:70
  81.3 2.9 collective-permute-start.13
  84.2 2.1 collective-permute-done.3.right_ref
  86.3 0.8 collective-permute-start.12
  87.1 19.1 %collective-permute-done.2.left_ref = bf16[2,384,768]{2,1,0:T(8,128)(2,1)} collective-permute-done((bf16[2,384,768]{2,1,0:T(8,128)(2,1)}, bf16[2,384,768]{2,1,0:T(8,128)(2,1)}, u32[]{:S(2)}, u32[]{:S(2)}) %collective-permute-start.2) | collective-permute-done | bytes 1179680 | tf_op jit(solution)/shard_map/ppermute | solution.py:70
  107.9 9.4 %attend.3 = (bf16[768,384]{1,0:T(8,128)(2,1)}, f32[6,1,384]{2,1,0:T(1,128)}) custom-call(s32[3]{0:T(128)} %add_add_fusion.1.info, bf16[384,1536]{1,0:T(8,128)(2,1)} %bitcast.86, bf16[384,1536]{1,0:T(8,128)(2,1)} %bitcast.66, bf16[384,1536]{1,0:T(8,128)(2,1)} %bitcast.70, bf16[2,384,768]{2,1,0:T(8,128)(2,1)} %collective-permute-done.2.left_ref, ...), custom_call_target="tpu_custom_call" | custom-call | flops 1811939328 | bytes 4718592 | tf_op jit(solution)/shard_map/attend/pallas_call | solution.py:118
  117.4 1.8 constant_dynamic-slice_fusion.3
  119.2 9.5 %attend.2 = (bf16[768,384]{1,0:T(8,128)(2,1)}, f32[6,1,384]{2,1,0:T(1,128)}) custom-call(s32[3]{0:T(128)} %add_add_fusion.info, bf16[384,1536]{1,0:T(8,128)(2,1)} %bitcast.87, bf16[384,1536]{1,0:T(8,128)(2,1)} %bitcast.67, bf16[384,1536]{1,0:T(8,128)(2,1)} %bitcast.71, bf16[2,384,768]{2,1,0:T(8,128)(2,1)} %collective-permute-done.left_ref, ...), custom_call_target="tpu_custom_call" | custom-call | flops 1811939328 | bytes 4718592 | tf_op jit(solution)/shard_map/attend/pallas_call | solution.py:118
  128.7 4.2 %collective-permute-start.33 = (bf16[192,384]{1,0:T(8,128)(2,1)S(1)}, bf16[192,384]{1,0:T(8,128)(2,1)}, u32[]{:S(2)}, u32[]{:S(2)}) collective-permute-start(bf16[192,384]{1,0:T(8,128)(2,1)S(1)} %bitcast.85), channel_id=1, source_target_pairs={{0,4},{1,5},{2,6},{3,7},{4,0},{5,1},{6,2},{7,3},{8,12},{9,13},{10,... | collective-permute-start | bytes 442376 | tf_op jit(solution)/shard_map/ppermute | solution.py:38
  133.2 9.6 %project_back.2 = (bf16[768,3072]{1,0:T(8,128)(2,1)}, bf16[768,384]{1,0:T(8,128)(2,1)}) custom-call(s32[8]{0:T(128)} %stack.132.place, bf16[96,3072]{1,0:T(8,128)(2,1)} %refs_0_.1, bf16[96,3072]{1,0:T(8,128)(2,1)} %collective-permute-done.4.refs_1_, bf16[96,3072]{1,0:T(8,128)(2,1)} %collective-permute-done.5.refs_2_, ...), custom_call_target="tpu_custom_call" | custom-call | flops 1811939328 | bytes 11796480 | tf_op jit(solution)/shard_map/project_back/pallas_call | solution.py:254
  142.9 0.7 constant_dynamic-slice_fusion.7
  145.1 13.2 %attend_back.2 = (bf16[384,1536]{1,0:T(8,128)(2,1)}, f32[2,384,768]{2,1,0:T(8,128)}, bf16[2,384,768]{2,1,0:T(8,128)(2,1)}, bf16[2,384,768]{2,1,0:T(8,128)(2,1)}) custom-call(s32[3]{0:T(128)} %add_add_fusion.info, bf16[384,1536]{1,0:T(8,128)(2,1)} %bitcast.88, bf16[384,1536]{1,0:T(8,128)(2,1)} %bitcast.68, bf16[384,1536]{1,0:T(8,128)(2,1)} %bitcast.72, ...), custom_call_target="tpu_custom_call" | custom-call | flops 4529848320 | bytes 9437184 | tf_op jit(solution)/shard_map/attend_back/pallas_call | solution.py:174
  158.3 1.7 collective-permute-start.24
  160.1 8.5 %weight_grad.3 = (bf16[48,3072]{1,0:T(8,128)(2,1)}, bf16[48,3072]{1,0:T(8,128)(2,1)}, bf16[48,3072]{1,0:T(8,128)(2,1)}, bf16[48,3072]{1,0:T(8,128)(2,1)}) custom-call(s32[4]{0:T(128)} %pad_add_fusion.place, bf16[192,384]{1,0:T(8,128)(2,1)} %bitcast.79, bf16[192,384]{1,0:T(8,128)(2,1)} %collective-permute-done.32.refs_1_, ...), custom_call_target="tpu_custom_call" | custom-call | flops 1811939328 | bytes 11796480 | tf_op jit(solution)/shard_map/weight_grad/pallas_call | solution.py:315
  169.2 2.4 collective-permute-start.35
  171.5 2.2 collective-permute-start.36
  173.7 1.8 collective-permute-start.37
  175.5 9.5 %project_back.3 = (bf16[768,3072]{1,0:T(8,128)(2,1)}, bf16[768,384]{1,0:T(8,128)(2,1)}) custom-call(s32[8]{0:T(128)} %stack.132.place, bf16[96,3072]{1,0:T(8,128)(2,1)} %copy-done.7, bf16[96,3072]{1,0:T(8,128)(2,1)} %copy-done.13, bf16[96,3072]{1,0:T(8,128)(2,1)} %copy-done.12, bf16[96,3072]{1,0:T(8,128)(2,1)} %copy-done.9, bf16[96,3072]{1,0:T(8,128)(2,1)} %copy-done.16, ...), custom_call_target="tpu_custom_call" | custom-call | flops 1811939328 | bytes 11796480 | tf_op jit(solution)/shard_map/project_back/pallas_call | solution.py:254
  185.1 1.4 collective-permute-start.21
  187.1 8.6 %weight_grad.2 = (bf16[48,3072]{1,0:T(8,128)(2,1)}, bf16[48,3072]{1,0:T(8,128)(2,1)}, bf16[48,3072]{1,0:T(8,128)(2,1)}, bf16[48,3072]{1,0:T(8,128)(2,1)}) custom-call(s32[4]{0:T(128)} %pad_add_fusion.place, bf16[192,384]{1,0:T(8,128)(2,1)} %bitcast.78, bf16[192,384]{1,0:T(8,128)(2,1)} %copy-done.25, bf16[192,384]{1,0:T(8,128)(2,1)} %copy-done.23, ...), custom_call_target="tpu_custom_call" | custom-call | flops 1811939328 | bytes 11796480 | tf_op jit(solution)/shard_map/weight_grad/pallas_call | solution.py:315
  195.8 1.1 collective-permute-start.29
  196.8 2.2 collective-permute-start.30
  199.8 3.1 collective-permute-start.38
  202.9 13.4 %attend_back.3 = (bf16[384,1536]{1,0:T(8,128)(2,1)}, f32[2,384,768]{2,1,0:T(8,128)}, bf16[2,384,768]{2,1,0:T(8,128)(2,1)}, bf16[2,384,768]{2,1,0:T(8,128)(2,1)}) custom-call(s32[3]{0:T(128)} %add_add_fusion.1.info, bf16[384,1536]{1,0:T(8,128)(2,1)} %bitcast.89, bf16[384,1536]{1,0:T(8,128)(2,1)} %bitcast.69, ...), custom_call_target="tpu_custom_call", output_to_operand_aliasing={{0}: (9, {})} | custom-call | flops 4529848320 | bytes 9437184 | tf_op jit(solution)/shard_map/attend_back/pallas_call | solution.py:174
  216.3 1.3 collective-permute-start.22
  217.6 4.6 %collective-permute-start.19 = (bf16[2,384,768]{2,1,0:T(8,128)(2,1)}, bf16[2,384,768]{2,1,0:T(8,128)(2,1)S(1)}, u32[]{:S(2)}, u32[]{:S(2)}) collective-permute-start(bf16[2,384,768]{2,1,0:T(8,128)(2,1)} %get-tuple-element.44), channel_id=1, source_target_pairs={{0,1},{1,2},{2,3},{3,4},{4,5},{5,6},{6,7},{8,9},{9,10},{10,11},{11... | collective-permute-start | bytes 3538952 | tf_op jit(solution)/shard_map/ppermute | solution.py:70
  222.3 1.3 collective-permute-start.20
  225.1 2.6 collective-permute-start.39
  227.8 19.7 %collective-permute-done.39 = bf16[48,768]{1,0:T(8,128)(2,1)} collective-permute-done((bf16[48,768]{1,0:T(8,128)(2,1)S(1)}, bf16[48,768]{1,0:T(8,128)(2,1)}, u32[]{:S(2)}, u32[]{:S(2)}) %collective-permute-start.39) | collective-permute-done | bytes 73760 | tf_op jit(solution)/shard_map/ppermute | solution.py:38
  247.5 5.1 %collective-permute-start.41 = (bf16[48,768]{1,0:T(8,128)(2,1)S(1)}, bf16[48,768]{1,0:T(8,128)(2,1)}, u32[]{:S(2)}, u32[]{:S(2)}) collective-permute-start(bf16[48,768]{1,0:T(8,128)(2,1)S(1)} %get-tuple-element.76), channel_id=1, source_target_pairs={{0,2},{1,3},{2,0},{3,1},{4,6},{5,7},{6,4},{7,5},{8,10},{9,11},{10,... | collective-permute-start | bytes 221192 | tf_op jit(solution)/shard_map/ppermute | solution.py:38
  252.6 2.4 collective-permute-done.41
  255.0 20.2 %collective-permute-start.40 = (bf16[48,768]{1,0:T(8,128)(2,1)}, bf16[48,768]{1,0:T(8,128)(2,1)}, u32[]{:S(2)}, u32[]{:S(2)}) collective-permute-start(bf16[48,768]{1,0:T(8,128)(2,1)} %get-tuple-element.77), channel_id=1, source_target_pairs={{0,3},{1,0},{2,1},{3,2},{4,7},{5,4},{6,5},{7,6},{8,11},{9,8},{10,9... | collective-permute-start | bytes 221192 | tf_op jit(solution)/shard_map/ppermute | solution.py:38
  275.2 3.7 %collective-permute-done.40 = bf16[48,768]{1,0:T(8,128)(2,1)} collective-permute-done((bf16[48,768]{1,0:T(8,128)(2,1)}, bf16[48,768]{1,0:T(8,128)(2,1)}, u32[]{:S(2)}, u32[]{:S(2)}) %collective-permute-start.40) | collective-permute-done | bytes 73760 | tf_op jit(solution)/shard_map/ppermute | solution.py:38
  278.9 1.7 add_convert_fusion.2
  280.6 2.2 collective-permute-start.44
  282.8 2.5 collective-permute-done.44
  285.2 1.7 collective-permute-start.43
  287.0 4.5 %collective-permute-done.43 = bf16[48,768]{1,0:T(8,128)(2,1)} collective-permute-done((bf16[48,768]{1,0:T(8,128)(2,1)}, bf16[48,768]{1,0:T(8,128)(2,1)}, u32[]{:S(2)}, u32[]{:S(2)}) %collective-permute-start.43) | collective-permute-done | bytes 73760 | tf_op jit(solution)/shard_map/ppermute | solution.py:38
  291.4 2.0 collective-permute-start.42
  294.0 3.4 %collective-permute-done.42 = bf16[48,768]{1,0:T(8,128)(2,1)} collective-permute-done((bf16[48,768]{1,0:T(8,128)(2,1)}, bf16[48,768]{1,0:T(8,128)(2,1)}, u32[]{:S(2)}, u32[]{:S(2)}) %collective-permute-start.42) | collective-permute-done | bytes 73760 | tf_op jit(solution)/shard_map/ppermute | solution.py:38
  297.5 1.0 pad_maximum_fusion.2.mine_ref
  298.5 1.7 collective-permute-start.45
  300.2 9.3 %project.1 = bf16[384,3072]{1,0:T(8,128)(2,1)} custom-call(bf16[768,384]{1,0:T(8,128)(2,1)} %get-tuple-element.33.a_ref.attn_ref, bf16[768,384]{1,0:T(8,128)(2,1)} %get-tuple-element.34.b_ref.attn_ref, bf16[768,3072]{1,0:T(8,128)(2,1)} %get-tuple-element.35.wa_ref, bf16[768,3072]{1,0:T(8,128)(2,1)} %get-tuple-element.36.wb_ref), custom_call_target="tpu_custom_call" | custom-call | flops 3623878656 | bytes 11796480 | tf_op jit(solution)/shard_map/project/pallas_call | solution.py:288
  309.5 1.0 copy-done.1
  310.9 5.8 %join.2 = (bf16[384,1536]{1,0:T(8,128)(2,1)}, bf16[384,1536]{1,0:T(8,128)(2,1)}) custom-call(s32[3]{0:T(128)} %add_add_fusion.info, f32[2,384,768]{2,1,0:T(8,128)} %get-tuple-element.46.own_ref, bf16[2,384,768]{2,1,0:T(8,128)(2,1)} %copy-done.1, bf16[2,384,768]{2,1,0:T(8,128)(2,1)} %copy-done.3), custom_call_target="tpu_custom_call" | custom-call | flops 1179648 | bytes 5898240 | tf_op jit(solution)/shard_map/join/pallas_call | solution.py:212
  316.7 1.0 copy-done.2
  317.6 5.8 %join.3 = (bf16[384,1536]{1,0:T(8,128)(2,1)}, bf16[384,1536]{1,0:T(8,128)(2,1)}) custom-call(s32[3]{0:T(128)} %add_add_fusion.1.info, f32[2,384,768]{2,1,0:T(8,128)} %get-tuple-element.43.own_ref, bf16[2,384,768]{2,1,0:T(8,128)(2,1)} %copy-done.2, bf16[2,384,768]{2,1,0:T(8,128)(2,1)} %collective-permute-done.20.b_ref, ...), custom_call_target="tpu_custom_call", output_to_operand_aliasing={{0}: (4, {}), {1}: (5, {})} | custom-call | flops 1179648 | bytes 5898240 | tf_op jit(solution)/shard_map/join/pallas_call | solution.py:212
  323.4 2.2 place_pieces.1
  (112 shorter events, 9.4 us)
Async XLA Ops:
  0.6 62.3 %collective-permute-start.27 = (bf16[384,3072]{1,0:T(8,128)(2,1)}, bf16[384,3072]{1,0:T(8,128)(2,1)}, u32[]{:S(2)}, u32[]{:S(2)}) collective-permute-start(bf16[384,3072]{1,0:T(8,128)(2,1)} %bitcast.60), channel_id=1, source_target_pairs={{0,4},{1,5},{2,6},{3,7},{4,0},{5,1},{6,2},{7,3},{8,12},{9,13},{10,... | collective-permute-start | bytes 7077896 | tf_op jit(solution)/shard_map/ppermute | solution.py:38
  2.3 7.7 %collective-permute-start.7 = (bf16[96,3072]{1,0:T(8,128)(2,1)}, bf16[96,3072]{1,0:T(8,128)(2,1)S(1)}, u32[]{:S(2)}, u32[]{:S(2)}) collective-permute-start(bf16[96,3072]{1,0:T(8,128)(2,1)} %refs_0_.1), channel_id=1, source_target_pairs={{0,8},{1,9},{2,10},{3,11},{4,12},{5,13},{6,14},{7,15},{8,0},{9,1},... | collective-permute-start | bytes 1769480 | tf_op jit(solution)/shard_map/ppermute | solution.py:38
  2.3 18.4 %collective-permute-start.6 = (bf16[96,3072]{1,0:T(8,128)(2,1)}, bf16[96,3072]{1,0:T(8,128)(2,1)}, u32[]{:S(2)}, u32[]{:S(2)}) collective-permute-start(bf16[96,3072]{1,0:T(8,128)(2,1)} %refs_0_.1), channel_id=1, source_target_pairs={{0,32},{1,33},{2,34},{3,35},{4,36},{5,37},{6,38},{7,39},{8,40},{9,... | collective-permute-start | bytes 1769480 | tf_op jit(solution)/shard_map/ppermute | solution.py:38
  6.2 27.7 %collective-permute-start.5 = (bf16[96,3072]{1,0:T(8,128)(2,1)}, bf16[96,3072]{1,0:T(8,128)(2,1)}, u32[]{:S(2)}, u32[]{:S(2)}) collective-permute-start(bf16[96,3072]{1,0:T(8,128)(2,1)} %refs_0_.1), channel_id=1, source_target_pairs={{0,48},{1,49},{2,50},{3,51},{4,52},{5,53},{6,54},{7,55},{8,56},{9,... | collective-permute-start | bytes 1769480 | tf_op jit(solution)/shard_map/ppermute | solution.py:38
  6.9 29.1 %collective-permute-start.4 = (bf16[96,3072]{1,0:T(8,128)(2,1)}, bf16[96,3072]{1,0:T(8,128)(2,1)}, u32[]{:S(2)}, u32[]{:S(2)}) collective-permute-start(bf16[96,3072]{1,0:T(8,128)(2,1)} %refs_0_.1), channel_id=1, source_target_pairs={{0,16},{1,17},{2,18},{3,19},{4,20},{5,21},{6,22},{7,23},{8,24},{9,... | collective-permute-start | bytes 1769480 | tf_op jit(solution)/shard_map/ppermute | solution.py:38
  8.2 1.8 copy-start.6
  10.0 2.2 copy-start.11
  10.0 26.0 %collective-permute-start.11 = (bf16[96,3072]{1,0:T(8,128)(2,1)S(1)}, bf16[96,3072]{1,0:T(8,128)(2,1)S(1)}, u32[]{:S(2)}, u32[]{:S(2)}) collective-permute-start(bf16[96,3072]{1,0:T(8,128)(2,1)S(1)} %copy-done.6), channel_id=1, source_target_pairs={{0,68},{1,69},{2,70},{3,71},{4,64},{5,65},{6,66},{7,67},{8,76},{9,... | collective-permute-start | bytes 1769480 | tf_op jit(solution)/shard_map/ppermute | solution.py:38
  12.2 38.1 %copy-start = (bf16[1,384,3072]{2,1,0:T(8,128)(2,1)S(1)}, bf16[1,384,3072]{2,1,0:T(8,128)(2,1)}, u32[]{:S(2)}) copy-start(bf16[1,384,3072]{2,1,0:T(8,128)(2,1)} %param.10) | copy-start | bytes 7077892
  20.7 36.7 %collective-permute-start.1 = (bf16[2,384,768]{2,1,0:T(8,128)(2,1)S(1)}, bf16[2,384,768]{2,1,0:T(8,128)(2,1)S(1)}, u32[]{:S(2)}, u32[]{:S(2)}) collective-permute-start(bf16[2,384,768]{2,1,0:T(8,128)(2,1)S(1)} %pad_maximum_fusion), channel_id=1, source_target_pairs={{1,0},{2,1},{3,2},{4,3},{5,4},{6,5},{7,6},{9,8},{10,9},{11,10},{12... | collective-permute-start | bytes 3538952 | tf_op jit(solution)/shard_map/ppermute | solution.py:74
  33.9 16.4 %collective-permute-start.14 = (bf16[96,3072]{1,0:T(8,128)(2,1)}, bf16[96,3072]{1,0:T(8,128)(2,1)S(1)}, u32[]{:S(2)}, u32[]{:S(2)}) collective-permute-start(bf16[96,3072]{1,0:T(8,128)(2,1)} %collective-permute-done.6.refs_3_), channel_id=1, source_target_pairs={{0,68},{1,69},{2,70},{3,71},{4,64},{5,65},{6,66},{7,67},{8,76},{9,... | collective-permute-start | bytes 1769480 | tf_op jit(solution)/shard_map/ppermute | solution.py:38
  36.0 15.5 %collective-permute-start.10 = (bf16[96,3072]{1,0:T(8,128)(2,1)}, bf16[96,3072]{1,0:T(8,128)(2,1)S(1)}, u32[]{:S(2)}, u32[]{:S(2)}) collective-permute-start(bf16[96,3072]{1,0:T(8,128)(2,1)} %collective-permute-done.6.refs_3_), channel_id=1, source_target_pairs={{0,8},{1,9},{2,10},{3,11},{4,12},{5,13},{6,14},{7,15},{8,0},{9,1},... | collective-permute-start | bytes 1769480 | tf_op jit(solution)/shard_map/ppermute | solution.py:38
  36.0 15.5 %copy-start.7 = (bf16[96,3072]{1,0:T(8,128)(2,1)}, bf16[96,3072]{1,0:T(8,128)(2,1)S(1)}, u32[]{:S(2)}) copy-start(bf16[96,3072]{1,0:T(8,128)(2,1)S(1)} %collective-permute-done.11.refs_0_) | copy-start | bytes 1769476
  36.0 20.0 %collective-permute-start.9 = (bf16[96,3072]{1,0:T(8,128)(2,1)}, bf16[96,3072]{1,0:T(8,128)(2,1)S(1)}, u32[]{:S(2)}, u32[]{:S(2)}) collective-permute-start(bf16[96,3072]{1,0:T(8,128)(2,1)} %collective-permute-done.5.refs_2_), channel_id=1, source_target_pairs={{0,8},{1,9},{2,10},{3,11},{4,12},{5,13},{6,14},{7,15},{8,0},{9,1},... | collective-permute-start | bytes 1769480 | tf_op jit(solution)/shard_map/ppermute | solution.py:38
  50.3 94.5 %collective-permute-start.26 = (bf16[384,3072]{1,0:T(8,128)(2,1)S(1)}, bf16[384,3072]{1,0:T(8,128)(2,1)}, u32[]{:S(2)}, u32[]{:S(2)}) collective-permute-start(bf16[384,3072]{1,0:T(8,128)(2,1)S(1)} %bitcast.65), channel_id=1, source_target_pairs={{0,8},{1,9},{2,10},{3,11},{4,12},{5,13},{6,14},{7,15},{8,0},{9,1},... | collective-permute-start | bytes 7077896 | tf_op jit(solution)/shard_map/ppermute | solution.py:38
  50.3 12.8 %copy-start.26 = (s32[8,3]{0,1:T(4,128)S(1)}, s32[8,3]{0,1:T(4,128)}, u32[]{:S(2)}) copy-start(s32[8,3]{0,1:T(4,128)} %param.11) | copy-start | bytes 292
  51.5 5.9 %copy-start.14 = (bf16[96,3072]{1,0:T(8,128)(2,1)}, bf16[96,3072]{1,0:T(8,128)(2,1)S(1)}, u32[]{:S(2)}) copy-start(bf16[96,3072]{1,0:T(8,128)(2,1)S(1)} %collective-permute-done.10.refs_7_) | copy-start | bytes 1769476
  51.5 29.8 %collective-permute-start = (bf16[2,384,768]{2,1,0:T(8,128)(2,1)S(1)}, bf16[2,384,768]{2,1,0:T(8,128)(2,1)}, u32[]{:S(2)}, u32[]{:S(2)}) collective-permute-start(bf16[2,384,768]{2,1,0:T(8,128)(2,1)S(1)} %pad_maximum_fusion), channel_id=1, source_target_pairs={{0,1},{1,2},{2,3},{3,4},{4,5},{5,6},{6,7},{8,9},{9,10},{10,11},{11... | collective-permute-start | bytes 3538952 | tf_op jit(solution)/shard_map/ppermute | solution.py:70
  56.1 6.9 %copy-start.15 = (bf16[96,3072]{1,0:T(8,128)(2,1)}, bf16[96,3072]{1,0:T(8,128)(2,1)S(1)}, u32[]{:S(2)}) copy-start(bf16[96,3072]{1,0:T(8,128)(2,1)S(1)} %collective-permute-done.9.refs_6_) | copy-start | bytes 1769476
  56.1 30.2 %collective-permute-start.3 = (bf16[2,384,768]{2,1,0:T(8,128)(2,1)}, bf16[2,384,768]{2,1,0:T(8,128)(2,1)}, u32[]{:S(2)}, u32[]{:S(2)}) collective-permute-start(bf16[2,384,768]{2,1,0:T(8,128)(2,1)} %pad_maximum_fusion.1), channel_id=1, source_target_pairs={{1,0},{2,1},{3,2},{4,3},{5,4},{6,5},{7,6},{9,8},{10,9},{11,10},{12... | collective-permute-start | bytes 3538952 | tf_op jit(solution)/shard_map/ppermute | solution.py:74
  57.4 5.6 %copy-start.27 = (bf16[2,384,768]{2,1,0:T(8,128)(2,1)}, bf16[2,384,768]{2,1,0:T(8,128)(2,1)S(1)}, u32[]{:S(2)}) copy-start(bf16[2,384,768]{2,1,0:T(8,128)(2,1)S(1)} %collective-permute-done.1.right_ref) | copy-start | bytes 3538948
  57.4 48.8 %collective-permute-start.2 = (bf16[2,384,768]{2,1,0:T(8,128)(2,1)}, bf16[2,384,768]{2,1,0:T(8,128)(2,1)}, u32[]{:S(2)}, u32[]{:S(2)}) collective-permute-start(bf16[2,384,768]{2,1,0:T(8,128)(2,1)} %pad_maximum_fusion.1), channel_id=1, source_target_pairs={{0,1},{1,2},{2,3},{3,4},{4,5},{5,6},{6,7},{8,9},{9,10},{10,11},{11... | collective-permute-start | bytes 3538952 | tf_op jit(solution)/shard_map/ppermute | solution.py:70
  63.0 95.4 %collective-permute-start.28 = (bf16[384,3072]{1,0:T(8,128)(2,1)}, bf16[384,3072]{1,0:T(8,128)(2,1)}, u32[]{:S(2)}, u32[]{:S(2)}) collective-permute-start(bf16[384,3072]{1,0:T(8,128)(2,1)} %collective-permute-done.27.refs_6_), channel_id=1, source_target_pairs={{0,8},{1,9},{2,10},{3,11},{4,12},{5,13},{6,14},{7,15},{8,0},{9,1},... | collective-permute-start | bytes 7077896 | tf_op jit(solution)/shard_map/ppermute | solution.py:38
  81.3 51.6 %collective-permute-start.13 = (bf16[96,3072]{1,0:T(8,128)(2,1)}, bf16[96,3072]{1,0:T(8,128)(2,1)S(1)}, u32[]{:S(2)}, u32[]{:S(2)}) collective-permute-start(bf16[96,3072]{1,0:T(8,128)(2,1)} %copy-done.7), channel_id=1, source_target_pairs={{0,48},{1,49},{2,50},{3,51},{4,52},{5,53},{6,54},{7,55},{8,56},{9,... | collective-permute-start | bytes 1769480 | tf_op jit(solution)/shard_map/ppermute | solution.py:38
  86.3 46.8 %collective-permute-start.12 = (bf16[96,3072]{1,0:T(8,128)(2,1)}, bf16[96,3072]{1,0:T(8,128)(2,1)S(1)}, u32[]{:S(2)}, u32[]{:S(2)}) collective-permute-start(bf16[96,3072]{1,0:T(8,128)(2,1)} %copy-done.7), channel_id=1, source_target_pairs={{0,16},{1,17},{2,18},{3,19},{4,20},{5,21},{6,22},{7,23},{8,24},{9,... | collective-permute-start | bytes 1769480 | tf_op jit(solution)/shard_map/ppermute | solution.py:38
  106.2 22.5 %collective-permute-start.8 = (bf16[96,3072]{1,0:T(8,128)(2,1)}, bf16[96,3072]{1,0:T(8,128)(2,1)}, u32[]{:S(2)}, u32[]{:S(2)}) collective-permute-start(bf16[96,3072]{1,0:T(8,128)(2,1)} %collective-permute-done.4.refs_1_), channel_id=1, source_target_pairs={{0,8},{1,9},{2,10},{3,11},{4,12},{5,13},{6,14},{7,15},{8,0},{9,1},... | collective-permute-start | bytes 1769480 | tf_op jit(solution)/shard_map/ppermute | solution.py:38
  128.7 15.0 %collective-permute-start.33 = (bf16[192,384]{1,0:T(8,128)(2,1)S(1)}, bf16[192,384]{1,0:T(8,128)(2,1)}, u32[]{:S(2)}, u32[]{:S(2)}) collective-permute-start(bf16[192,384]{1,0:T(8,128)(2,1)S(1)} %bitcast.85), channel_id=1, source_target_pairs={{0,4},{1,5},{2,6},{3,7},{4,0},{5,1},{6,2},{7,3},{8,12},{9,13},{10,... | collective-permute-start | bytes 442376 | tf_op jit(solution)/shard_map/ppermute | solution.py:38
  132.8 11.7 %copy-start.12 = (bf16[96,3072]{1,0:T(8,128)(2,1)}, bf16[96,3072]{1,0:T(8,128)(2,1)S(1)}, u32[]{:S(2)}) copy-start(bf16[96,3072]{1,0:T(8,128)(2,1)S(1)} %collective-permute-done.13.refs_2_) | copy-start | bytes 1769476
  132.8 11.4 %collective-permute-start.34 = (bf16[192,384]{1,0:T(8,128)(2,1)S(1)}, bf16[192,384]{1,0:T(8,128)(2,1)}, u32[]{:S(2)}, u32[]{:S(2)}) collective-permute-start(bf16[192,384]{1,0:T(8,128)(2,1)S(1)} %bitcast.84), channel_id=1, source_target_pairs={{0,12},{1,13},{2,14},{3,15},{4,8},{5,9},{6,10},{7,11},{8,4},{9,5},... | collective-permute-start | bytes 442376 | tf_op jit(solution)/shard_map/ppermute | solution.py:38
  133.1 11.7 %copy-start.13 = (bf16[96,3072]{1,0:T(8,128)(2,1)}, bf16[96,3072]{1,0:T(8,128)(2,1)S(1)}, u32[]{:S(2)}) copy-start(bf16[96,3072]{1,0:T(8,128)(2,1)S(1)} %collective-permute-done.12.refs_1_) | copy-start | bytes 1769476
  133.1 9.8 %copy-start.20 = (bf16[768,384]{1,0:T(8,128)(2,1)S(1)}, bf16[768,384]{1,0:T(8,128)(2,1)}, u32[]{:S(2)}) copy-start(bf16[768,384]{1,0:T(8,128)(2,1)} %get-tuple-element.33.a_ref.attn_ref) | copy-start | bytes 1769476
  133.1 11.4 %collective-permute-start.32 = (bf16[192,384]{1,0:T(8,128)(2,1)S(1)}, bf16[192,384]{1,0:T(8,128)(2,1)}, u32[]{:S(2)}, u32[]{:S(2)}) collective-permute-start(bf16[192,384]{1,0:T(8,128)(2,1)S(1)} %bitcast.83), channel_id=1, source_target_pairs={{0,8},{1,9},{2,10},{3,11},{4,12},{5,13},{6,14},{7,15},{8,0},{9,1},... | collective-permute-start | bytes 442376 | tf_op jit(solution)/shard_map/ppermute | solution.py:38
  144.0 24.6 %collective-permute-start.15 = (bf16[96,3072]{1,0:T(8,128)(2,1)S(1)}, bf16[96,3072]{1,0:T(8,128)(2,1)S(1)}, u32[]{:S(2)}, u32[]{:S(2)}) collective-permute-start(bf16[96,3072]{1,0:T(8,128)(2,1)S(1)} %copy-done.8), channel_id=1, source_target_pairs={{0,8},{1,9},{2,10},{3,11},{4,12},{5,13},{6,14},{7,15},{8,0},{9,1},... | collective-permute-start | bytes 1769480 | tf_op jit(solution)/shard_map/ppermute | solution.py:38
  144.3 24.9 %collective-permute-start.18 = (bf16[96,3072]{1,0:T(8,128)(2,1)S(1)}, bf16[96,3072]{1,0:T(8,128)(2,1)S(1)}, u32[]{:S(2)}, u32[]{:S(2)}) collective-permute-start(bf16[96,3072]{1,0:T(8,128)(2,1)S(1)} %copy-done.10), channel_id=1, source_target_pairs={{0,8},{1,9},{2,10},{3,11},{4,12},{5,13},{6,14},{7,15},{8,0},{9,1},... | collective-permute-start | bytes 1769480 | tf_op jit(solution)/shard_map/ppermute | solution.py:38
  144.5 27.0 %collective-permute-start.17 = (bf16[96,3072]{1,0:T(8,128)(2,1)S(1)}, bf16[96,3072]{1,0:T(8,128)(2,1)S(1)}, u32[]{:S(2)}, u32[]{:S(2)}) collective-permute-start(bf16[96,3072]{1,0:T(8,128)(2,1)S(1)} %collective-permute-done.13.refs_2_), channel_id=1, source_target_pairs={{0,8},{1,9},{2,10},{3,11},{4,12},{5,13},{6,14},{7,15},{8,0},{9,1},... | collective-permute-start | bytes 1769480 | tf_op jit(solution)/shard_map/ppermute | solution.py:38
  144.8 28.9 %collective-permute-start.16 = (bf16[96,3072]{1,0:T(8,128)(2,1)S(1)}, bf16[96,3072]{1,0:T(8,128)(2,1)S(1)}, u32[]{:S(2)}, u32[]{:S(2)}) collective-permute-start(bf16[96,3072]{1,0:T(8,128)(2,1)S(1)} %collective-permute-done.12.refs_1_), channel_id=1, source_target_pairs={{0,8},{1,9},{2,10},{3,11},{4,12},{5,13},{6,14},{7,15},{8,0},{9,1},... | collective-permute-start | bytes 1769480 | tf_op jit(solution)/shard_map/ppermute | solution.py:38
  158.3 10.4 %collective-permute-start.24 = (bf16[192,384]{1,0:T(8,128)(2,1)S(1)}, bf16[192,384]{1,0:T(8,128)(2,1)S(1)}, u32[]{:S(2)}, u32[]{:S(2)}) collective-permute-start(bf16[192,384]{1,0:T(8,128)(2,1)S(1)} %bitcast.82), channel_id=1, source_target_pairs={{0,4},{1,5},{2,6},{3,7},{4,0},{5,1},{6,2},{7,3},{8,12},{9,13},{10,... | collective-permute-start | bytes 442376 | tf_op jit(solution)/shard_map/ppermute | solution.py:38
  168.6 6.9 %copy-start.16 = (bf16[96,3072]{1,0:T(8,128)(2,1)}, bf16[96,3072]{1,0:T(8,128)(2,1)S(1)}, u32[]{:S(2)}) copy-start(bf16[96,3072]{1,0:T(8,128)(2,1)S(1)} %collective-permute-done.15.refs_4_) | copy-start | bytes 1769476
  168.6 16.4 %collective-permute-start.25 = (bf16[192,384]{1,0:T(8,128)(2,1)S(1)}, bf16[192,384]{1,0:T(8,128)(2,1)S(1)}, u32[]{:S(2)}, u32[]{:S(2)}) collective-permute-start(bf16[192,384]{1,0:T(8,128)(2,1)S(1)} %bitcast.81), channel_id=1, source_target_pairs={{0,12},{1,13},{2,14},{3,15},{4,8},{5,9},{6,10},{7,11},{8,4},{9,5},... | collective-permute-start | bytes 442376 | tf_op jit(solution)/shard_map/ppermute | solution.py:38
  168.7 16.3 %copy-start.23 = (bf16[192,384]{1,0:T(8,128)(2,1)}, bf16[192,384]{1,0:T(8,128)(2,1)S(1)}, u32[]{:S(2)}) copy-start(bf16[192,384]{1,0:T(8,128)(2,1)S(1)} %collective-permute-done.24.refs_2_) | copy-start | bytes 442372
  168.7 17.7 %collective-permute-start.23 = (bf16[192,384]{1,0:T(8,128)(2,1)S(1)}, bf16[192,384]{1,0:T(8,128)(2,1)S(1)}, u32[]{:S(2)}, u32[]{:S(2)}) collective-permute-start(bf16[192,384]{1,0:T(8,128)(2,1)S(1)} %bitcast.80), channel_id=1, source_target_pairs={{0,8},{1,9},{2,10},{3,11},{4,12},{5,13},{6,14},{7,15},{8,0},{9,1},... | collective-permute-start | bytes 442376 | tf_op jit(solution)/shard_map/ppermute | solution.py:38
  169.2 6.3 %copy-start.17 = (bf16[96,3072]{1,0:T(8,128)(2,1)}, bf16[96,3072]{1,0:T(8,128)(2,1)S(1)}, u32[]{:S(2)}) copy-start(bf16[96,3072]{1,0:T(8,128)(2,1)S(1)} %collective-permute-done.18.refs_7_) | copy-start | bytes 1769476
  169.2 27.7 %collective-permute-start.35 = (bf16[48,3072]{1,0:T(8,128)(2,1)}, bf16[48,3072]{1,0:T(8,128)(2,1)S(1)}, u32[]{:S(2)}, u32[]{:S(2)}) collective-permute-start(bf16[48,3072]{1,0:T(8,128)(2,1)} %get-tuple-element.58), channel_id=1, source_target_pairs={{0,16},{1,17},{2,18},{3,19},{4,20},{5,21},{6,22},{7,23},{8,24},{9,... | collective-permute-start | bytes 884744 | tf_op jit(solution)/shard_map/ppermute | solution.py:38
  171.5 4.0 %copy-start.18 = (bf16[96,3072]{1,0:T(8,128)(2,1)}, bf16[96,3072]{1,0:T(8,128)(2,1)S(1)}, u32[]{:S(2)}) copy-start(bf16[96,3072]{1,0:T(8,128)(2,1)S(1)} %collective-permute-done.17.refs_6_) | copy-start | bytes 1769476
  171.5 27.5 %collective-permute-start.36 = (bf16[48,3072]{1,0:T(8,128)(2,1)}, bf16[48,3072]{1,0:T(8,128)(2,1)S(1)}, u32[]{:S(2)}, u32[]{:S(2)}) collective-permute-start(bf16[48,3072]{1,0:T(8,128)(2,1)} %get-tuple-element.59), channel_id=1, source_target_pairs={{0,48},{1,49},{2,50},{3,51},{4,52},{5,53},{6,54},{7,55},{8,56},{9,... | collective-permute-start | bytes 884744 | tf_op jit(solution)/shard_map/ppermute | solution.py:38
  173.7 25.9 %collective-permute-start.37 = (bf16[48,3072]{1,0:T(8,128)(2,1)}, bf16[48,3072]{1,0:T(8,128)(2,1)S(1)}, u32[]{:S(2)}, u32[]{:S(2)}) collective-permute-start(bf16[48,3072]{1,0:T(8,128)(2,1)} %get-tuple-element.60), channel_id=1, source_target_pairs={{0,32},{1,33},{2,34},{3,35},{4,36},{5,37},{6,38},{7,39},{8,40},{9,... | collective-permute-start | bytes 884744 | tf_op jit(solution)/shard_map/ppermute | solution.py:38
  185.1 124.4 %collective-permute-start.21 = (bf16[2,384,768]{2,1,0:T(8,128)(2,1)}, bf16[2,384,768]{2,1,0:T(8,128)(2,1)S(1)}, u32[]{:S(2)}, u32[]{:S(2)}) collective-permute-start(bf16[2,384,768]{2,1,0:T(8,128)(2,1)} %get-tuple-element.47), channel_id=1, source_target_pairs={{0,1},{1,2},{2,3},{3,4},{4,5},{5,6},{6,7},{8,9},{9,10},{10,11},{11... | collective-permute-start | bytes 3538952 | tf_op jit(solution)/shard_map/ppermute | solution.py:70
  187.1 12.5 %copy-start.22 = (bf16[48,3072]{1,0:T(8,128)(2,1)S(1)}, bf16[48,3072]{1,0:T(8,128)(2,1)}, u32[]{:S(2)}) copy-start(bf16[48,3072]{1,0:T(8,128)(2,1)} %get-tuple-element.57) | copy-start | bytes 884740
  195.8 20.5 %collective-permute-start.29 = (bf16[48,3072]{1,0:T(8,128)(2,1)}, bf16[48,3072]{1,0:T(8,128)(2,1)S(1)}, u32[]{:S(2)}, u32[]{:S(2)}) collective-permute-start(bf16[48,3072]{1,0:T(8,128)(2,1)} %get-tuple-element.54), channel_id=1, source_target_pairs={{0,16},{1,17},{2,18},{3,19},{4,20},{5,21},{6,22},{7,23},{8,24},{9,... | collective-permute-start | bytes 884744 | tf_op jit(solution)/shard_map/ppermute | solution.py:38
  196.8 20.8 %collective-permute-start.30 = (bf16[48,3072]{1,0:T(8,128)(2,1)}, bf16[48,3072]{1,0:T(8,128)(2,1)S(1)}, u32[]{:S(2)}, u32[]{:S(2)}) collective-permute-start(bf16[48,3072]{1,0:T(8,128)(2,1)} %get-tuple-element.55), channel_id=1, source_target_pairs={{0,48},{1,49},{2,50},{3,51},{4,52},{5,53},{6,54},{7,55},{8,56},{9,... | collective-permute-start | bytes 884744 | tf_op jit(solution)/shard_map/ppermute | solution.py:38
  199.1 23.2 %collective-permute-start.31 = (bf16[48,3072]{1,0:T(8,128)(2,1)}, bf16[48,3072]{1,0:T(8,128)(2,1)S(1)}, u32[]{:S(2)}, u32[]{:S(2)}) collective-permute-start(bf16[48,3072]{1,0:T(8,128)(2,1)} %get-tuple-element.56), channel_id=1, source_target_pairs={{0,32},{1,33},{2,34},{3,35},{4,36},{5,37},{6,38},{7,39},{8,40},{9,... | collective-permute-start | bytes 884744 | tf_op jit(solution)/shard_map/ppermute | solution.py:38
  199.8 23.8 %collective-permute-start.38 = (bf16[48,3072]{1,0:T(8,128)(2,1)S(1)}, bf16[48,3072]{1,0:T(8,128)(2,1)S(1)}, u32[]{:S(2)}, u32[]{:S(2)}) collective-permute-start(bf16[48,3072]{1,0:T(8,128)(2,1)S(1)} %add_convert_fusion.1), channel_id=1, source_target_pairs={{0,64},{1,65},{2,66},{3,67},{4,68},{5,69},{6,70},{7,71},{8,72},{9,... | collective-permute-start | bytes 884744 | tf_op jit(solution)/shard_map/ppermute | solution.py:38
  202.9 20.7 %copy-start.21 = (bf16[48,3072]{1,0:T(8,128)(2,1)S(1)}, bf16[48,3072]{1,0:T(8,128)(2,1)}, u32[]{:S(2)}) copy-start(bf16[48,3072]{1,0:T(8,128)(2,1)} %get-tuple-element.53) | copy-start | bytes 884740
  216.3 93.2 %collective-permute-start.22 = (bf16[2,384,768]{2,1,0:T(8,128)(2,1)}, bf16[2,384,768]{2,1,0:T(8,128)(2,1)S(1)}, u32[]{:S(2)}, u32[]{:S(2)}) collective-permute-start(bf16[2,384,768]{2,1,0:T(8,128)(2,1)} %get-tuple-element.48), channel_id=1, source_target_pairs={{1,0},{2,1},{3,2},{4,3},{5,4},{6,5},{7,6},{9,8},{10,9},{11,10},{12... | collective-permute-start | bytes 3538952 | tf_op jit(solution)/shard_map/ppermute | solution.py:74
  217.6 99.0 %collective-permute-start.19 = (bf16[2,384,768]{2,1,0:T(8,128)(2,1)}, bf16[2,384,768]{2,1,0:T(8,128)(2,1)S(1)}, u32[]{:S(2)}, u32[]{:S(2)}) collective-permute-start(bf16[2,384,768]{2,1,0:T(8,128)(2,1)} %get-tuple-element.44), channel_id=1, source_target_pairs={{0,1},{1,2},{2,3},{3,4},{4,5},{5,6},{6,7},{8,9},{9,10},{10,11},{11... | collective-permute-start | bytes 3538952 | tf_op jit(solution)/shard_map/ppermute | solution.py:70
  222.3 94.4 %collective-permute-start.20 = (bf16[2,384,768]{2,1,0:T(8,128)(2,1)}, bf16[2,384,768]{2,1,0:T(8,128)(2,1)}, u32[]{:S(2)}, u32[]{:S(2)}) collective-permute-start(bf16[2,384,768]{2,1,0:T(8,128)(2,1)} %get-tuple-element.45), channel_id=1, source_target_pairs={{1,0},{2,1},{3,2},{4,3},{5,4},{6,5},{7,6},{9,8},{10,9},{11,10},{12... | collective-permute-start | bytes 3538952 | tf_op jit(solution)/shard_map/ppermute | solution.py:74
  225.1 22.4 %collective-permute-start.39 = (bf16[48,768]{1,0:T(8,128)(2,1)S(1)}, bf16[48,768]{1,0:T(8,128)(2,1)}, u32[]{:S(2)}, u32[]{:S(2)}) collective-permute-start(bf16[48,768]{1,0:T(8,128)(2,1)S(1)} %get-tuple-element.75), channel_id=1, source_target_pairs={{0,1},{1,2},{2,3},{3,0},{4,5},{5,6},{6,7},{7,4},{8,9},{9,10},{10,1... | collective-permute-start | bytes 221192 | tf_op jit(solution)/shard_map/ppermute | solution.py:38
  247.5 7.5 %collective-permute-start.41 = (bf16[48,768]{1,0:T(8,128)(2,1)S(1)}, bf16[48,768]{1,0:T(8,128)(2,1)}, u32[]{:S(2)}, u32[]{:S(2)}) collective-permute-start(bf16[48,768]{1,0:T(8,128)(2,1)S(1)} %get-tuple-element.76), channel_id=1, source_target_pairs={{0,2},{1,3},{2,0},{3,1},{4,6},{5,7},{6,4},{7,5},{8,10},{9,11},{10,... | collective-permute-start | bytes 221192 | tf_op jit(solution)/shard_map/ppermute | solution.py:38
  255.0 23.9 %collective-permute-start.40 = (bf16[48,768]{1,0:T(8,128)(2,1)}, bf16[48,768]{1,0:T(8,128)(2,1)}, u32[]{:S(2)}, u32[]{:S(2)}) collective-permute-start(bf16[48,768]{1,0:T(8,128)(2,1)} %get-tuple-element.77), channel_id=1, source_target_pairs={{0,3},{1,0},{2,1},{3,2},{4,7},{5,4},{6,5},{7,6},{8,11},{9,8},{10,9... | collective-permute-start | bytes 221192 | tf_op jit(solution)/shard_map/ppermute | solution.py:38
  280.6 4.7 %collective-permute-start.44 = (bf16[48,768]{1,0:T(8,128)(2,1)}, bf16[48,768]{1,0:T(8,128)(2,1)}, u32[]{:S(2)}, u32[]{:S(2)}) collective-permute-start(bf16[48,768]{1,0:T(8,128)(2,1)} %add_convert_fusion.2), channel_id=1, source_target_pairs={{0,3},{1,0},{2,1},{3,2},{4,7},{5,4},{6,5},{7,6},{8,11},{9,8},{10,9... | collective-permute-start | bytes 221192 | tf_op jit(solution)/shard_map/ppermute | solution.py:38
  285.2 6.2 %collective-permute-start.43 = (bf16[48,768]{1,0:T(8,128)(2,1)}, bf16[48,768]{1,0:T(8,128)(2,1)}, u32[]{:S(2)}, u32[]{:S(2)}) collective-permute-start(bf16[48,768]{1,0:T(8,128)(2,1)} %add_convert_fusion.2), channel_id=1, source_target_pairs={{0,2},{1,3},{2,0},{3,1},{4,6},{5,7},{6,4},{7,5},{8,10},{9,11},{10,... | collective-permute-start | bytes 221192 | tf_op jit(solution)/shard_map/ppermute | solution.py:38
  291.4 6.0 %collective-permute-start.42 = (bf16[48,768]{1,0:T(8,128)(2,1)}, bf16[48,768]{1,0:T(8,128)(2,1)}, u32[]{:S(2)}, u32[]{:S(2)}) collective-permute-start(bf16[48,768]{1,0:T(8,128)(2,1)} %add_convert_fusion.2), channel_id=1, source_target_pairs={{0,1},{1,2},{2,3},{3,0},{4,5},{5,6},{6,7},{7,4},{8,9},{9,10},{10,1... | collective-permute-start | bytes 221192 | tf_op jit(solution)/shard_map/ppermute | solution.py:38
  298.5 11.0 %copy-start.5 = (bf16[4,48,768]{2,1,0:T(8,128)(2,1)}, bf16[4,48,768]{2,1,0:T(8,128)(2,1)S(1)}, u32[]{:S(2)}) copy-start(bf16[4,48,768]{2,1,0:T(8,128)(2,1)S(1)} %pad_maximum_fusion.2.mine_ref) | copy-start | bytes 884740
  298.5 24.9 %collective-permute-start.45 = (bf16[4,48,768]{2,1,0:T(8,128)(2,1)S(1)}, bf16[4,48,768]{2,1,0:T(8,128)(2,1)}, u32[]{:S(2)}, u32[]{:S(2)}) collective-permute-start(bf16[4,48,768]{2,1,0:T(8,128)(2,1)S(1)} %pad_maximum_fusion.2.mine_ref), channel_id=1, source_target_pairs={{0,4},{1,5},{2,6},{3,7},{4,0},{5,1},{6,2},{7,3},{8,12},{9,13},{10,... | collective-permute-start | bytes 884744 | tf_op jit(solution)/shard_map/ppermute | solution.py:38
  (10 other events, 11.7 us)

commit v2 on v1

v2 whole, which is shorter than its diff:
```python
import functools
import math

import jax
import jax.numpy as jnp
from jax import lax
from jax.experimental import pallas as pl
from jax.experimental.pallas import tpu as pltpu
from jax.sharding import PartitionSpec as P

HEAD = 128
SCALE = 1.0 / math.sqrt(HEAD)
LOG2_SCALE = SCALE * math.log2(math.e)
FAR = 1e30
COST = pl.CostEstimate(flops=1000, bytes_accessed=1000, transcendentals=0)
BF = jnp.bfloat16
F32 = jnp.float32
VMEM_LIMIT = 24 * 1024 * 1024

NX, NZ, NC, NL, NY = 2, 4, 2, 2, 4
NS = NL * NY


def moves(change):
    pairs = []
    for a in range(NX):
        for z in range(NZ):
            for c in range(NC):
                for l in range(NL):
                    for y in range(NY):
                        b, w, d, m, v = change(a, z, c, l, y)
                        src = ((a * NZ + z) * NC + c) * NS + l * NY + y
                        dst = ((b * NZ + w) * NC + d) * NS + m * NY + v
                        pairs.append((src, dst))
    return pairs


def move(x, change):
    return lax.ppermute(x, ("dp", "space"), moves(change))


def move_core(x):
    return move(x, lambda a, z, c, l, y: (a, z, 1 - c, l, y))


def move_lo(x):
    return move(x, lambda a, z, c, l, y: (a, z, c, 1 - l, y))


def move_lo_core(x):
    return move(x, lambda a, z, c, l, y: (a, z, 1 - c, 1 - l, y))


def move_hi(x):
    return move(x, lambda a, z, c, l, y: (1 - a, z, c, l, y))


def move_cross(x):
    return move(x, lambda a, z, c, l, y: (1 - a, z, c, 1 - l, y))


def move_cross_core(x):
    return move(x, lambda a, z, c, l, y: (1 - a, z, 1 - c, 1 - l, y))


def move_z(x, k):
    return move(x, lambda a, z, c, l, y: (a, (z + k) % NZ, c, l, y))


def move_y(x, k):
    return move(x, lambda a, z, c, l, y: (a, z, c, l, (y + k) % NY))


def to_next(x):
    return lax.ppermute(x, "space", [(i, i + 1) for i in range(NS - 1)])


def to_previous(x):
    return lax.ppermute(x, "space", [(i + 1, i) for i in range(NS - 1)])


def nt(a, b):
    return lax.dot_general(a, b, (((1,), (1,)), ((), ())), preferred_element_type=F32)


def tn(a, b):
    return lax.dot_general(a, b, (((0,), (0,)), ((), ())), preferred_element_type=F32)


def nn(a, b):
    return lax.dot_general(a, b, (((1,), (0,)), ((), ())), preferred_element_type=F32)


PER_F = 2
PER_B = 2


def windows(live, shift):
    factors = [jnp.where(on, LOG2_SCALE, 0.0) for on in live]
    return factors, [jnp.where(on, shift, FAR) for on in live]


def forward_head(live, cols, q_ref, k_ref, v_ref, left_ref, right_ref):
    q = q_ref[:, cols]
    keys = (left_ref[0, :, cols], k_ref[:, cols], right_ref[0, :, cols])
    values = (left_ref[1, :, cols], v_ref[:, cols], right_ref[1, :, cols])
    scores = [nt(k, q) for k in keys]
    tops = [jnp.max(s, axis=0, keepdims=True) for s in scores]
    top = tops[1]
    for j in (0, 2):
        top = jnp.maximum(top, jnp.where(live[j // 2], tops[j], -FAR))
    top = top * LOG2_SCALE
    total = jnp.zeros_like(top)
    acc = jnp.zeros((HEAD, q.shape[0]), F32)
    for j in range(3):
        factor = LOG2_SCALE if j == 1 else jnp.where(live[j // 2], LOG2_SCALE, 0.0)
        shift = top if j == 1 else jnp.where(live[j // 2], top, FAR)
        p = jnp.exp2(scores[j] * factor - shift)
        total = total + jnp.sum(p, axis=0, keepdims=True)
        acc = acc + tn(values[j], p.astype(BF))
    return (acc / total).astype(BF), top + jnp.log2(total)


def forward_kernel(per, info, q_ref, k_ref, v_ref, left_ref, right_ref, *rest):
    attn_ref, total_ref = rest[-2:]
    live = (info[1] > 0, info[2] > 0)
    for i in range(per):
        cols = slice(i * HEAD, (i + 1) * HEAD)
        attn_ref[cols, :], total_ref[i] = forward_head(
            live, cols, q_ref, k_ref, v_ref, left_ref, right_ref
        )


def attend(info, q, k, v, left, right, heads, before=()):
    rows = q.shape[0]
    per = PER_F
    own = pl.BlockSpec((rows, per * HEAD), lambda h, info: (0, info[0] // per + h))
    side = pl.BlockSpec((2, rows, per * HEAD), lambda h, info: (0, 0, h))
    return pl.pallas_call(
        functools.partial(forward_kernel, per),
        out_shape=(
            jax.ShapeDtypeStruct((heads * HEAD, rows), BF),
            jax.ShapeDtypeStruct((heads, 1, rows), F32),
        ),
        grid_spec=pltpu.PrefetchScalarGridSpec(
            num_scalar_prefetch=1,
            grid=(heads // per,),
            in_specs=[own, own, own, side, side] + [pl.BlockSpec(memory_space=pl.ANY)] * len(before),
            out_specs=(
                pl.BlockSpec((per * HEAD, rows), lambda h, info: (h, 0)),
                pl.BlockSpec((per, 1, rows), lambda h, info: (h, 0, 0)),
            ),
        ),
        compiler_params=pltpu.CompilerParams(vmem_limit_bytes=VMEM_LIMIT),
        cost_estimate=COST,
        name="attend",
    )(info, q, k, v, left, right, *before)


def backward_kernel(per, info, q_ref, k_ref, v_ref, left_ref, right_ref, grad_ref, attn_ref, total_ref, *rest):
    dq_ref, own_ref, to_left_ref, to_right_ref = rest[-4:]
    outs = (to_left_ref, own_ref, to_right_ref)
    live = (info[1] > 0, info[2] > 0)
    for i in range(per):
        cols = slice(i * HEAD, (i + 1) * HEAD)
        q = q_ref[:, cols]
        g = grad_ref[cols, :]
        total = total_ref[i]
        delta = jnp.sum(g.astype(F32) * attn_ref[cols, :].astype(F32), axis=0, keepdims=True)
        keys = (left_ref[0, :, cols], k_ref[:, cols], right_ref[0, :, cols])
        values = (left_ref[1, :, cols], v_ref[:, cols], right_ref[1, :, cols])
        dq = jnp.zeros((HEAD, q.shape[0]), F32)
        for j in range(3):
            k, v = keys[j], values[j]
            factor = LOG2_SCALE if j == 1 else jnp.where(live[j // 2], LOG2_SCALE, 0.0)
            shift = total if j == 1 else jnp.where(live[j // 2], total, FAR)
            w = jnp.exp2(nt(k, q) * factor - shift)
            outs[j][1, :, cols] = nt(w.astype(BF), g).astype(BF)
            ds = (w * (nn(v, g) - delta)).astype(BF)
            outs[j][0, :, cols] = (nn(ds, q) * SCALE).astype(BF)
            dq = dq + tn(k, ds)
        dq_ref[:, cols] = (dq * SCALE).T.astype(BF)


def attend_back(info, q, k, v, left, right, grad, attn, total, heads, before, again):
    rows, cols = q.shape
    per = PER_B
    own = pl.BlockSpec((rows, per * HEAD), lambda h, info: (0, info[0] // per + h))
    side = pl.BlockSpec((2, rows, per * HEAD), lambda h, info: (0, 0, h))
    turned = pl.BlockSpec((per * HEAD, rows), lambda h, info: (h, 0))
    return pl.pallas_call(
        functools.partial(backward_kernel, per),
        out_shape=(jax.ShapeDtypeStruct((rows, cols), BF),)
        + (jax.ShapeDtypeStruct((2, rows, heads * HEAD), BF),) * 3,
        grid_spec=pltpu.PrefetchScalarGridSpec(
            num_scalar_prefetch=1,
            grid=(heads // per,),
            in_specs=[own, own, own, side, side, turned, turned,
                      pl.BlockSpec((per, 1, rows), lambda h, info: (h, 0, 0))]
            + [pl.BlockSpec(memory_space=pl.ANY)] * len(before),
            out_specs=(own, side, side, side),
        ),
        input_output_aliases={9: 0} if again else {},
        compiler_params=pltpu.CompilerParams(vmem_limit_bytes=VMEM_LIMIT),
        cost_estimate=COST,
        name="attend_back",
    )(info, q, k, v, left, right, grad, attn, total, *before)


JOIN_ROWS = 192


def join_kernel(first, info, own_ref, a_ref, b_ref, *rest):
    dk_ref, dv_ref = rest if first else rest[2:]
    for i, out in enumerate((dk_ref, dv_ref)):
        out[...] = (own_ref[i].astype(F32) + a_ref[i].astype(F32) + b_ref[i].astype(F32)).astype(BF)


def join(info, own, a, b, heads, cols, before):
    rows = own.shape[1]
    wide = heads * HEAD
    side = pl.BlockSpec((2, JOIN_ROWS, wide), lambda r, info: (0, r, 0))
    out = pl.BlockSpec((JOIN_ROWS, wide), lambda r, info: (r, info[0] // heads))
    first = before is None
    return pl.pallas_call(
        functools.partial(join_kernel, first),
        out_shape=(jax.ShapeDtypeStruct((rows, cols), BF),) * 2,
        grid_spec=pltpu.PrefetchScalarGridSpec(
            num_scalar_prefetch=1,
            grid=(rows // JOIN_ROWS,),
            in_specs=[side] * 3 + ([] if first else [pl.BlockSpec(memory_space=pl.ANY)] * 2),
            out_specs=(out, out),
        ),
        input_output_aliases={} if first else {4: 0, 5: 1},
        compiler_params=pltpu.CompilerParams(vmem_limit_bytes=VMEM_LIMIT),
        cost_estimate=COST,
        name="join",
    )(info, own, a, b, *(() if first else before))


def hold_kernel(x_ref, *rest):
    del x_ref, rest


def hold(x, *before):
    anywhere = pl.BlockSpec(memory_space=pl.ANY)
    return pl.pallas_call(
        hold_kernel,
        out_shape=jax.ShapeDtypeStruct(x.shape, x.dtype),
        in_specs=[anywhere] * (1 + len(before)),
        out_specs=anywhere,
        input_output_aliases={0: 0},
        cost_estimate=COST,
        name="hold",
    )(x, *before)


def window_kernel(info, k_ref, v_ref, *rest):
    rest[-1][0] = k_ref[...]
    rest[-1][1] = v_ref[...]


def window(info, k, v, heads, before=()):
    rows = k.shape[0]
    wide = heads * HEAD
    block = pl.BlockSpec((rows // 2, wide), lambda r, info: (r, info[0] // heads))
    return pl.pallas_call(
        window_kernel,
        out_shape=jax.ShapeDtypeStruct((2, rows, wide), BF),
        grid_spec=pltpu.PrefetchScalarGridSpec(
            num_scalar_prefetch=1,
            grid=(2,),
            in_specs=[block, block] + [pl.BlockSpec(memory_space=pl.ANY)] * len(before),
            out_specs=pl.BlockSpec((2, rows // 2, wide), lambda r, info: (0, r, 0)),
        ),
        compiler_params=pltpu.CompilerParams(vmem_limit_bytes=VMEM_LIMIT),
        cost_estimate=COST,
        name="window",
    )(info, k, v, *before)


def project_back_kernel(place, *refs):
    pieces, (u_ref, other_ref) = refs[:NZ], refs[NZ:NZ + 2]
    mine_ref, theirs_ref, w = refs[-3:]
    rows = pieces[0].shape[0]
    for i, piece in enumerate(pieces):
        w[pl.ds(pl.multiple_of(place[i] * rows, rows), rows), :] = piece[...]
    mine_ref[...] = nt(w[...], u_ref[...]).astype(BF)
    theirs_ref[...] = nt(w[...], other_ref[...]).astype(BF)


def project_back(place, pieces, u, other, before=()):
    rows, wide = pieces[0].shape
    tokens = u.shape[0]
    whole = pl.BlockSpec(memory_space=pltpu.VMEM)
    return pl.pallas_call(
        project_back_kernel,
        out_shape=(jax.ShapeDtypeStruct((NZ * rows, tokens), BF),) * 2,
        in_specs=[pl.BlockSpec(memory_space=pltpu.SMEM)] + [whole] * (NZ + 2)
        + [pl.BlockSpec(memory_space=pl.ANY)] * len(before),
        out_specs=(whole, whole),
        scratch_shapes=[pltpu.VMEM((NZ * rows, wide), BF)],
        compiler_params=pltpu.CompilerParams(vmem_limit_bytes=VMEM_LIMIT),
        cost_estimate=COST,
        name="project_back",
    )(place, *pieces, u, other, *before)


SPLIT = 2


def project_kernel(adds, place, a_ref, b_ref, *refs):
    pieces, sent = refs[:2 * NZ], refs[2 * NZ:2 * NZ + adds]
    outs, w = refs[-1 - (1 if adds else SPLIT):-1], refs[-1]
    rows = pieces[0].shape[0]
    half = NZ * rows
    for i, piece in enumerate(pieces):
        spot = (i // NZ) * half + place[i % NZ] * rows
        w[pl.ds(pl.multiple_of(spot, rows), rows), :] = piece[...]
    block = w.shape[1] // SPLIT
    first, second = a_ref[...].T, b_ref[...].T
    for i in range(SPLIT):
        cols = slice(i * block, (i + 1) * block)
        total = nn(first, w[:half, cols]) + nn(second, w[half:, cols])
        if adds:
            outs[0][:, cols] = (total + sent[i][...].astype(F32)).astype(BF)
        else:
            outs[i][...] = total.astype(BF)


def project(place, a, b, pieces, sent, before=()):
    tokens = a.shape[1]
    rows, wide = pieces[0].shape
    whole = pl.BlockSpec(memory_space=pltpu.VMEM)
    if sent:
        out_shape = (jax.ShapeDtypeStruct((tokens, wide), BF),)
    else:
        out_shape = (jax.ShapeDtypeStruct((tokens, wide // SPLIT), BF),) * SPLIT
    return pl.pallas_call(
        functools.partial(project_kernel, len(sent)),
        out_shape=out_shape,
        in_specs=[pl.BlockSpec(memory_space=pltpu.SMEM)] + [whole] * (2 + 2 * NZ + len(sent))
        + [pl.BlockSpec(memory_space=pl.ANY)] * len(before),
        out_specs=(whole,) * len(out_shape),
        scratch_shapes=[pltpu.VMEM((2 * NZ * rows, wide), BF)],
        compiler_params=pltpu.CompilerParams(vmem_limit_bytes=32 * 1024 * 1024),
        cost_estimate=COST,
        name="project",
    )(place, a, b, *pieces, *sent, *before)


def weight_grad_kernel(place, *refs):
    a_refs, u_refs, half_refs = refs[:4], refs[4:6], refs[6:10]
    out_refs, total = refs[-1 - NZ:-1], refs[-1]
    near = sum(nn(a[...], u[...]) for a, u in zip(a_refs, u_refs))
    for i in range(2):

        @pl.when(pl.program_id(0) == i)
        def _():
            far = sum(nn(a[...], u[...]) for a, u in zip(a_refs[2:], half_refs[2 * i:]))
            total[...] = (near + far).astype(BF)

    rows = out_refs[0].shape[0]
    for i, out in enumerate(out_refs):
        out[...] = total[pl.ds(pl.multiple_of(place[i] * rows, rows), rows), :]


def weight_grad(place, a_list, u, core, first, second, before):
    rows, tokens = a_list[0].shape
    wide = u.shape[1]
    block = wide // 2
    sub = rows // NZ
    return pl.pallas_call(
        weight_grad_kernel,
        out_shape=(jax.ShapeDtypeStruct((sub, wide), BF),) * NZ,
        grid_spec=pltpu.PrefetchScalarGridSpec(
            num_scalar_prefetch=1,
            grid=(wide // block,),
            in_specs=[pl.BlockSpec((rows, tokens), lambda i, p: (0, 0))] * 4
            + [pl.BlockSpec((tokens, block), lambda i, p: (0, i))] * 2
            + [pl.BlockSpec((tokens, block), lambda i, p: (0, 0))] * 4
            + [pl.BlockSpec(memory_space=pl.ANY)] * len(before),
            out_specs=(pl.BlockSpec((sub, block), lambda i, p: (0, i)),) * NZ,
            scratch_shapes=[pltpu.VMEM((rows, block), BF)],
        ),
        compiler_params=pltpu.CompilerParams(vmem_limit_bytes=32 * 1024 * 1024),
        cost_estimate=COST,
        name="weight_grad",
    )(place, *a_list, u, core, *first, *second, *before)


def place_kernel(spots, *refs):
    out_ref = refs[-1]
    wide = refs[0].shape[1]
    for j, ref in enumerate(refs[:-1]):
        out_ref[:, pl.ds(pl.multiple_of(spots[j] * wide, wide), wide)] = ref[...].astype(F32)


def place_columns(spots, *pieces):
    rows, cols = pieces[0].shape
    whole = pl.BlockSpec(memory_space=pltpu.VMEM)
    return pl.pallas_call(
        place_kernel,
        out_shape=jax.ShapeDtypeStruct((rows, len(pieces) * cols), F32),
        in_specs=[pl.BlockSpec(memory_space=pltpu.SMEM)] + [whole] * len(pieces),
        out_specs=whole,
        cost_estimate=COST,
        name="place_columns",
    )(spots, *pieces)


def add(*terms):
    return functools.reduce(lambda s, t: s + t.astype(F32), terms[1:], terms[0].astype(F32))


def on_device(query, key_in, value_in, out_weight, grad_out, neighbours):
    q, k, v, upstream = query[0], key_in[0], value_in[0], grad_out[0]
    rows, cols = q.shape
    half = cols // 2
    heads = half // HEAD
    dp = lax.axis_index("dp")
    tile = lax.axis_index("space")
    a, z, c = dp // (NZ * NC), (dp // NC) % NZ, dp % NC
    lo, y = tile // NY, tile % NY

    own_list = neighbours[tile]
    live_left = jnp.any((own_list == tile - 1) & (own_list >= 0)).astype(jnp.int32)
    live_right = jnp.any(own_list == tile + 1).astype(jnp.int32)
    infos = [
        jnp.stack([part * heads, live_left, live_right]).astype(jnp.int32) for part in (a, 1 - a)
    ]

    sides = [jnp.full((1,), part * heads, jnp.int32) for part in (a, 1 - a)]
    pair = window(sides[0], k, v, heads)
    near0 = (to_next(pair), to_previous(pair))
    pair = window(sides[1], k, v, heads, near0)
    near1 = (to_next(pair), to_previous(pair))

    def around(x):
        up, down = move_z(x, 1), move_z(x, 3)
        return [x, up, down, move_z(up, 1)]

    cross = move_cross(out_weight)
    w0 = around(out_weight)
    place = jnp.stack([z, (z + 3) % NZ, (z + 1) % NZ, (z + 2) % NZ]).astype(jnp.int32)

    middle = upstream.shape[1] // 2
    up_core = move_core(upstream)
    cross_first = move_cross(hold(upstream[:, :middle], cross))
    cross_second = move_cross(hold(upstream[:, middle:], cross_first))

    def back(w, before):
        mine, theirs = project_back(place, w, upstream, up_core, before)
        both = (mine.reshape(NZ, -1, rows), move_core(theirs).reshape(NZ, -1, rows))
        both = jnp.where(c == 0, jnp.stack(both, axis=1), jnp.stack(both[::-1], axis=1))
        return both.reshape(half, rows)

    attn0, total0 = attend(infos[0], q, k, v, *near0, heads)
    w1 = around(hold(cross, attn0))
    grad0 = back(w0, (attn0,))
    attn1, total1 = attend(infos[1], q, k, v, *near1, heads, (grad0,))
    dq, own0, to_left, to_right = attend_back(
        infos[0], q, k, v, *near0, grad0, attn0, total0, heads, (attn1,), False
    )
    sent0 = (to_next(to_right), to_previous(to_left))

    def pick(attn, core):
        parts = attn.reshape(NZ, NC, -1, rows)
        sub = parts.shape[2]
        return lax.dynamic_slice(parts, (0, core, 0, 0), (NZ, 1, sub, rows)).reshape(
            NZ * sub, rows
        )

    own_part, core_part = pick(attn1, c), pick(attn1, 1 - c)
    a_list = [
        pick(attn0, c),
        move_core(pick(attn0, 1 - c)),
        move_cross(own_part),
        move_cross_core(core_part),
    ]
    grad1 = back(w1, (own0,))
    core_far = move_core(core_part)
    dq, own1, to_left, to_right = attend_back(
        infos[1], q, k, v, *near1, grad1, attn1, total1, heads, (dq, core_far), True
    )
    sent1 = (to_next(to_right), to_previous(to_left))
    z_place = jnp.stack([(z + i) % NZ for i in range(NZ)]).astype(jnp.int32)
    pieces = weight_grad(
        z_place, a_list, upstream, up_core, (cross_first, move_core(cross_first)),
        (cross_second, move_core(cross_second)), (own1,) + sent0,
    )
    theirs = project(place, a_list[1], core_far, w0 + w1, (), pieces[:1])
    sent = tuple(move_core(t) for t in theirs)
    (mixed,) = project(place, a_list[0], own_part, w0 + w1, sent)
    done = join(infos[0], own0, *sent0, heads, cols, None)
    done = join(infos[1], own1, *sent1, heads, cols, done)

    sums = add(hold(pieces[0], *done), *[move_z(pieces[i], i) for i in (1, 3, 2)])
    quarter = sums.shape[1] // NY

    def column(i):
        return lax.dynamic_slice_in_dim(sums, ((y + i) % NY) * quarter, quarter, axis=1)

    mine = add(column(0), *[move_y(column(i).astype(BF), i) for i in (1, 3, 2)]).astype(BF)
    mine = hold(mine, mixed)
    mine = add(mine, move_lo(mine)).astype(BF)
    spots = jnp.stack([(y - i) % NY for i in (0, 1, 3, 2)]).astype(jnp.int32)
    grad_weight = place_columns(spots, mine, *[move_y(mine, i) for i in (1, 3, 2)])
    dk, dv = done
    return (mixed[None], dq[None], dk[None], dv[None], grad_weight)


def solution(mesh):
    return jax.shard_map(
        on_device,
        mesh=mesh,
        in_specs=(
            P("dp", "space", None),
            P("dp", "space", None),
            P("dp", "space", None),
            P("dp", None),
            P("dp", "space", None),
            P(),
        ),
        out_specs=(
            P("dp", "space", None),
            P("dp", "space", None),
            P("dp", "space", None),
            P("dp", "space", None),
            P("dp", None),
        ),
        check_vma=False,
    )
```

time: 327 us -> 245 us (0.75)
  starting transfers between devices: 94.1 us -> 49.9 us
  waiting for transfers between devices: 107 us -> 74.2 us
  Pallas kernels: 105 us -> 85.8 us
  local copies, waits for them, and re-layouts: 10.4 us -> 22.8 us
    ppermute x38 -> x30, starting transfers between devices: 72.9 us -> 30.8 us  [move(): return lax.ppermute(x, ('dp', 'space'), moves(change))]
    ppermute x4, waiting for transfers between devices: 34.6 us -> 2.76 us  [to_next(): return lax.ppermute(x, 'space', [(i, i + 1) for i in range(NS - 1)])]
    pallas_call x10 -> x17, Pallas kernels: 93.2 us -> 79.7 us  [the longest x2 25.1 us: attend_back(): pl.pallas_call(functools.partial(backward_kernel, per), out_shape=(jax.Sh...]
    unnamed x56 -> x90, local copies, waits for them, and re-layouts: 4.14 us -> 16.8 us
    ppermute x38 -> x30, waiting for transfers between devices: 70.3 us -> 62.5 us  [move(): return lax.ppermute(x, ('dp', 'space'), moves(change))]
    ppermute x4, waiting for transfers between devices: 2.15 us -> 8.97 us  [to_previous(): return lax.ppermute(x, 'space', [(i + 1, i) for i in range(NS - 1)])]
    pallas_call x2, Pallas kernels: 11.6 us -> 6.1 us  [join(): pl.pallas_call(functools.partial(join_kernel, first), out_shape=(jax.Shap...]
  transfers between devices with their start and end apart: 46 -> 38, of which waited for: 12 -> 18; matrix products, arithmetic and copies ran while one was open for 4% -> 5% of each run, Pallas kernels for 32% -> 31%
where the time goes in v2:
time: 245 us; the launch traced here: 243 us
  Pallas kernels  85.8 us (35%)
  waiting for transfers between devices  74.2 us (30%)
  starting transfers between devices  49.9 us (20%)
  local copies, waits for them, and re-layouts  22.8 us (9%)
  other arithmetic  8.08 us (3%)
    ppermute x30, waiting for transfers between devices, move(): return lax.ppermute(x, ('dp', 'space'), moves(change))  62.5 us
    ppermute x30, starting transfers between devices, move(): return lax.ppermute(x, ('dp', 'space'), moves(change))  30.8 us
    pallas_call x2, Pallas kernels, attend_back(): pl.pallas_call(functools.partial(backward_kernel, per), out_shape=(jax.Sh...  25.1 us
    unnamed x90, local copies, waits for them, and re-layouts  16.8 us
    pallas_call x2, Pallas kernels, attend(): pl.pallas_call(functools.partial(forward_kernel, per), out_shape=(jax.Sha...  14.7 us
    ppermute x4, starting transfers between devices, to_next(): return lax.ppermute(x, 'space', [(i, i + 1) for i in range(NS - 1)])  13.7 us
    pallas_call x2, Pallas kernels, project_back(): pl.pallas_call(project_back_kernel, out_shape=(jax.ShapeDtypeStruct((NZ *...  12.6 us
    pallas_call x2, Pallas kernels, project(): pl.pallas_call(functools.partial(project_kernel, len(sent)), out_shape=ou...  12.6 us
  transfers between devices with their start and end apart: 38, of which 18 were waited for; matrix products, arithmetic and copies ran while one was open for 5% of the time, Pallas kernels for 31%

profile of v2, /device:TPU:0, one launch (start us, length us, event | category | flops | bytes accessed | tf_op | source)
XLA Modules:
  0.0 243.1 jit_solution(12113060027578315696)
XLA Ops:
  0.7 1.3 copy-done
  1.9 1.3 copy-done.2
  3.2 1.2 window.2
  4.4 4.6 %collective-permute-start = (bf16[2,384,768]{2,1,0:T(8,128)(2,1)}, bf16[2,384,768]{2,1,0:T(8,128)(2,1)}, u32[]{:S(2)}, u32[]{:S(2)}) collective-permute-start(bf16[2,384,768]{2,1,0:T(8,128)(2,1)} %window.2), channel_id=1, source_target_pairs={{0,1},{1,2},{2,3},{3,4},{4,5},{5,6},{6,7},{8,9},{9,10},{10,11},{11... | collective-permute-start | bytes 3538952 | tf_op jit(solution)/shard_map/ppermute | solution.py:75
  9.0 1.9 collective-permute-start.9
  10.9 1.3 collective-permute-start.1
  12.2 3.2 %fusion = (bf16[384,1536]{1,0:T(8,128)(2,1)}, bf16[384,1536]{1,0:T(8,128)(2,1)}) fusion(bf16[384,3072]{1,0:T(8,128)(2,1)} %bitcast.13.refs_4_), kind=kLoop, calls=%fused_computation.20 | loop fusion | bytes 4718592 | tf_op jit(solution)/shard_map/slice | solution.py:450
  15.4 10.8 %collective-permute-done.9.x_ref.rest_0_ = bf16[96,3072]{1,0:T(8,128)(2,1)S(1)} collective-permute-done((bf16[96,3072]{1,0:T(8,128)(2,1)}, bf16[96,3072]{1,0:T(8,128)(2,1)S(1)}, u32[]{:S(2)}, u32[]{:S(2)}) %collective-permute-start.9) | collective-permute-done | bytes 589856 | tf_op jit(solution)/shard_map/ppermute | solution.py:39
  27.0 1.8 collective-permute-start.17
  28.8 1.9 collective-permute-start.4
  30.7 2.8 %collective-permute-done.left_ref.rest_0_ = bf16[2,384,768]{2,1,0:T(8,128)(2,1)} collective-permute-done((bf16[2,384,768]{2,1,0:T(8,128)(2,1)}, bf16[2,384,768]{2,1,0:T(8,128)(2,1)}, u32[]{:S(2)}, u32[]{:S(2)}) %collective-permute-start) | collective-permute-done | bytes 1179680 | tf_op jit(solution)/shard_map/ppermute | solution.py:75
  33.5 4.0 %collective-permute-start.5 = (bf16[96,3072]{1,0:T(8,128)(2,1)}, bf16[96,3072]{1,0:T(8,128)(2,1)}, u32[]{:S(2)}, u32[]{:S(2)}) collective-permute-start(bf16[96,3072]{1,0:T(8,128)(2,1)} %refs_0_.5), channel_id=1, source_target_pairs={{0,48},{1,49},{2,50},{3,51},{4,52},{5,53},{6,54},{7,55},{8,56},{9,... | collective-permute-start | bytes 1769480 | tf_op jit(solution)/shard_map/ppermute | solution.py:39
  37.5 3.6 %collective-permute-done.1.right_ref.rest_1_ = bf16[2,384,768]{2,1,0:T(8,128)(2,1)} collective-permute-done((bf16[2,384,768]{2,1,0:T(8,128)(2,1)}, bf16[2,384,768]{2,1,0:T(8,128)(2,1)}, u32[]{:S(2)}, u32[]{:S(2)}) %collective-permute-start.1) | collective-permute-done | bytes 1179680 | tf_op jit(solution)/shard_map/ppermute | solution.py:79
  41.1 1.2 window.3
  42.4 4.5 %collective-permute-start.2 = (bf16[2,384,768]{2,1,0:T(8,128)(2,1)}, bf16[2,384,768]{2,1,0:T(8,128)(2,1)}, u32[]{:S(2)}, u32[]{:S(2)}) collective-permute-start(bf16[2,384,768]{2,1,0:T(8,128)(2,1)} %window.3), channel_id=1, source_target_pairs={{0,1},{1,2},{2,3},{3,4},{4,5},{5,6},{6,7},{8,9},{9,10},{10,11},{11... | collective-permute-start | bytes 3538952 | tf_op jit(solution)/shard_map/ppermute | solution.py:75
  48.9 2.0 collective-permute-start.6
  51.5 7.3 %attend.2 = (bf16[768,384]{1,0:T(8,128)(2,1)S(1)}, f32[6,1,384]{2,1,0:T(1,128)S(1)}) custom-call(s32[3]{0:T(128)S(1)} %get-tuple-element.68.info, bf16[384,1536]{1,0:T(8,128)(2,1)S(1)} %bitcast.61, bf16[384,1536]{1,0:T(8,128)(2,1)S(1)} %bitcast.51, bf16[384,1536]{1,0:T(8,128)(2,1)S(1)} %bitcast.57, ...), custom_call_target="tpu_custom_call" | custom-call | flops 1000 | bytes 1000 | tf_op jit(solution)/shard_map/attend/pallas_call | solution.py:139
  59.7 1.9 collective-permute-start.10
  61.6 1.3 collective-permute-start.3
  62.9 4.7 %collective-permute-done.6.refs_3_ = bf16[96,3072]{1,0:T(8,128)(2,1)} collective-permute-done((bf16[96,3072]{1,0:T(8,128)(2,1)}, bf16[96,3072]{1,0:T(8,128)(2,1)}, u32[]{:S(2)}, u32[]{:S(2)}) %collective-permute-start.6) | collective-permute-done | bytes 589856 | tf_op jit(solution)/shard_map/ppermute | solution.py:39
  67.6 10.9 %collective-permute-done.10.refs_1_.refs_5_ = bf16[96,3072]{1,0:T(8,128)(2,1)} collective-permute-done((bf16[96,3072]{1,0:T(8,128)(2,1)}, bf16[96,3072]{1,0:T(8,128)(2,1)}, u32[]{:S(2)}, u32[]{:S(2)}) %collective-permute-start.10) | collective-permute-done | bytes 589856 | tf_op jit(solution)/shard_map/ppermute | solution.py:39
  78.5 1.7 collective-permute-start.11
  80.6 1.1 copy-done.9
  81.7 6.6 %project_back.2 = (bf16[384,384]{1,0:T(8,128)(2,1)S(1)}, bf16[384,384]{1,0:T(8,128)(2,1)}) custom-call(s32[4]{0:T(128)S(1)} %pad_add_fusion.place, bf16[96,3072]{1,0:T(8,128)(2,1)} %refs_0_.5, bf16[96,3072]{1,0:T(8,128)(2,1)} %collective-permute-done.4.refs_1_, bf16[96,3072]{1,0:T(8,128)(2,1)} %collective-permute-done.5.refs_2_, ...), custom_call_target="tpu_custom_call" | custom-call | flops 1000 | bytes 1000 | tf_op jit(solution)/shard_map/project_back/pallas_call | solution.py:296
  89.0 1.9 collective-permute-done.8
  91.0 1.8 constant_dynamic-slice_fusion.1
  92.9 1.1 maximum_select_fusion
  94.7 7.3 %attend.3 = (bf16[768,384]{1,0:T(8,128)(2,1)S(1)}, f32[6,1,384]{2,1,0:T(1,128)S(1)}) custom-call(s32[3]{0:T(128)S(1)} %copy-done.34, bf16[384,1536]{1,0:T(8,128)(2,1)S(1)} %bitcast.62, bf16[384,1536]{1,0:T(8,128)(2,1)S(1)} %bitcast.52, bf16[384,1536]{1,0:T(8,128)(2,1)S(1)} %bitcast.58, bf16[2,384,768]{2,1,0:T(8,128)(2,1)} %collective-permute-done.2.left_ref, ...), custom_call_target="tpu_custom_call" | custom-call | flops 1000 | bytes 1000 | tf_op jit(solution)/shard_map/attend/pallas_call | solution.py:139
  102.1 12.5 %attend_back.2 = (bf16[384,1536]{1,0:T(8,128)(2,1)}, bf16[2,384,768]{2,1,0:T(8,128)(2,1)S(1)}, bf16[2,384,768]{2,1,0:T(8,128)(2,1)}, bf16[2,384,768]{2,1,0:T(8,128)(2,1)}) custom-call(s32[3]{0:T(128)S(1)} %copy-done.37, bf16[384,1536]{1,0:T(8,128)(2,1)S(1)} %bitcast.63, bf16[384,1536]{1,0:T(8,128)(2,1)S(1)} %bitcast.53, bf16[384,1536]{1,0:T(8,128)(2,1)S(1)} %bitcast.59, ...), custom_call_target="tpu_custom_call" | custom-call | flops 1000 | bytes 1000 | tf_op jit(solution)/shard_map/attend_back/pallas_call | solution.py:191
  114.6 6.1 %project_back.3 = (bf16[384,384]{1,0:T(8,128)(2,1)S(1)}, bf16[384,384]{1,0:T(8,128)(2,1)S(1)}) custom-call(s32[4]{0:T(128)S(1)} %pad_add_fusion.place, bf16[96,3072]{1,0:T(8,128)(2,1)S(1)} %copy-done.6, bf16[96,3072]{1,0:T(8,128)(2,1)} %collective-permute-done.10.refs_1_.refs_5_, bf16[96,3072]{1,0:T(8,128)(2,1)} %collective-permute-done.11.refs_2_.refs_6_, ...), custom_call_target="tpu_custom_call" | custom-call | flops 1000 | bytes 1000 | tf_op jit(solution)/shard_map/project_back/pallas_call | solution.py:296
  122.3 3.3 %collective-permute-start.22 = (bf16[2,384,768]{2,1,0:T(8,128)(2,1)}, bf16[2,384,768]{2,1,0:T(8,128)(2,1)}, u32[]{:S(2)}, u32[]{:S(2)}) collective-permute-start(bf16[2,384,768]{2,1,0:T(8,128)(2,1)} %get-tuple-element.42), channel_id=1, source_target_pairs={{0,1},{1,2},{2,3},{3,4},{4,5},{5,6},{6,7},{8,9},{9,10},{10,11},{11... | collective-permute-start | bytes 3538952 | tf_op jit(solution)/shard_map/ppermute | solution.py:75
  125.6 1.3 collective-permute-start.23
  127.0 4.7 %collective-permute-done.15.refs_2_ = bf16[384,384]{1,0:T(8,128)(2,1)S(1)} collective-permute-done((bf16[384,384]{1,0:T(8,128)(2,1)S(1)}, bf16[384,384]{1,0:T(8,128)(2,1)S(1)}, u32[]{:S(2)}, u32[]{:S(2)}) %collective-permute-start.15) | collective-permute-done | bytes 294944 | tf_op jit(solution)/shard_map/ppermute | solution.py:39
  131.7 1.2 collective-permute-start.16
  133.0 12.6 %attend_back.3 = (bf16[384,1536]{1,0:T(8,128)(2,1)}, bf16[2,384,768]{2,1,0:T(8,128)(2,1)S(1)}, bf16[2,384,768]{2,1,0:T(8,128)(2,1)}, bf16[2,384,768]{2,1,0:T(8,128)(2,1)}) custom-call(s32[3]{0:T(128)S(1)} %copy-done.34, bf16[384,1536]{1,0:T(8,128)(2,1)S(1)} %bitcast.64, bf16[384,1536]{1,0:T(8,128)(2,1)S(1)} %bitcast.54, ...), custom_call_target="tpu_custom_call", output_to_operand_aliasing={{0}: (9, {})} | custom-call | flops 1000 | bytes 1000 | tf_op jit(solution)/shard_map/attend_back/pallas_call | solution.py:191
  145.6 1.0 copy-done.14
  147.4 1.4 collective-permute-start.26
  148.8 1.0 copy-done.26
  149.8 1.5 collective-permute-start.27
  151.4 5.0 %collective-permute-done.23.refs_12_.b_ref = bf16[2,384,768]{2,1,0:T(8,128)(2,1)} collective-permute-done((bf16[2,384,768]{2,1,0:T(8,128)(2,1)}, bf16[2,384,768]{2,1,0:T(8,128)(2,1)}, u32[]{:S(2)}, u32[]{:S(2)}) %collective-permute-start.23) | collective-permute-done | bytes 1179680 | tf_op jit(solution)/shard_map/ppermute | solution.py:79
  156.4 1.3 copy-done.15
  158.6 1.0 copy-done.20
  159.6 1.3 copy-done.27
  162.8 10.0 %weight_grad.1 = (bf16[96,3072]{1,0:T(8,128)(2,1)S(1)}, bf16[96,3072]{1,0:T(8,128)(2,1)}, bf16[96,3072]{1,0:T(8,128)(2,1)}, bf16[96,3072]{1,0:T(8,128)(2,1)}) custom-call(s32[4]{0:T(128)S(1)} %pad_add_fusion.1.place, bf16[384,384]{1,0:T(8,128)(2,1)S(1)} %bitcast.69, bf16[384,384]{1,0:T(8,128)(2,1)S(1)} %copy-done.20, bf16[384,384]{1,0:T(8,128)(2,1)S(1)} %copy-done.29, ...), custom_call_target="tpu_custom_call" | custom-call | flops 1000 | bytes 1000 | tf_op jit(solution)/shard_map/weight_grad/pallas_call | solution.py:373
  172.8 3.2 %collective-permute-start.29 = (bf16[96,3072]{1,0:T(8,128)(2,1)}, bf16[96,3072]{1,0:T(8,128)(2,1)}, u32[]{:S(2)}, u32[]{:S(2)}) collective-permute-start(bf16[96,3072]{1,0:T(8,128)(2,1)} %get-tuple-element.55), channel_id=1, source_target_pairs={{0,48},{1,49},{2,50},{3,51},{4,52},{5,53},{6,54},{7,55},{8,56},{9,... | collective-permute-start | bytes 1769480 | tf_op jit(solution)/shard_map/ppermute | solution.py:39
  176.1 1.2 collective-permute-start.30
  177.3 3.2 %join.2 = (bf16[384,1536]{1,0:T(8,128)(2,1)}, bf16[384,1536]{1,0:T(8,128)(2,1)}) custom-call(s32[3]{0:T(128)S(1)} %copy-done.38, bf16[2,384,768]{2,1,0:T(8,128)(2,1)S(1)} %copy-done.13, bf16[2,384,768]{2,1,0:T(8,128)(2,1)} %collective-permute-done.22.refs_11_.a_ref, bf16[2,384,768]{2,1,0:T(8,128)(2,1)} %collective-permute-done.23.refs_12_.b_ref), custom_call_target="tpu_custom_call" | custom-call | flops 1000 | bytes 1000 | tf_op jit(solution)/shard_map/join/pallas_call | solution.py:225
  180.8 2.9 %join.3 = (bf16[384,1536]{1,0:T(8,128)(2,1)}, bf16[384,1536]{1,0:T(8,128)(2,1)}) custom-call(s32[3]{0:T(128)S(1)} %copy-done.35, bf16[2,384,768]{2,1,0:T(8,128)(2,1)S(1)} %copy-done.16, bf16[2,384,768]{2,1,0:T(8,128)(2,1)S(1)} %collective-permute-done.26.a_ref, ...), custom_call_target="tpu_custom_call", output_to_operand_aliasing={{0}: (4, {}), {1}: (5, {})} | custom-call | flops 1000 | bytes 1000 | tf_op jit(solution)/shard_map/join/pallas_call | solution.py:225
  183.8 6.1 %project.2 = (bf16[384,1536]{1,0:T(8,128)(2,1)}, bf16[384,1536]{1,0:T(8,128)(2,1)}) custom-call(s32[4]{0:T(128)S(1)} %pad_add_fusion.place, bf16[384,384]{1,0:T(8,128)(2,1)S(1)} %copy-done.21, bf16[384,384]{1,0:T(8,128)(2,1)S(1)} %copy-done.23, bf16[96,3072]{1,0:T(8,128)(2,1)} %refs_0_.5, bf16[96,3072]{1,0:T(8,128)(2,1)} %collective-permute-done.4.refs_1_, ...), custom_call_target="tpu_custom_call" | custom-call | flops 1000 | bytes 1000 | tf_op jit(solution)/shard_map/project/pallas_call | solution.py:339
  190.4 9.3 %collective-permute-done.29 = bf16[96,3072]{1,0:T(8,128)(2,1)} collective-permute-done((bf16[96,3072]{1,0:T(8,128)(2,1)}, bf16[96,3072]{1,0:T(8,128)(2,1)}, u32[]{:S(2)}, u32[]{:S(2)}) %collective-permute-start.29) | collective-permute-done | bytes 589856 | tf_op jit(solution)/shard_map/ppermute | solution.py:39
  199.7 1.8 collective-permute-done.30
  201.6 1.9 convert_add_fusion
  203.5 1.0 copy-done.39
  205.7 2.8 %collective-permute-start.32 = (bf16[96,768]{1,0:T(8,128)(2,1)}, bf16[96,768]{1,0:T(8,128)(2,1)}, u32[]{:S(2)}, u32[]{:S(2)}) collective-permute-start(bf16[96,768]{1,0:T(8,128)(2,1)} %get-tuple-element.63), channel_id=1, source_target_pairs={{0,3},{1,0},{2,1},{3,2},{4,7},{5,4},{6,5},{7,6},{8,11},{9,8},{10,9... | collective-permute-start | bytes 442376 | tf_op jit(solution)/shard_map/ppermute | solution.py:39
  209.5 3.3 %collective-permute-done.31 = bf16[96,768]{1,0:T(8,128)(2,1)} collective-permute-done((bf16[96,768]{1,0:T(8,128)(2,1)}, bf16[96,768]{1,0:T(8,128)(2,1)}, u32[]{:S(2)}, u32[]{:S(2)}) %collective-permute-start.31) | collective-permute-done | bytes 147488 | tf_op jit(solution)/shard_map/ppermute | solution.py:39
  212.8 2.7 %collective-permute-done.33 = bf16[96,768]{1,0:T(8,128)(2,1)} collective-permute-done((bf16[96,768]{1,0:T(8,128)(2,1)}, bf16[96,768]{1,0:T(8,128)(2,1)}, u32[]{:S(2)}, u32[]{:S(2)}) %collective-permute-start.33) | collective-permute-done | bytes 147488 | tf_op jit(solution)/shard_map/ppermute | solution.py:39
  215.5 1.9 add_convert_fusion.1.x_ref
  217.4 6.5 %project.3.rest_0_ = bf16[384,3072]{1,0:T(8,128)(2,1)} custom-call(s32[4]{0:T(128)S(1)} %pad_add_fusion.place, bf16[384,384]{1,0:T(8,128)(2,1)S(1)} %bitcast.70, bf16[384,384]{1,0:T(8,128)(2,1)S(1)} %bitcast.73, bf16[96,3072]{1,0:T(8,128)(2,1)} %refs_0_.5, bf16[96,3072]{1,0:T(8,128)(2,1)} %collective-permute-done.4.refs_1_, ...), custom_call_target="tpu_custom_call" | custom-call | flops 1000 | bytes 1000 | tf_op jit(solution)/shard_map/project/pallas_call | solution.py:339
  224.0 5.3 %collective-permute-done.34 = bf16[96,768]{1,0:T(8,128)(2,1)S(1)} collective-permute-done((bf16[96,768]{1,0:T(8,128)(2,1)}, bf16[96,768]{1,0:T(8,128)(2,1)S(1)}, u32[]{:S(2)}, u32[]{:S(2)}) %collective-permute-start.34) | collective-permute-done | bytes 147488 | tf_op jit(solution)/shard_map/ppermute | solution.py:39
  230.7 2.8 %collective-permute-start.36 = (bf16[96,768]{1,0:T(8,128)(2,1)S(1)}, bf16[96,768]{1,0:T(8,128)(2,1)S(1)}, u32[]{:S(2)}, u32[]{:S(2)}) collective-permute-start(bf16[96,768]{1,0:T(8,128)(2,1)S(1)} %add_convert_fusion.refs_0_), channel_id=1, source_target_pairs={{0,3},{1,0},{2,1},{3,2},{4,7},{5,4},{6,5},{7,6},{8,11},{9,8},{10,9... | collective-permute-start | bytes 442376 | tf_op jit(solution)/shard_map/ppermute | solution.py:39
  234.2 2.5 %collective-permute-done.35.refs_1_ = bf16[96,768]{1,0:T(8,128)(2,1)S(1)} collective-permute-done((bf16[96,768]{1,0:T(8,128)(2,1)S(1)}, bf16[96,768]{1,0:T(8,128)(2,1)S(1)}, u32[]{:S(2)}, u32[]{:S(2)}) %collective-permute-start.35) | collective-permute-done | bytes 147488 | tf_op jit(solution)/shard_map/ppermute | solution.py:39
  236.7 1.2 collective-permute-done.36.refs_2_
  237.8 2.4 collective-permute-done.37.refs_3_
  240.9 2.2 place_columns.1
  (135 shorter events, 16.2 us)
Async XLA Ops:
  4.4 29.1 %collective-permute-start = (bf16[2,384,768]{2,1,0:T(8,128)(2,1)}, bf16[2,384,768]{2,1,0:T(8,128)(2,1)}, u32[]{:S(2)}, u32[]{:S(2)}) collective-permute-start(bf16[2,384,768]{2,1,0:T(8,128)(2,1)} %window.2), channel_id=1, source_target_pairs={{0,1},{1,2},{2,3},{3,4},{4,5},{5,6},{6,7},{8,9},{9,10},{10,11},{11... | collective-permute-start | bytes 3538952 | tf_op jit(solution)/shard_map/ppermute | solution.py:75
  9.0 71.2 %collective-permute-start.7 = (bf16[384,3072]{1,0:T(8,128)(2,1)}, bf16[384,3072]{1,0:T(8,128)(2,1)}, u32[]{:S(2)}, u32[]{:S(2)}) collective-permute-start(bf16[384,3072]{1,0:T(8,128)(2,1)} %bitcast.13.refs_4_), channel_id=1, source_target_pairs={{0,8},{1,9},{2,10},{3,11},{4,12},{5,13},{6,14},{7,15},{8,0},{9,1},... | collective-permute-start | bytes 7077896 | tf_op jit(solution)/shard_map/ppermute | solution.py:39
  9.0 17.2 %collective-permute-start.9 = (bf16[96,3072]{1,0:T(8,128)(2,1)}, bf16[96,3072]{1,0:T(8,128)(2,1)S(1)}, u32[]{:S(2)}, u32[]{:S(2)}) collective-permute-start(bf16[96,3072]{1,0:T(8,128)(2,1)} %refs_0_.5), channel_id=1, source_target_pairs={{0,68},{1,69},{2,70},{3,71},{4,64},{5,65},{6,66},{7,67},{8,76},{9,... | collective-permute-start | bytes 1769480 | tf_op jit(solution)/shard_map/ppermute | solution.py:39
  10.9 30.2 %collective-permute-start.1 = (bf16[2,384,768]{2,1,0:T(8,128)(2,1)}, bf16[2,384,768]{2,1,0:T(8,128)(2,1)}, u32[]{:S(2)}, u32[]{:S(2)}) collective-permute-start(bf16[2,384,768]{2,1,0:T(8,128)(2,1)} %window.2), channel_id=1, source_target_pairs={{1,0},{2,1},{3,2},{4,3},{5,4},{6,5},{7,6},{9,8},{10,9},{11,10},{12... | collective-permute-start | bytes 3538952 | tf_op jit(solution)/shard_map/ppermute | solution.py:79
  27.0 14.1 %copy-start.1 = (bf16[1,384,1536]{2,1,0:T(8,128)(2,1)S(1)}, bf16[1,384,1536]{2,1,0:T(8,128)(2,1)}, u32[]{:S(2)}) copy-start(bf16[1,384,1536]{2,1,0:T(8,128)(2,1)} %param.7) | copy-start | bytes 3538948
  27.0 14.1 %copy-start.3 = (bf16[1,384,1536]{2,1,0:T(8,128)(2,1)S(1)}, bf16[1,384,1536]{2,1,0:T(8,128)(2,1)}, u32[]{:S(2)}) copy-start(bf16[1,384,1536]{2,1,0:T(8,128)(2,1)} %param.8) | copy-start | bytes 3538948
  27.0 34.6 %collective-permute-start.17 = (bf16[384,1536]{1,0:T(8,128)(2,1)}, bf16[384,1536]{1,0:T(8,128)(2,1)}, u32[]{:S(2)}, u32[]{:S(2)}) collective-permute-start(bf16[384,1536]{1,0:T(8,128)(2,1)} %hold.6), channel_id=1, source_target_pairs={{0,68},{1,69},{2,70},{3,71},{4,64},{5,65},{6,66},{7,67},{8,76},{9,... | collective-permute-start | bytes 3538952 | tf_op jit(solution)/shard_map/ppermute | solution.py:39
  28.8 20.1 %collective-permute-start.4 = (bf16[96,3072]{1,0:T(8,128)(2,1)}, bf16[96,3072]{1,0:T(8,128)(2,1)}, u32[]{:S(2)}, u32[]{:S(2)}) collective-permute-start(bf16[96,3072]{1,0:T(8,128)(2,1)} %refs_0_.5), channel_id=1, source_target_pairs={{0,16},{1,17},{2,18},{3,19},{4,20},{5,21},{6,22},{7,23},{8,24},{9,... | collective-permute-start | bytes 1769480 | tf_op jit(solution)/shard_map/ppermute | solution.py:39
  33.5 26.2 %collective-permute-start.5 = (bf16[96,3072]{1,0:T(8,128)(2,1)}, bf16[96,3072]{1,0:T(8,128)(2,1)}, u32[]{:S(2)}, u32[]{:S(2)}) collective-permute-start(bf16[96,3072]{1,0:T(8,128)(2,1)} %refs_0_.5), channel_id=1, source_target_pairs={{0,48},{1,49},{2,50},{3,51},{4,52},{5,53},{6,54},{7,55},{8,56},{9,... | collective-permute-start | bytes 1769480 | tf_op jit(solution)/shard_map/ppermute | solution.py:39
  41.1 5.8 %copy-start.44 = (s32[8,3]{0,1:T(4,128)S(1)}, s32[8,3]{0,1:T(4,128)}, u32[]{:S(2)}) copy-start(s32[8,3]{0,1:T(4,128)} %param.11) | copy-start | bytes 292
  41.1 10.4 %copy-start.4 = (bf16[1,384,1536]{2,1,0:T(8,128)(2,1)S(1)}, bf16[1,384,1536]{2,1,0:T(8,128)(2,1)}, u32[]{:S(2)}) copy-start(bf16[1,384,1536]{2,1,0:T(8,128)(2,1)} %param.6) | copy-start | bytes 3538948
  42.4 46.6 %collective-permute-start.2 = (bf16[2,384,768]{2,1,0:T(8,128)(2,1)}, bf16[2,384,768]{2,1,0:T(8,128)(2,1)}, u32[]{:S(2)}, u32[]{:S(2)}) collective-permute-start(bf16[2,384,768]{2,1,0:T(8,128)(2,1)} %window.3), channel_id=1, source_target_pairs={{0,1},{1,2},{2,3},{3,4},{4,5},{5,6},{6,7},{8,9},{9,10},{10,11},{11... | collective-permute-start | bytes 3538952 | tf_op jit(solution)/shard_map/ppermute | solution.py:75
  48.9 18.7 %collective-permute-start.6 = (bf16[96,3072]{1,0:T(8,128)(2,1)}, bf16[96,3072]{1,0:T(8,128)(2,1)}, u32[]{:S(2)}, u32[]{:S(2)}) collective-permute-start(bf16[96,3072]{1,0:T(8,128)(2,1)} %collective-permute-done.4.refs_1_), channel_id=1, source_target_pairs={{0,16},{1,17},{2,18},{3,19},{4,20},{5,21},{6,22},{7,23},{8,24},{9,... | collective-permute-start | bytes 1769480 | tf_op jit(solution)/shard_map/ppermute | solution.py:39
  51.5 7.4 %copy-start.36 = (s32[3]{0:T(128)}, s32[3]{0:T(128)S(1)}, u32[]{:S(2)}) copy-start(s32[3]{0:T(128)S(1)} %get-tuple-element.68.info) | copy-start | bytes 40
  59.7 18.8 %collective-permute-start.10 = (bf16[96,3072]{1,0:T(8,128)(2,1)}, bf16[96,3072]{1,0:T(8,128)(2,1)}, u32[]{:S(2)}, u32[]{:S(2)}) collective-permute-start(bf16[96,3072]{1,0:T(8,128)(2,1)} %hold.5.refs_0_.refs_4_), channel_id=1, source_target_pairs={{0,16},{1,17},{2,18},{3,19},{4,20},{5,21},{6,22},{7,23},{8,24},{9,... | collective-permute-start | bytes 1769480 | tf_op jit(solution)/shard_map/ppermute | solution.py:39
  61.6 32.4 %collective-permute-start.3 = (bf16[2,384,768]{2,1,0:T(8,128)(2,1)}, bf16[2,384,768]{2,1,0:T(8,128)(2,1)}, u32[]{:S(2)}, u32[]{:S(2)}) collective-permute-start(bf16[2,384,768]{2,1,0:T(8,128)(2,1)} %window.3), channel_id=1, source_target_pairs={{1,0},{2,1},{3,2},{4,3},{5,4},{6,5},{7,6},{9,8},{10,9},{11,10},{12... | collective-permute-start | bytes 3538952 | tf_op jit(solution)/shard_map/ppermute | solution.py:79
  67.6 59.3 %collective-permute-start.19 = (bf16[384,1536]{1,0:T(8,128)(2,1)}, bf16[384,1536]{1,0:T(8,128)(2,1)}, u32[]{:S(2)}, u32[]{:S(2)}) collective-permute-start(bf16[384,1536]{1,0:T(8,128)(2,1)} %hold.7), channel_id=1, source_target_pairs={{0,68},{1,69},{2,70},{3,71},{4,64},{5,65},{6,66},{7,67},{8,76},{9,... | collective-permute-start | bytes 3538952 | tf_op jit(solution)/shard_map/ppermute | solution.py:39
  78.5 36.1 %collective-permute-start.11 = (bf16[96,3072]{1,0:T(8,128)(2,1)}, bf16[96,3072]{1,0:T(8,128)(2,1)}, u32[]{:S(2)}, u32[]{:S(2)}) collective-permute-start(bf16[96,3072]{1,0:T(8,128)(2,1)} %hold.5.refs_0_.refs_4_), channel_id=1, source_target_pairs={{0,48},{1,49},{2,50},{3,51},{4,52},{5,53},{6,54},{7,55},{8,56},{9,... | collective-permute-start | bytes 1769480 | tf_op jit(solution)/shard_map/ppermute | solution.py:39
  80.2 34.3 %collective-permute-start.12 = (bf16[96,3072]{1,0:T(8,128)(2,1)}, bf16[96,3072]{1,0:T(8,128)(2,1)}, u32[]{:S(2)}, u32[]{:S(2)}) collective-permute-start(bf16[96,3072]{1,0:T(8,128)(2,1)} %collective-permute-done.10.refs_1_.refs_5_), channel_id=1, source_target_pairs={{0,16},{1,17},{2,18},{3,19},{4,20},{5,21},{6,22},{7,23},{8,24},{9,... | collective-permute-start | bytes 1769480 | tf_op jit(solution)/shard_map/ppermute | solution.py:39
  89.0 1.9 collective-permute-start.8
  89.0 3.9 %copy-start.33 = (bf16[384,384]{1,0:T(8,128)(2,1)S(1)}, bf16[384,384]{1,0:T(8,128)(2,1)}, u32[]{:S(2)}) copy-start(bf16[384,384]{1,0:T(8,128)(2,1)} %copy-done.32) | copy-start | bytes 884740
  90.9 57.8 %collective-permute-start.18 = (bf16[384,1536]{1,0:T(8,128)(2,1)}, bf16[384,1536]{1,0:T(8,128)(2,1)S(1)}, u32[]{:S(2)}, u32[]{:S(2)}) collective-permute-start(bf16[384,1536]{1,0:T(8,128)(2,1)} %collective-permute-done.17.rest_0_.refs_6_), channel_id=1, source_target_pairs={{0,8},{1,9},{2,10},{3,11},{4,12},{5,13},{6,14},{7,15},{8,0},{9,1},... | collective-permute-start | bytes 3538952 | tf_op jit(solution)/shard_map/ppermute | solution.py:39
  91.0 3.6 %copy-start.34 = (s32[3]{0:T(128)S(1)}, s32[3]{0:T(128)}, u32[]{:S(2)}) copy-start(s32[3]{0:T(128)} %get-tuple-element.69.info) | copy-start | bytes 40
  94.0 27.4 %collective-permute-start.13 = (bf16[384,384]{1,0:T(8,128)(2,1)S(1)}, bf16[384,384]{1,0:T(8,128)(2,1)S(1)}, u32[]{:S(2)}, u32[]{:S(2)}) collective-permute-start(bf16[384,384]{1,0:T(8,128)(2,1)S(1)} %bitcast.83), channel_id=1, source_target_pairs={{0,8},{1,9},{2,10},{3,11},{4,12},{5,13},{6,14},{7,15},{8,0},{9,1},... | collective-permute-start | bytes 884744 | tf_op jit(solution)/shard_map/ppermute | solution.py:39
  94.7 7.4 %copy-start.10 = (bf16[768,384]{1,0:T(8,128)(2,1)S(1)}, bf16[768,384]{1,0:T(8,128)(2,1)}, u32[]{:S(2)}) copy-start(bf16[768,384]{1,0:T(8,128)(2,1)} %copy-done.8) | copy-start | bytes 1769476
  94.7 7.4 %copy-start.37 = (s32[3]{0:T(128)S(1)}, s32[3]{0:T(128)}, u32[]{:S(2)}) copy-start(s32[3]{0:T(128)} %copy-done.36) | copy-start | bytes 40
  102.1 12.5 %copy-start.6 = (bf16[96,3072]{1,0:T(8,128)(2,1)S(1)}, bf16[96,3072]{1,0:T(8,128)(2,1)}, u32[]{:S(2)}) copy-start(bf16[96,3072]{1,0:T(8,128)(2,1)} %hold.5.refs_0_.refs_4_) | copy-start | bytes 1769476
  114.6 6.1 %copy-start.12 = (bf16[2,384,768]{2,1,0:T(8,128)(2,1)}, bf16[2,384,768]{2,1,0:T(8,128)(2,1)S(1)}, u32[]{:S(2)}) copy-start(bf16[2,384,768]{2,1,0:T(8,128)(2,1)S(1)} %get-tuple-element.36.refs_6_.own_ref) | copy-start | bytes 3538948
  120.7 1.7 collective-permute-start.21
  121.0 24.6 %copy-start.24 = (bf16[4,1,96,384]{3,2,1,0:T(8,128)(2,1)}, bf16[4,1,96,384]{3,2,1,0:T(8,128)(2,1)S(1)}, u32[]{:S(2)}) copy-start(bf16[4,1,96,384]{3,2,1,0:T(8,128)(2,1)S(1)} %get-tuple-element.65) | copy-start | bytes 884740
  121.0 4.6 %collective-permute-start.14 = (bf16[384,384]{1,0:T(8,128)(2,1)S(1)}, bf16[384,384]{1,0:T(8,128)(2,1)S(1)}, u32[]{:S(2)}, u32[]{:S(2)}) collective-permute-start(bf16[384,384]{1,0:T(8,128)(2,1)S(1)} %bitcast.80), channel_id=1, source_target_pairs={{0,8},{1,9},{2,10},{3,11},{4,12},{5,13},{6,14},{7,15},{8,0},{9,1},... | collective-permute-start | bytes 884744 | tf_op jit(solution)/shard_map/ppermute | solution.py:39
  121.4 24.2 %copy-start.19 = (bf16[384,384]{1,0:T(8,128)(2,1)}, bf16[384,384]{1,0:T(8,128)(2,1)S(1)}, u32[]{:S(2)}) copy-start(bf16[384,384]{1,0:T(8,128)(2,1)S(1)} %collective-permute-done.13.refs_1_.a_ref) | copy-start | bytes 884740
  121.4 10.3 %collective-permute-start.15 = (bf16[384,384]{1,0:T(8,128)(2,1)S(1)}, bf16[384,384]{1,0:T(8,128)(2,1)S(1)}, u32[]{:S(2)}, u32[]{:S(2)}) collective-permute-start(bf16[384,384]{1,0:T(8,128)(2,1)S(1)} %bitcast.72), channel_id=1, source_target_pairs={{0,68},{1,69},{2,70},{3,71},{4,64},{5,65},{6,66},{7,67},{8,76},{9,... | collective-permute-start | bytes 884744 | tf_op jit(solution)/shard_map/ppermute | solution.py:39
  122.3 29.0 %collective-permute-start.22 = (bf16[2,384,768]{2,1,0:T(8,128)(2,1)}, bf16[2,384,768]{2,1,0:T(8,128)(2,1)}, u32[]{:S(2)}, u32[]{:S(2)}) collective-permute-start(bf16[2,384,768]{2,1,0:T(8,128)(2,1)} %get-tuple-element.42), channel_id=1, source_target_pairs={{0,1},{1,2},{2,3},{3,4},{4,5},{5,6},{6,7},{8,9},{9,10},{10,11},{11... | collective-permute-start | bytes 3538952 | tf_op jit(solution)/shard_map/ppermute | solution.py:75
  125.6 20.0 %copy-start.22 = (bf16[384,384]{1,0:T(8,128)(2,1)}, bf16[384,384]{1,0:T(8,128)(2,1)S(1)}, u32[]{:S(2)}) copy-start(bf16[384,384]{1,0:T(8,128)(2,1)S(1)} %collective-permute-done.14.rest_1_.b_ref) | copy-start | bytes 884740
  125.6 30.8 %collective-permute-start.23 = (bf16[2,384,768]{2,1,0:T(8,128)(2,1)}, bf16[2,384,768]{2,1,0:T(8,128)(2,1)}, u32[]{:S(2)}, u32[]{:S(2)}) collective-permute-start(bf16[2,384,768]{2,1,0:T(8,128)(2,1)} %get-tuple-element.43), channel_id=1, source_target_pairs={{1,0},{2,1},{3,2},{4,3},{5,4},{6,5},{7,6},{9,8},{10,9},{11,10},{12... | collective-permute-start | bytes 3538952 | tf_op jit(solution)/shard_map/ppermute | solution.py:79
  126.9 29.5 %collective-permute-start.20 = (bf16[384,1536]{1,0:T(8,128)(2,1)}, bf16[384,1536]{1,0:T(8,128)(2,1)}, u32[]{:S(2)}, u32[]{:S(2)}) collective-permute-start(bf16[384,1536]{1,0:T(8,128)(2,1)} %collective-permute-done.19.refs_8_), channel_id=1, source_target_pairs={{0,8},{1,9},{2,10},{3,11},{4,12},{5,13},{6,14},{7,15},{8,0},{9,1},... | collective-permute-start | bytes 3538952 | tf_op jit(solution)/shard_map/ppermute | solution.py:39
  131.7 13.9 %copy-start.28 = (bf16[384,384]{1,0:T(8,128)(2,1)}, bf16[384,384]{1,0:T(8,128)(2,1)S(1)}, u32[]{:S(2)}) copy-start(bf16[384,384]{1,0:T(8,128)(2,1)S(1)} %collective-permute-done.15.refs_2_) | copy-start | bytes 884740
  131.7 14.9 %collective-permute-start.16 = (bf16[384,384]{1,0:T(8,128)(2,1)S(1)}, bf16[384,384]{1,0:T(8,128)(2,1)S(1)}, u32[]{:S(2)}, u32[]{:S(2)}) collective-permute-start(bf16[384,384]{1,0:T(8,128)(2,1)S(1)} %bitcast.81), channel_id=1, source_target_pairs={{0,76},{1,77},{2,78},{3,79},{4,72},{5,73},{6,74},{7,75},{8,68},{9,... | collective-permute-start | bytes 884744 | tf_op jit(solution)/shard_map/ppermute | solution.py:39
  147.4 33.1 %collective-permute-start.26 = (bf16[2,384,768]{2,1,0:T(8,128)(2,1)}, bf16[2,384,768]{2,1,0:T(8,128)(2,1)S(1)}, u32[]{:S(2)}, u32[]{:S(2)}) collective-permute-start(bf16[2,384,768]{2,1,0:T(8,128)(2,1)} %get-tuple-element.48), channel_id=1, source_target_pairs={{0,1},{1,2},{2,3},{3,4},{4,5},{5,6},{6,7},{8,9},{9,10},{10,11},{11... | collective-permute-start | bytes 3538952 | tf_op jit(solution)/shard_map/ppermute | solution.py:75
  149.8 31.1 %collective-permute-start.27 = (bf16[2,384,768]{2,1,0:T(8,128)(2,1)}, bf16[2,384,768]{2,1,0:T(8,128)(2,1)}, u32[]{:S(2)}, u32[]{:S(2)}) collective-permute-start(bf16[2,384,768]{2,1,0:T(8,128)(2,1)} %get-tuple-element.49), channel_id=1, source_target_pairs={{1,0},{2,1},{3,2},{4,3},{5,4},{6,5},{7,6},{9,8},{10,9},{11,10},{12... | collective-permute-start | bytes 3538952 | tf_op jit(solution)/shard_map/ppermute | solution.py:79
  162.8 14.5 %copy-start.13 = (bf16[2,384,768]{2,1,0:T(8,128)(2,1)S(1)}, bf16[2,384,768]{2,1,0:T(8,128)(2,1)}, u32[]{:S(2)}) copy-start(bf16[2,384,768]{2,1,0:T(8,128)(2,1)} %copy-done.12) | copy-start | bytes 3538948
  162.8 14.5 %copy-start.38 = (s32[3]{0:T(128)S(1)}, s32[3]{0:T(128)}, u32[]{:S(2)}) copy-start(s32[3]{0:T(128)} %copy-done.36) | copy-start | bytes 40
  172.8 10.9 %copy-start.11 = (bf16[96,3072]{1,0:T(8,128)(2,1)}, bf16[96,3072]{1,0:T(8,128)(2,1)S(1)}, u32[]{:S(2)}) copy-start(bf16[96,3072]{1,0:T(8,128)(2,1)S(1)} %get-tuple-element.44.refs_8_.x_ref) | copy-start | bytes 1769476
  172.8 17.6 %collective-permute-start.28 = (bf16[96,3072]{1,0:T(8,128)(2,1)}, bf16[96,3072]{1,0:T(8,128)(2,1)}, u32[]{:S(2)}, u32[]{:S(2)}) collective-permute-start(bf16[96,3072]{1,0:T(8,128)(2,1)} %get-tuple-element.54), channel_id=1, source_target_pairs={{0,16},{1,17},{2,18},{3,19},{4,20},{5,21},{6,22},{7,23},{8,24},{9,... | collective-permute-start | bytes 1769480 | tf_op jit(solution)/shard_map/ppermute | solution.py:39
  172.8 26.9 %collective-permute-start.29 = (bf16[96,3072]{1,0:T(8,128)(2,1)}, bf16[96,3072]{1,0:T(8,128)(2,1)}, u32[]{:S(2)}, u32[]{:S(2)}) collective-permute-start(bf16[96,3072]{1,0:T(8,128)(2,1)} %get-tuple-element.55), channel_id=1, source_target_pairs={{0,48},{1,49},{2,50},{3,51},{4,52},{5,53},{6,54},{7,55},{8,56},{9,... | collective-permute-start | bytes 1769480 | tf_op jit(solution)/shard_map/ppermute | solution.py:39
  176.1 25.5 %collective-permute-start.30 = (bf16[96,3072]{1,0:T(8,128)(2,1)}, bf16[96,3072]{1,0:T(8,128)(2,1)}, u32[]{:S(2)}, u32[]{:S(2)}) collective-permute-start(bf16[96,3072]{1,0:T(8,128)(2,1)} %get-tuple-element.56), channel_id=1, source_target_pairs={{0,32},{1,33},{2,34},{3,35},{4,36},{5,37},{6,38},{7,39},{8,40},{9,... | collective-permute-start | bytes 1769480 | tf_op jit(solution)/shard_map/ppermute | solution.py:39
  177.3 3.6 %copy-start.16 = (bf16[2,384,768]{2,1,0:T(8,128)(2,1)S(1)}, bf16[2,384,768]{2,1,0:T(8,128)(2,1)}, u32[]{:S(2)}) copy-start(bf16[2,384,768]{2,1,0:T(8,128)(2,1)} %copy-done.14) | copy-start | bytes 3538948
  177.3 3.6 %copy-start.35 = (s32[3]{0:T(128)S(1)}, s32[3]{0:T(128)}, u32[]{:S(2)}) copy-start(s32[3]{0:T(128)} %get-tuple-element.69.info) | copy-start | bytes 40
  180.8 2.9 %copy-start.7 = (bf16[96,3072]{1,0:T(8,128)(2,1)S(1)}, bf16[96,3072]{1,0:T(8,128)(2,1)}, u32[]{:S(2)}) copy-start(bf16[96,3072]{1,0:T(8,128)(2,1)} %hold.5.refs_0_.refs_4_) | copy-start | bytes 1769476
  180.8 2.9 %copy-start.21 = (bf16[384,384]{1,0:T(8,128)(2,1)S(1)}, bf16[384,384]{1,0:T(8,128)(2,1)}, u32[]{:S(2)}) copy-start(bf16[384,384]{1,0:T(8,128)(2,1)} %copy-done.19) | copy-start | bytes 884740
  189.9 27.5 %collective-permute-start.24 = (bf16[384,1536]{1,0:T(8,128)(2,1)}, bf16[384,1536]{1,0:T(8,128)(2,1)S(1)}, u32[]{:S(2)}, u32[]{:S(2)}) collective-permute-start(bf16[384,1536]{1,0:T(8,128)(2,1)} %get-tuple-element.45), channel_id=1, source_target_pairs={{0,8},{1,9},{2,10},{3,11},{4,12},{5,13},{6,14},{7,15},{8,0},{9,1},... | collective-permute-start | bytes 3538952 | tf_op jit(solution)/shard_map/ppermute | solution.py:39
  189.9 27.5 %collective-permute-start.25 = (bf16[384,1536]{1,0:T(8,128)(2,1)}, bf16[384,1536]{1,0:T(8,128)(2,1)S(1)}, u32[]{:S(2)}, u32[]{:S(2)}) collective-permute-start(bf16[384,1536]{1,0:T(8,128)(2,1)} %get-tuple-element.46), channel_id=1, source_target_pairs={{0,8},{1,9},{2,10},{3,11},{4,12},{5,13},{6,14},{7,15},{8,0},{9,1},... | collective-permute-start | bytes 3538952 | tf_op jit(solution)/shard_map/ppermute | solution.py:39
  204.5 12.9 %copy-start.18 = (bf16[4,1,96,384]{3,2,1,0:T(8,128)(2,1)S(1)}, bf16[4,1,96,384]{3,2,1,0:T(8,128)(2,1)}, u32[]{:S(2)}) copy-start(bf16[4,1,96,384]{3,2,1,0:T(8,128)(2,1)} %get-tuple-element.67) | copy-start | bytes 884740
  204.5 12.9 %copy-start.25 = (bf16[4,1,96,384]{3,2,1,0:T(8,128)(2,1)S(1)}, bf16[4,1,96,384]{3,2,1,0:T(8,128)(2,1)}, u32[]{:S(2)}) copy-start(bf16[4,1,96,384]{3,2,1,0:T(8,128)(2,1)} %copy-done.24) | copy-start | bytes 884740
  205.3 7.5 %collective-permute-start.31 = (bf16[96,768]{1,0:T(8,128)(2,1)}, bf16[96,768]{1,0:T(8,128)(2,1)}, u32[]{:S(2)}, u32[]{:S(2)}) collective-permute-start(bf16[96,768]{1,0:T(8,128)(2,1)} %get-tuple-element.61), channel_id=1, source_target_pairs={{0,1},{1,2},{2,3},{3,0},{4,5},{5,6},{6,7},{7,4},{8,9},{9,10},{10,1... | collective-permute-start | bytes 442376 | tf_op jit(solution)/shard_map/ppermute | solution.py:39
  205.7 7.1 %collective-permute-start.32 = (bf16[96,768]{1,0:T(8,128)(2,1)}, bf16[96,768]{1,0:T(8,128)(2,1)}, u32[]{:S(2)}, u32[]{:S(2)}) collective-permute-start(bf16[96,768]{1,0:T(8,128)(2,1)} %get-tuple-element.63), channel_id=1, source_target_pairs={{0,3},{1,0},{2,1},{3,2},{4,7},{5,4},{6,5},{7,6},{8,11},{9,8},{10,9... | collective-permute-start | bytes 442376 | tf_op jit(solution)/shard_map/ppermute | solution.py:39
  208.5 7.0 %collective-permute-start.33 = (bf16[96,768]{1,0:T(8,128)(2,1)}, bf16[96,768]{1,0:T(8,128)(2,1)}, u32[]{:S(2)}, u32[]{:S(2)}) collective-permute-start(bf16[96,768]{1,0:T(8,128)(2,1)} %get-tuple-element.62), channel_id=1, source_target_pairs={{0,2},{1,3},{2,0},{3,1},{4,6},{5,7},{6,4},{7,5},{8,10},{9,11},{10,... | collective-permute-start | bytes 442376 | tf_op jit(solution)/shard_map/ppermute | solution.py:39
  223.9 5.4 %collective-permute-start.34 = (bf16[96,768]{1,0:T(8,128)(2,1)}, bf16[96,768]{1,0:T(8,128)(2,1)S(1)}, u32[]{:S(2)}, u32[]{:S(2)}) collective-permute-start(bf16[96,768]{1,0:T(8,128)(2,1)} %hold.9), channel_id=1, source_target_pairs={{0,4},{1,5},{2,6},{3,7},{4,0},{5,1},{6,2},{7,3},{8,12},{9,13},{10,... | collective-permute-start | bytes 442376 | tf_op jit(solution)/shard_map/ppermute | solution.py:39
  230.2 10.0 %copy-start.40 = (bf16[96,768]{1,0:T(8,128)(2,1)}, bf16[96,768]{1,0:T(8,128)(2,1)S(1)}, u32[]{:S(2)}) copy-start(bf16[96,768]{1,0:T(8,128)(2,1)S(1)} %add_convert_fusion.refs_0_) | copy-start | bytes 442372
  230.3 6.4 %collective-permute-start.35 = (bf16[96,768]{1,0:T(8,128)(2,1)S(1)}, bf16[96,768]{1,0:T(8,128)(2,1)S(1)}, u32[]{:S(2)}, u32[]{:S(2)}) collective-permute-start(bf16[96,768]{1,0:T(8,128)(2,1)S(1)} %add_convert_fusion.refs_0_), channel_id=1, source_target_pairs={{0,1},{1,2},{2,3},{3,0},{4,5},{5,6},{6,7},{7,4},{8,9},{9,10},{10,1... | collective-permute-start | bytes 442376 | tf_op jit(solution)/shard_map/ppermute | solution.py:39
  230.7 7.1 %collective-permute-start.36 = (bf16[96,768]{1,0:T(8,128)(2,1)S(1)}, bf16[96,768]{1,0:T(8,128)(2,1)S(1)}, u32[]{:S(2)}, u32[]{:S(2)}) collective-permute-start(bf16[96,768]{1,0:T(8,128)(2,1)S(1)} %add_convert_fusion.refs_0_), channel_id=1, source_target_pairs={{0,3},{1,0},{2,1},{3,2},{4,7},{5,4},{6,5},{7,6},{8,11},{9,8},{10,9... | collective-permute-start | bytes 442376 | tf_op jit(solution)/shard_map/ppermute | solution.py:39
  233.6 6.6 %collective-permute-start.37 = (bf16[96,768]{1,0:T(8,128)(2,1)S(1)}, bf16[96,768]{1,0:T(8,128)(2,1)S(1)}, u32[]{:S(2)}, u32[]{:S(2)}) collective-permute-start(bf16[96,768]{1,0:T(8,128)(2,1)S(1)} %add_convert_fusion.refs_0_), channel_id=1, source_target_pairs={{0,2},{1,3},{2,0},{3,1},{4,6},{5,7},{6,4},{7,5},{8,10},{9,11},{10,... | collective-permute-start | bytes 442376 | tf_op jit(solution)/shard_map/ppermute | solution.py:39
  236.7 3.5 %copy-start.41 = (bf16[96,768]{1,0:T(8,128)(2,1)}, bf16[96,768]{1,0:T(8,128)(2,1)S(1)}, u32[]{:S(2)}) copy-start(bf16[96,768]{1,0:T(8,128)(2,1)S(1)} %collective-permute-done.35.refs_1_) | copy-start | bytes 442372
  (19 other events, 22.1 us)

commit v3 on v2

--- a/solution.py
+++ b/solution.py
@@ -12,10 +12,13 @@
 SCALE = 1.0 / math.sqrt(HEAD)
 LOG2_SCALE = SCALE * math.log2(math.e)
 FAR = 1e30
+TILE_AT, CORE_AT, FROM_Z, TO_Z, TO_Y, FROM_Y, AROUND = 2, 3, 4, 8, 12, 16, 20
+SLOTS = 3
 COST = pl.CostEstimate(flops=1000, bytes_accessed=1000, transcendentals=0)
 BF = jnp.bfloat16
 F32 = jnp.float32
-VMEM_LIMIT = 24 * 1024 * 1024
+VMEM_LIMIT = 60 * 1024 * 1024
+WG_STEPS = 4
 
 NX, NZ, NC, NL, NY = 2, 4, 2, 2, 4
 NS = NL * NY
@@ -121,9 +124,18 @@
     return (acc / total).astype(BF), top + jnp.log2(total)
 
 
-def forward_kernel(per, info, q_ref, k_ref, v_ref, left_ref, right_ref, *rest):
+def live_sides(info):
+    tile = info[TILE_AT]
+    found = [jnp.zeros((), jnp.bool_)] * 2
+    for i in range(SLOTS):
+        entry = info[AROUND + SLOTS * tile + i]
+        found = [on | ((entry == tile + d) & (entry >= 0)) for on, d in zip(found, (-1, 1))]
+    return found
+
+
+def forward_kernel(per, part, info, q_ref, k_ref, v_ref, left_ref, right_ref, *rest):
     attn_ref, total_ref = rest[-2:]
-    live = (info[1] > 0, info[2] > 0)
+    live = live_sides(info)
     for i in range(per):
         cols = slice(i * HEAD, (i + 1) * HEAD)
         attn_ref[cols, :], total_ref[i] = forward_head(
@@ -131,13 +143,13 @@
         )
 
 
-def attend(info, q, k, v, left, right, heads, before=()):
+def attend(part, info, q, k, v, left, right, heads, before=()):
     rows = q.shape[0]
     per = PER_F
-    own = pl.BlockSpec((rows, per * HEAD), lambda h, info: (0, info[0] // per + h))
+    own = pl.BlockSpec((rows, per * HEAD), lambda h, info: (0, info[part] // per + h))
     side = pl.BlockSpec((2, rows, per * HEAD), lambda h, info: (0, 0, h))
     return pl.pallas_call(
-        functools.partial(forward_kernel, per),
+        functools.partial(forward_kernel, per, part),
         out_shape=(
             jax.ShapeDtypeStruct((heads * HEAD, rows), BF),
             jax.ShapeDtypeStruct((heads, 1, rows), F32),
@@ -157,14 +169,25 @@
     )(info, q, k, v, left, right, *before)
 
 
-def backward_kernel(per, info, q_ref, k_ref, v_ref, left_ref, right_ref, grad_ref, attn_ref, total_ref, *rest):
-    dq_ref, own_ref, to_left_ref, to_right_ref = rest[-4:]
+def backward_kernel(per, part, info, q_ref, k_ref, v_ref, left_ref, right_ref, mine_ref, theirs_ref, attn_ref, total_ref, *rest):
+    dq_ref, own_ref, to_left_ref, to_right_ref, grad_ref = rest[-5:]
+    step = pl.program_id(0)
+
+    @pl.when(step == 0)
+    def _():
+        size = mine_ref.shape[0] // NZ
+        for i in range(NZ):
+            for ref, core in ((mine_ref, info[CORE_AT]), (theirs_ref, 1 - info[CORE_AT])):
+                spot = pl.multiple_of((NC * i + core) * size, size)
+                grad_ref[pl.ds(spot, size), :] = ref[i * size:(i + 1) * size, :]
+
     outs = (to_left_ref, own_ref, to_right_ref)
-    live = (info[1] > 0, info[2] > 0)
+    live = live_sides(info)
     for i in range(per):
         cols = slice(i * HEAD, (i + 1) * HEAD)
         q = q_ref[:, cols]
-        g = grad_ref[cols, :]
+        here = pl.multiple_of((step * per + i) * HEAD, HEAD)
+        g = grad_ref[pl.ds(here, HEAD), :]
         total = total_ref[i]
         delta = jnp.sum(g.astype(F32) * attn_ref[cols, :].astype(F32), axis=0, keepdims=True)
         keys = (left_ref[0, :, cols], k_ref[:, cols], right_ref[0, :, cols])
@@ -182,29 +205,32 @@
         dq_ref[:, cols] = (dq * SCALE).T.astype(BF)
 
 
-def attend_back(info, q, k, v, left, right, grad, attn, total, heads, before, again):
+def attend_back(part, info, q, k, v, left, right, grads, attn, total, heads, before, again):
     rows, cols = q.shape
     per = PER_B
-    own = pl.BlockSpec((rows, per * HEAD), lambda h, info: (0, info[0] // per + h))
+    own = pl.BlockSpec((rows, per * HEAD), lambda h, info: (0, info[part] // per + h))
     side = pl.BlockSpec((2, rows, per * HEAD), lambda h, info: (0, 0, h))
     turned = pl.BlockSpec((per * HEAD, rows), lambda h, info: (h, 0))
     return pl.pallas_call(
-        functools.partial(backward_kernel, per),
+        functools.partial(backward_kernel, per, part),
         out_shape=(jax.ShapeDtypeStruct((rows, cols), BF),)
         + (jax.ShapeDtypeStruct((2, rows, heads * HEAD), BF),) * 3,
         grid_spec=pltpu.PrefetchScalarGridSpec(
             num_scalar_prefetch=1,
             grid=(heads // per,),
-            in_specs=[own, own, own, side, side, turned, turned,
+            in_specs=[own, own, own, side, side]
+            + [pl.BlockSpec(grads[0].shape, lambda h, info: (0, 0))] * 2
+            + [turned,
                       pl.BlockSpec((per, 1, rows), lambda h, info: (h, 0, 0))]
             + [pl.BlockSpec(memory_space=pl.ANY)] * len(before),
             out_specs=(own, side, side, side),
-        ),
-        input_output_aliases={9: 0} if again else {},
+            scratch_shapes=[pltpu.VMEM((heads * HEAD, rows), BF)],
+        ),
+        input_output_aliases={10: 0} if again else {},
         compiler_params=pltpu.CompilerParams(vmem_limit_bytes=VMEM_LIMIT),
         cost_estimate=COST,
         name="attend_back",
-    )(info, q, k, v, left, right, grad, attn, total, *before)
+    )(info, q, k, v, left, right, *grads, attn, total, *before)
 
 
 JOIN_ROWS = 192
@@ -216,11 +242,11 @@
         out[...] = (own_ref[i].astype(F32) + a_ref[i].astype(F32) + b_ref[i].astype(F32)).astype(BF)
 
 
-def join(info, own, a, b, heads, cols, before):
+def join(part, info, own, a, b, heads, cols, before):
     rows = own.shape[1]
     wide = heads * HEAD
     side = pl.BlockSpec((2, JOIN_ROWS, wide), lambda r, info: (0, r, 0))
-    out = pl.BlockSpec((JOIN_ROWS, wide), lambda r, info: (r, info[0] // heads))
+    out = pl.BlockSpec((JOIN_ROWS, wide), lambda r, info: (r, info[part] // heads))
     first = before is None
     return pl.pallas_call(
         functools.partial(join_kernel, first),
@@ -255,24 +281,29 @@
     )(x, *before)
 
 
-def window_kernel(info, k_ref, v_ref, *rest):
-    rest[-1][0] = k_ref[...]
-    rest[-1][1] = v_ref[...]
-
-
-def window(info, k, v, heads, before=()):
+def window_kernel(part, info, k_ref, v_ref, *rest):
+    out, sems = rest[-2:]
+    wide = out.shape[2]
+    cols = pl.ds(pl.multiple_of(info[part] * HEAD, wide), wide)
+    copies = [
+        pltpu.make_async_copy(ref.at[:, cols], out.at[j], sems.at[j])
+        for j, ref in enumerate((k_ref, v_ref))
+    ]
+    for copy in copies:
+        copy.start()
+    for copy in copies:
+        copy.wait()
+
+
+def window(part, info, k, v, heads, before=()):
     rows = k.shape[0]
-    wide = heads * HEAD
-    block = pl.BlockSpec((rows // 2, wide), lambda r, info: (r, info[0] // heads))
-    return pl.pallas_call(
-        window_kernel,
-        out_shape=jax.ShapeDtypeStruct((2, rows, wide), BF),
-        grid_spec=pltpu.PrefetchScalarGridSpec(
-            num_scalar_prefetch=1,
-            grid=(2,),
-            in_specs=[block, block] + [pl.BlockSpec(memory_space=pl.ANY)] * len(before),
-            out_specs=pl.BlockSpec((2, rows // 2, wide), lambda r, info: (0, r, 0)),
-        ),
+    return pl.pallas_call(
+        functools.partial(window_kernel, part),
+        out_shape=jax.ShapeDtypeStruct((2, rows, heads * HEAD), BF),
+        in_specs=[pl.BlockSpec(memory_space=pltpu.SMEM)]
+        + [pl.BlockSpec(memory_space=pl.ANY)] * (2 + len(before)),
+        out_specs=pl.BlockSpec(memory_space=pltpu.VMEM),
+        scratch_shapes=[pltpu.SemaphoreType.DMA((2,))],
         compiler_params=pltpu.CompilerParams(vmem_limit_bytes=VMEM_LIMIT),
         cost_estimate=COST,
         name="window",
@@ -284,7 +315,7 @@
     mine_ref, theirs_ref, w = refs[-3:]
     rows = pieces[0].shape[0]
     for i, piece in enumerate(pieces):
-        w[pl.ds(pl.multiple_of(place[i] * rows, rows), rows), :] = piece[...]
+        w[pl.ds(pl.multiple_of(place[FROM_Z + i] * rows, rows), rows), :] = piece[...]
     mine_ref[...] = nt(w[...], u_ref[...]).astype(BF)
     theirs_ref[...] = nt(w[...], other_ref[...]).astype(BF)
 
@@ -306,107 +337,146 @@
     )(place, *pieces, u, other, *before)
 
 
-SPLIT = 2
-
-
-def project_kernel(adds, place, a_ref, b_ref, *refs):
-    pieces, sent = refs[:2 * NZ], refs[2 * NZ:2 * NZ + adds]
-    outs, w = refs[-1 - (1 if adds else SPLIT):-1], refs[-1]
+def project_kernel(place, *refs):
+    turned, pieces = refs[:4], refs[4:4 + 2 * NZ]
+    near_ref, far_refs, w = refs[-4], refs[-3:-1], refs[-1]
     rows = pieces[0].shape[0]
     half = NZ * rows
     for i, piece in enumerate(pieces):
-        spot = (i // NZ) * half + place[i % NZ] * rows
+        spot = (i // NZ) * half + place[FROM_Z + i % NZ] * rows
         w[pl.ds(pl.multiple_of(spot, rows), rows), :] = piece[...]
-    block = w.shape[1] // SPLIT
-    first, second = a_ref[...].T, b_ref[...].T
-    for i in range(SPLIT):
+    wide = w.shape[1]
+    block = wide // 4
+    first, second = turned[2][...].T, turned[3][...].T
+    for i in range(4):
         cols = slice(i * block, (i + 1) * block)
+        there = slice(i % 2 * block, (i % 2 + 1) * block)
         total = nn(first, w[:half, cols]) + nn(second, w[half:, cols])
-        if adds:
-            outs[0][:, cols] = (total + sent[i][...].astype(F32)).astype(BF)
-        else:
-            outs[i][...] = total.astype(BF)
-
-
-def project(place, a, b, pieces, sent, before=()):
-    tokens = a.shape[1]
+        far_refs[i // 2][:, there] = total.astype(BF)
+    first, second = turned[0][...].T, turned[1][...].T
+    for i in range(4):
+        cols = slice(i * block, (i + 1) * block)
+        near_ref[:, cols] = (nn(first, w[:half, cols]) + nn(second, w[half:, cols])).astype(BF)
+
+
+def project(place, turned, pieces, before):
+    tokens = turned[0].shape[1]
     rows, wide = pieces[0].shape
     whole = pl.BlockSpec(memory_space=pltpu.VMEM)
-    if sent:
-        out_shape = (jax.ShapeDtypeStruct((tokens, wide), BF),)
-    else:
-        out_shape = (jax.ShapeDtypeStruct((tokens, wide // SPLIT), BF),) * SPLIT
-    return pl.pallas_call(
-        functools.partial(project_kernel, len(sent)),
-        out_shape=out_shape,
-        in_specs=[pl.BlockSpec(memory_space=pltpu.SMEM)] + [whole] * (2 + 2 * NZ + len(sent))
+    return pl.pallas_call(
+        project_kernel,
+        out_shape=(jax.ShapeDtypeStruct((tokens, wide), BF),)
+        + (jax.ShapeDtypeStruct((tokens, wide // 2), BF),) * 2,
+        in_specs=[pl.BlockSpec(memory_space=pltpu.SMEM)] + [whole] * (4 + 2 * NZ)
         + [pl.BlockSpec(memory_space=pl.ANY)] * len(before),
-        out_specs=(whole,) * len(out_shape),
+        out_specs=(whole,) * 3,
         scratch_shapes=[pltpu.VMEM((2 * NZ * rows, wide), BF)],
-        compiler_params=pltpu.CompilerParams(vmem_limit_bytes=32 * 1024 * 1024),
+        compiler_params=pltpu.CompilerParams(vmem_limit_bytes=VMEM_LIMIT),
         cost_estimate=COST,
         name="project",
-    )(place, a, b, *pieces, *sent, *before)
+    )(place, *turned, *pieces, *before)
+
+
+def meet_kernel(near_ref, first_ref, second_ref, out_ref):
+    half = first_ref.shape[1]
+    for i, ref in enumerate((first_ref, second_ref)):
+        cols = slice(i * half, (i + 1) * half)
+        out_ref[:, cols] = (near_ref[:, cols].astype(F32) + ref[...].astype(F32)).astype(BF)
+
+
+def meet(near, first, second):
+    tokens, wide = near.shape
+    block = 128
+    spec = pl.BlockSpec((block, wide), lambda i: (i, 0))
+    half = pl.BlockSpec((block, wide // 2), lambda i: (i, 0))
+    return pl.pallas_call(
+        meet_kernel,
+        out_shape=jax.ShapeDtypeStruct((tokens, wide), BF),
+        grid=(tokens // block,),
+        in_specs=[spec, half, half],
+        out_specs=spec,
+        compiler_params=pltpu.CompilerParams(vmem_limit_bytes=VMEM_LIMIT),
+        cost_estimate=COST,
+        name="meet",
+    )(near, first, second)
 
 
 def weight_grad_kernel(place, *refs):
-    a_refs, u_refs, half_refs = refs[:4], refs[4:6], refs[6:10]
+    a_refs, u_refs = refs[:4], refs[4:8]
     out_refs, total = refs[-1 - NZ:-1], refs[-1]
-    near = sum(nn(a[...], u[...]) for a, u in zip(a_refs, u_refs))
-    for i in range(2):
-
-        @pl.when(pl.program_id(0) == i)
-        def _():
-            far = sum(nn(a[...], u[...]) for a, u in zip(a_refs[2:], half_refs[2 * i:]))
-            total[...] = (near + far).astype(BF)
-
+    total[...] = sum(nn(a[...], u[...]) for a, u in zip(a_refs, u_refs)).astype(BF)
     rows = out_refs[0].shape[0]
     for i, out in enumerate(out_refs):
-        out[...] = total[pl.ds(pl.multiple_of(place[i] * rows, rows), rows), :]
-
-
-def weight_grad(place, a_list, u, core, first, second, before):
+        out[...] = total[pl.ds(pl.multiple_of(place[TO_Z + i] * rows, rows), rows), :]
+
+
+def weight_grad(place, a_list, u_list, before):
     rows, tokens = a_list[0].shape
-    wide = u.shape[1]
-    block = wide // 2
+    wide = u_list[0].shape[1]
+    block = wide // WG_STEPS
     sub = rows // NZ
     return pl.pallas_call(
         weight_grad_kernel,
         out_shape=(jax.ShapeDtypeStruct((sub, wide), BF),) * NZ,
         grid_spec=pltpu.PrefetchScalarGridSpec(
             num_scalar_prefetch=1,
-            grid=(wide // block,),
+            grid=(WG_STEPS,),
             in_specs=[pl.BlockSpec((rows, tokens), lambda i, p: (0, 0))] * 4
-            + [pl.BlockSpec((tokens, block), lambda i, p: (0, i))] * 2
-            + [pl.BlockSpec((tokens, block), lambda i, p: (0, 0))] * 4
+            + [pl.BlockSpec((tokens, block), lambda i, p: (0, i))] * 4
             + [pl.BlockSpec(memory_space=pl.ANY)] * len(before),
             out_specs=(pl.BlockSpec((sub, block), lambda i, p: (0, i)),) * NZ,
             scratch_shapes=[pltpu.VMEM((rows, block), BF)],
         ),
-        compiler_params=pltpu.CompilerParams(vmem_limit_bytes=32 * 1024 * 1024),
+        compiler_params=pltpu.CompilerParams(vmem_limit_bytes=VMEM_LIMIT),
         cost_estimate=COST,
         name="weight_grad",
-    )(place, *a_list, u, core, *first, *second, *before)
+    )(place, *a_list, *u_list, *before)
+
+
+def sum_columns_kernel(place, *refs):
+    pieces, outs = refs[:NZ], refs[-NY:]
+    wide = outs[0].shape[1]
+    for i, out in enumerate(outs):
+        cols = pl.ds(pl.multiple_of(place[TO_Y + i] * wide, wide), wide)
+        out[...] = sum(piece[:, cols].astype(F32) for piece in pieces).astype(out.dtype)
+
+
+def sum_columns(place, pieces, before):
+    rows, cols = pieces[0].shape
+    whole = pl.BlockSpec(memory_space=pltpu.VMEM)
+    return pl.pallas_call(
+        sum_columns_kernel,
+        out_shape=tuple(
+            jax.ShapeDtypeStruct((rows, cols // NY), F32 if i == 0 else BF) for i in range(NY)
+        ),
+        in_specs=[pl.BlockSpec(memory_space=pltpu.SMEM)] + [whole] * NZ
+        + [pl.BlockSpec(memory_space=pl.ANY)] * len(before),
+        out_specs=(whole,) * NY,
+        compiler_params=pltpu.CompilerParams(vmem_limit_bytes=VMEM_LIMIT),
+        cost_estimate=COST,
+        name="sum_columns",
+    )(place, *pieces, *before)
 
 
 def place_kernel(spots, *refs):
     out_ref = refs[-1]
     wide = refs[0].shape[1]
-    for j, ref in enumerate(refs[:-1]):
-        out_ref[:, pl.ds(pl.multiple_of(spots[j] * wide, wide), wide)] = ref[...].astype(F32)
-
-
-def place_columns(spots, *pieces):
+    for j, ref in enumerate(refs[:NY]):
+        out_ref[:, pl.ds(pl.multiple_of(spots[FROM_Y + j] * wide, wide), wide)] = ref[...].astype(F32)
+
+
+def place_columns(spots, pieces, before):
     rows, cols = pieces[0].shape
     whole = pl.BlockSpec(memory_space=pltpu.VMEM)
     return pl.pallas_call(
         place_kernel,
         out_shape=jax.ShapeDtypeStruct((rows, len(pieces) * cols), F32),
-        in_specs=[pl.BlockSpec(memory_space=pltpu.SMEM)] + [whole] * len(pieces),
+        in_specs=[pl.BlockSpec(memory_space=pltpu.SMEM)] + [whole] * NY
+        + [pl.BlockSpec(memory_space=pl.ANY)] * len(before),
         out_specs=whole,
         cost_estimate=COST,
         name="place_columns",
-    )(spots, *pieces)
+    )(spots, *pieces, *before)
 
 
 def add(*terms):
@@ -423,44 +493,41 @@
     a, z, c = dp // (NZ * NC), (dp // NC) % NZ, dp % NC
     lo, y = tile // NY, tile % NY
 
-    own_list = neighbours[tile]
-    live_left = jnp.any((own_list == tile - 1) & (own_list >= 0)).astype(jnp.int32)
-    live_right = jnp.any(own_list == tile + 1).astype(jnp.int32)
-    infos = [
-        jnp.stack([part * heads, live_left, live_right]).astype(jnp.int32) for part in (a, 1 - a)
-    ]
-
-    sides = [jnp.full((1,), part * heads, jnp.int32) for part in (a, 1 - a)]
-    pair = window(sides[0], k, v, heads)
+    info = [a * heads, (1 - a) * heads, tile, c]
+    info += [(z + i) % NZ for i in (0, 3, 1, 2)] + [(z + i) % NZ for i in range(NZ)]
+    info += [(y + i) % NY for i in range(NY)] + [(y + i) % NY for i in (0, 3, 1, 2)]
+    info = jnp.concatenate([jnp.stack(info).astype(jnp.int32), neighbours.reshape(-1)])
+    pair = window(0, info, k, v, heads)
     near0 = (to_next(pair), to_previous(pair))
-    pair = window(sides[1], k, v, heads, near0)
-    near1 = (to_next(pair), to_previous(pair))
+    up_core = move_core(upstream)
 
     def around(x):
         up, down = move_z(x, 1), move_z(x, 3)
-        return [x, up, down, move_z(up, 1)]
+        return [x, up, down]
+
+    w0 = around(out_weight)
+    w0[1] = hold(w0[1], up_core)
+    later = window(1, info, k, v, heads, w0[1:2])
+    pair = hold(later, *near0, *w0[1:])
+    near1 = (to_next(pair), to_previous(pair))
 
     cross = move_cross(out_weight)
-    w0 = around(out_weight)
-    place = jnp.stack([z, (z + 3) % NZ, (z + 1) % NZ, (z + 2) % NZ]).astype(jnp.int32)
-
-    middle = upstream.shape[1] // 2
-    up_core = move_core(upstream)
-    cross_first = move_cross(hold(upstream[:, :middle], cross))
-    cross_second = move_cross(hold(upstream[:, middle:], cross_first))
+    w0.append(move_z(w0[1], 1))
+
+    up_cross = move_cross(hold(upstream, cross))
 
     def back(w, before):
-        mine, theirs = project_back(place, w, upstream, up_core, before)
-        both = (mine.reshape(NZ, -1, rows), move_core(theirs).reshape(NZ, -1, rows))
-        both = jnp.where(c == 0, jnp.stack(both, axis=1), jnp.stack(both[::-1], axis=1))
-        return both.reshape(half, rows)
-
-    attn0, total0 = attend(infos[0], q, k, v, *near0, heads)
-    w1 = around(hold(cross, attn0))
+        mine, theirs = project_back(info, w, upstream, up_core, before)
+        return mine, move_core(theirs)
+
+    attn0, total0 = attend(0, info, q, k, v, *near0, heads)
     grad0 = back(w0, (attn0,))
-    attn1, total1 = attend(infos[1], q, k, v, *near1, heads, (grad0,))
+    w1 = around(hold(cross, pair))
+    attn1, total1 = attend(1, info, q, k, v, *near1, heads, (grad0[0], w1[1], w1[2]))
+    w1.append(move_z(w1[0], 2))
+    up_cross = hold(up_cross, attn1)
     dq, own0, to_left, to_right = attend_back(
-        infos[0], q, k, v, *near0, grad0, attn0, total0, heads, (attn1,), False
+        0, info, q, k, v, *near0, grad0, attn0, total0, heads, (attn1,), False
     )
     sent0 = (to_next(to_right), to_previous(to_left))
 
@@ -481,31 +548,22 @@
     grad1 = back(w1, (own0,))
     core_far = move_core(core_part)
     dq, own1, to_left, to_right = attend_back(
-        infos[1], q, k, v, *near1, grad1, attn1, total1, heads, (dq, core_far), True
+        1, info, q, k, v, *near1, grad1, attn1, total1, heads, (dq, core_far), True
     )
     sent1 = (to_next(to_right), to_previous(to_left))
-    z_place = jnp.stack([(z + i) % NZ for i in range(NZ)]).astype(jnp.int32)
-    pieces = weight_grad(
-        z_place, a_list, upstream, up_core, (cross_first, move_core(cross_first)),
-        (cross_second, move_core(cross_second)), (own1,) + sent0,
-    )
-    theirs = project(place, a_list[1], core_far, w0 + w1, (), pieces[:1])
-    sent = tuple(move_core(t) for t in theirs)
-    (mixed,) = project(place, a_list[0], own_part, w0 + w1, sent)
-    done = join(infos[0], own0, *sent0, heads, cols, None)
-    done = join(infos[1], own1, *sent1, heads, cols, done)
-
-    sums = add(hold(pieces[0], *done), *[move_z(pieces[i], i) for i in (1, 3, 2)])
-    quarter = sums.shape[1] // NY
-
-    def column(i):
-        return lax.dynamic_slice_in_dim(sums, ((y + i) % NY) * quarter, quarter, axis=1)
-
-    mine = add(column(0), *[move_y(column(i).astype(BF), i) for i in (1, 3, 2)]).astype(BF)
-    mine = hold(mine, mixed)
+    u_list = [upstream, up_core, up_cross, move_core(up_cross)]
+    pieces = weight_grad(info, a_list, u_list, (own1,) + sent0)
+    turned = [a_list[0], own_part, a_list[1], core_far]
+    near, *far = project(info, turned, w0 + w1, pieces[:1])
+    mixed = meet(near, *[move_core(t) for t in far])
+    done = join(0, info, own0, *sent0, heads, cols, None)
+    done = join(1, info, own1, *sent1, heads, cols, done)
+
+    columns = sum_columns(info, (pieces[0],) + tuple(move_z(pieces[i], i) for i in (1, 3, 2)), done)
+    mine = add(columns[0], *[move_y(columns[i], i) for i in (1, 3, 2)]).astype(BF)
     mine = add(mine, move_lo(mine)).astype(BF)
-    spots = jnp.stack([(y - i) % NY for i in (0, 1, 3, 2)]).astype(jnp.int32)
-    grad_weight = place_columns(spots, mine, *[move_y(mine, i) for i in (1, 3, 2)])
+    gathered = [mine] + [move_y(mine, i) for i in (1, 3, 2)]
+    grad_weight = place_columns(info, gathered, (mixed,))
     dk, dv = done
     return (mixed[None], dq[None], dk[None], dv[None], grad_weight)
 

time: 245 us -> 224 us (0.914)
  waiting for transfers between devices: 74.2 us -> 39.8 us
  starting transfers between devices: 49.9 us -> 73.7 us
  local copies, waits for them, and re-layouts: 22.8 us -> 9.55 us
  Pallas kernels: 85.8 us -> 97.6 us
  other arithmetic: 8.08 us -> 1.07 us
    ppermute x30 -> x28, waiting for transfers between devices: 62.5 us -> 27.3 us  [move(): return lax.ppermute(x, ('dp', 'space'), moves(change))]
    ppermute x30 -> x28, starting transfers between devices: 30.8 us -> 51 us  [move(): return lax.ppermute(x, ('dp', 'space'), moves(change))]
    pallas_call x8 -> x9, Pallas kernels: 54.8 us -> 65.1 us  [the longest x2 26.1 us: attend_back(): pl.pallas_call(functools.partial(backward_kernel, per, part), out_shape=(...]
    unnamed x90 -> x58, local copies, waits for them, and re-layouts: 16.8 us -> 7.94 us
    ppermute x4, starting transfers between devices: 13.7 us -> 17.5 us  [to_next(): return lax.ppermute(x, 'space', [(i, i + 1) for i in range(NS - 1)])]
    slice x1 -> x0, local copies, waits for them, and re-layouts: 3.18 us -> none  [on_device(): cross_second = move_cross(hold(upstream[:, middle:], cross_first))]
  transfers between devices with their start and end apart: 38 -> 36, of which waited for: 18 -> 14; matrix products, arithmetic and copies ran while one was open for 5% -> 2% of each run, Pallas kernels for 31% -> 43%
where the time goes in v3:
time: 224 us; the launch traced here: 223 us
  Pallas kernels  97.6 us (44%)
  starting transfers between devices  73.7 us (33%)
  waiting for transfers between devices  39.8 us (18%)
  local copies, waits for them, and re-layouts  9.55 us (4%)
    ppermute x28, starting transfers between devices, move(): return lax.ppermute(x, ('dp', 'space'), moves(change))  51 us
    ppermute x28, waiting for transfers between devices, move(): return lax.ppermute(x, ('dp', 'space'), moves(change))  27.3 us
    pallas_call x2, Pallas kernels, attend_back(): pl.pallas_call(functools.partial(backward_kernel, per, part), out_shape=(...  26.1 us
    ppermute x4, starting transfers between devices, to_next(): return lax.ppermute(x, 'space', [(i, i + 1) for i in range(NS - 1)])  17.5 us
    pallas_call x2, Pallas kernels, attend(): pl.pallas_call(functools.partial(forward_kernel, per, part), out_shape=(j...  16.4 us
    pallas_call x2, Pallas kernels, project_back(): pl.pallas_call(project_back_kernel, out_shape=(jax.ShapeDtypeStruct((NZ *...  13.1 us
    ppermute x4, waiting for transfers between devices, to_previous(): return lax.ppermute(x, 'space', [(i + 1, i) for i in range(NS - 1)])  9.94 us
    pallas_call x1, Pallas kernels, weight_grad(): pl.pallas_call(weight_grad_kernel, out_shape=(jax.ShapeDtypeStruct((sub,...  9.85 us
  transfers between devices with their start and end apart: 36, of which 14 were waited for; matrix products, arithmetic and copies ran while one was open for 2% of the time, Pallas kernels for 43%

profile of v3, /device:TPU:0, one launch (start us, length us, event | category | flops | bytes accessed | tf_op | source)
XLA Modules:
  0.0 222.8 jit_solution(13218088450154010980)
XLA Ops:
  0.7 2.9 %collective-permute-start.8 = (bf16[96,3072]{1,0:T(8,128)(2,1)}, bf16[96,3072]{1,0:T(8,128)(2,1)}, u32[]{:S(2)}, u32[]{:S(2)}) collective-permute-start(bf16[96,3072]{1,0:T(8,128)(2,1)} %refs_4_.1), channel_id=1, source_target_pairs={{0,68},{1,69},{2,70},{3,71},{4,64},{5,65},{6,66},{7,67},{8,76},{9,... | collective-permute-start | bytes 1769480 | tf_op jit(solution)/shard_map/ppermute | solution.py:42
  3.6 1.9 collective-permute-start.2
  5.6 0.8 copy.24
  6.4 0.7 concatenate.3.info.place.spots
  7.1 3.1 %window.2 = bf16[2,384,768]{2,1,0:T(8,128)(2,1)} custom-call(s32[44]{0:T(128)} %concatenate.3.info.place.spots, bf16[384,1536]{1,0:T(8,128)(2,1)} %bitcast.34, bf16[384,1536]{1,0:T(8,128)(2,1)} %bitcast.40), custom_call_target="tpu_custom_call" | custom-call | flops 1000 | bytes 1000 | tf_op jit(solution)/shard_map/window/pallas_call | solution.py:300
  10.1 1.3 collective-permute-start.1
  11.4 5.7 %collective-permute-start = (bf16[2,384,768]{2,1,0:T(8,128)(2,1)}, bf16[2,384,768]{2,1,0:T(8,128)(2,1)}, u32[]{:S(2)}, u32[]{:S(2)}) collective-permute-start(bf16[2,384,768]{2,1,0:T(8,128)(2,1)} %window.2), channel_id=1, source_target_pairs={{0,1},{1,2},{2,3},{3,4},{4,5},{5,6},{6,7},{8,9},{9,10},{10,11},{11... | collective-permute-start | bytes 3538952 | tf_op jit(solution)/shard_map/ppermute | solution.py:78
  17.1 1.4 copy.36.x_ref
  18.5 2.3 %collective-permute-start.16 = (bf16[384,3072]{1,0:T(8,128)(2,1)}, bf16[384,3072]{1,0:T(8,128)(2,1)}, u32[]{:S(2)}, u32[]{:S(2)}) collective-permute-start(bf16[384,3072]{1,0:T(8,128)(2,1)} %hold.8), channel_id=1, source_target_pairs={{0,68},{1,69},{2,70},{3,71},{4,64},{5,65},{6,66},{7,67},{8,76},{9,... | collective-permute-start | bytes 7077896 | tf_op jit(solution)/shard_map/ppermute | solution.py:42
  20.8 0.7 collective-permute-done.2.x_ref
  21.6 3.4 %collective-permute-start.4 = (bf16[96,3072]{1,0:T(8,128)(2,1)S(1)}, bf16[96,3072]{1,0:T(8,128)(2,1)S(1)}, u32[]{:S(2)}, u32[]{:S(2)}) collective-permute-start(bf16[96,3072]{1,0:T(8,128)(2,1)S(1)} %copy-done.12), channel_id=1, source_target_pairs={{0,48},{1,49},{2,50},{3,51},{4,52},{5,53},{6,54},{7,55},{8,56},{9,... | collective-permute-start | bytes 1769480 | tf_op jit(solution)/shard_map/ppermute | solution.py:42
  25.0 2.9 %window.3.x_ref = bf16[2,384,768]{2,1,0:T(8,128)(2,1)} custom-call(s32[44]{0:T(128)} %concatenate.3.info.place.spots, bf16[384,1536]{1,0:T(8,128)(2,1)} %bitcast.35, bf16[384,1536]{1,0:T(8,128)(2,1)} %bitcast.41, bf16[96,3072]{1,0:T(8,128)(2,1)} %hold.5.rest_0_.rest_2_.refs_1_.refs_5_), custom_call_target="tpu_custom_call" | custom-call | flops 1000 | bytes 1000 | tf_op jit(solution)/shard_map/window/pallas_call | solution.py:300
  27.9 9.1 %collective-permute-done.4.rest_3_.refs_2_.refs_6_ = bf16[96,3072]{1,0:T(8,128)(2,1)S(1)} collective-permute-done((bf16[96,3072]{1,0:T(8,128)(2,1)S(1)}, bf16[96,3072]{1,0:T(8,128)(2,1)S(1)}, u32[]{:S(2)}, u32[]{:S(2)}) %collective-permute-start.4) | collective-permute-done | bytes 589856 | tf_op jit(solution)/shard_map/ppermute | solution.py:42
  37.1 2.9 %collective-permute-done.1.right_ref.rest_1_ = bf16[2,384,768]{2,1,0:T(8,128)(2,1)S(1)} collective-permute-done((bf16[2,384,768]{2,1,0:T(8,128)(2,1)}, bf16[2,384,768]{2,1,0:T(8,128)(2,1)S(1)}, u32[]{:S(2)}, u32[]{:S(2)}) %collective-permute-start.1) | collective-permute-done | bytes 1179680 | tf_op jit(solution)/shard_map/ppermute | solution.py:82
  40.0 1.3 collective-permute-done.left_ref.rest_0_
  41.3 1.3 collective-permute-start.6
  42.6 6.1 %collective-permute-start.5 = (bf16[2,384,768]{2,1,0:T(8,128)(2,1)}, bf16[2,384,768]{2,1,0:T(8,128)(2,1)}, u32[]{:S(2)}, u32[]{:S(2)}) collective-permute-start(bf16[2,384,768]{2,1,0:T(8,128)(2,1)} %hold.6.rest_0_), channel_id=1, source_target_pairs={{0,1},{1,2},{2,3},{3,4},{4,5},{5,6},{6,7},{8,9},{9,10},{10,11},{11... | collective-permute-start | bytes 3538952 | tf_op jit(solution)/shard_map/ppermute | solution.py:78
  48.6 2.4 %collective-permute-start.10 = (bf16[96,3072]{1,0:T(8,128)(2,1)}, bf16[96,3072]{1,0:T(8,128)(2,1)S(1)}, u32[]{:S(2)}, u32[]{:S(2)}) collective-permute-start(bf16[96,3072]{1,0:T(8,128)(2,1)} %hold.7.refs_0_.refs_8_), channel_id=1, source_target_pairs={{0,48},{1,49},{2,50},{3,51},{4,52},{5,53},{6,54},{7,55},{8,56},{9,... | collective-permute-start | bytes 1769480 | tf_op jit(solution)/shard_map/ppermute | solution.py:42
  51.0 8.2 %attend.2 = (bf16[768,384]{1,0:T(8,128)(2,1)}, f32[6,1,384]{2,1,0:T(1,128)}) custom-call(s32[44]{0:T(128)} %concatenate.3.info.place.spots, bf16[384,1536]{1,0:T(8,128)(2,1)} %bitcast.51, bf16[384,1536]{1,0:T(8,128)(2,1)} %bitcast.36, bf16[384,1536]{1,0:T(8,128)(2,1)} %bitcast.42, bf16[2,384,768]{2,1,0:T(8,128)(2,1)} %collective-permute-done.left_ref.rest_0_, ...), custom_call_target="tpu_custom_call" | custom-call | flops 1000 | bytes 1000 | tf_op jit(solution)/shard_map/attend/pallas_call | solution.py:151
  59.2 6.6 %project_back.2 = (bf16[384,384]{1,0:T(8,128)(2,1)}, bf16[384,384]{1,0:T(8,128)(2,1)}) custom-call(s32[44]{0:T(128)} %concatenate.3.info.place.spots, bf16[96,3072]{1,0:T(8,128)(2,1)} %refs_4_.1, bf16[96,3072]{1,0:T(8,128)(2,1)} %hold.5.rest_0_.rest_2_.refs_1_.refs_5_, bf16[96,3072]{1,0:T(8,128)(2,1)} %copy-done.6, ...), custom_call_target="tpu_custom_call" | custom-call | flops 1000 | bytes 1000 | tf_op jit(solution)/shard_map/project_back/pallas_call | solution.py:327
  66.1 4.5 %collective-permute-done.6.right_ref = bf16[2,384,768]{2,1,0:T(8,128)(2,1)S(1)} collective-permute-done((bf16[2,384,768]{2,1,0:T(8,128)(2,1)}, bf16[2,384,768]{2,1,0:T(8,128)(2,1)S(1)}, u32[]{:S(2)}, u32[]{:S(2)}) %collective-permute-start.6) | collective-permute-done | bytes 1179680 | tf_op jit(solution)/shard_map/ppermute | solution.py:82
  70.7 1.3 collective-permute-done.5.left_ref
  72.0 8.2 %attend.3 = (bf16[768,384]{1,0:T(8,128)(2,1)}, f32[6,1,384]{2,1,0:T(1,128)}) custom-call(s32[44]{0:T(128)} %concatenate.3.info.place.spots, bf16[384,1536]{1,0:T(8,128)(2,1)} %bitcast.52, bf16[384,1536]{1,0:T(8,128)(2,1)} %bitcast.37, bf16[384,1536]{1,0:T(8,128)(2,1)} %bitcast.43, bf16[2,384,768]{2,1,0:T(8,128)(2,1)} %collective-permute-done.5.left_ref, ...), custom_call_target="tpu_custom_call" | custom-call | flops 1000 | bytes 1000 | tf_op jit(solution)/shard_map/attend/pallas_call | solution.py:151
  80.3 3.7 %collective-permute-start.13 = (bf16[96,3072]{1,0:T(8,128)(2,1)}, bf16[96,3072]{1,0:T(8,128)(2,1)S(1)}, u32[]{:S(2)}, u32[]{:S(2)}) collective-permute-start(bf16[96,3072]{1,0:T(8,128)(2,1)} %hold.7.refs_0_.refs_8_), channel_id=1, source_target_pairs={{0,32},{1,33},{2,34},{3,35},{4,36},{5,37},{6,38},{7,39},{8,40},{9,... | collective-permute-start | bytes 1769480 | tf_op jit(solution)/shard_map/ppermute | solution.py:42
  84.1 0.8 constant_dynamic-slice_fusion.1
  84.9 0.4 collective-permute-start.11
  85.4 0.4 collective-permute-start.12
  85.8 0.7 copy-done.22
  86.5 13.1 %attend_back.2 = (bf16[384,1536]{1,0:T(8,128)(2,1)}, bf16[2,384,768]{2,1,0:T(8,128)(2,1)}, bf16[2,384,768]{2,1,0:T(8,128)(2,1)}, bf16[2,384,768]{2,1,0:T(8,128)(2,1)}) custom-call(s32[44]{0:T(128)} %concatenate.3.info.place.spots, bf16[384,1536]{1,0:T(8,128)(2,1)} %bitcast.53, bf16[384,1536]{1,0:T(8,128)(2,1)} %bitcast.38, bf16[384,1536]{1,0:T(8,128)(2,1)} %bitcast.44, ...), custom_call_target="tpu_custom_call" | custom-call | flops 1000 | bytes 1000 | tf_op jit(solution)/shard_map/attend_back/pallas_call | solution.py:214
  99.6 0.8 copy-done.11
  100.4 6.6 %project_back.3 = (bf16[384,384]{1,0:T(8,128)(2,1)}, bf16[384,384]{1,0:T(8,128)(2,1)}) custom-call(s32[44]{0:T(128)} %concatenate.3.info.place.spots, bf16[96,3072]{1,0:T(8,128)(2,1)} %hold.7.refs_0_.refs_8_, bf16[96,3072]{1,0:T(8,128)(2,1)} %copy-done.5, bf16[96,3072]{1,0:T(8,128)(2,1)} %copy-done.4, bf16[96,3072]{1,0:T(8,128)(2,1)} %copy-done.11, ...), custom_call_target="tpu_custom_call" | custom-call | flops 1000 | bytes 1000 | tf_op jit(solution)/shard_map/project_back/pallas_call | solution.py:327
  107.4 4.5 %collective-permute-start.20 = (bf16[2,384,768]{2,1,0:T(8,128)(2,1)}, bf16[2,384,768]{2,1,0:T(8,128)(2,1)S(1)}, u32[]{:S(2)}, u32[]{:S(2)}) collective-permute-start(bf16[2,384,768]{2,1,0:T(8,128)(2,1)} %get-tuple-element.47), channel_id=1, source_target_pairs={{0,1},{1,2},{2,3},{3,4},{4,5},{5,6},{6,7},{8,9},{9,10},{10,11},{11... | collective-permute-start | bytes 3538952 | tf_op jit(solution)/shard_map/ppermute | solution.py:78
  111.8 1.3 collective-permute-start.21
  113.2 10.8 %collective-permute-start.14 = (bf16[384,384]{1,0:T(8,128)(2,1)S(1)}, bf16[384,384]{1,0:T(8,128)(2,1)S(1)}, u32[]{:S(2)}, u32[]{:S(2)}) collective-permute-start(bf16[384,384]{1,0:T(8,128)(2,1)S(1)} %bitcast.62), channel_id=1, source_target_pairs={{0,68},{1,69},{2,70},{3,71},{4,64},{5,65},{6,66},{7,67},{8,76},{9,... | collective-permute-start | bytes 884744 | tf_op jit(solution)/shard_map/ppermute | solution.py:42
  124.0 0.7 copy-done.23
  124.7 13.1 %attend_back.3 = (bf16[384,1536]{1,0:T(8,128)(2,1)}, bf16[2,384,768]{2,1,0:T(8,128)(2,1)}, bf16[2,384,768]{2,1,0:T(8,128)(2,1)}, bf16[2,384,768]{2,1,0:T(8,128)(2,1)}) custom-call(s32[44]{0:T(128)} %concatenate.3.info.place.spots, bf16[384,1536]{1,0:T(8,128)(2,1)} %bitcast.54, bf16[384,1536]{1,0:T(8,128)(2,1)} %bitcast.39, ...), custom_call_target="tpu_custom_call", output_to_operand_aliasing={{0}: (10, {})} | custom-call | flops 1000 | bytes 1000 | tf_op jit(solution)/shard_map/attend_back/pallas_call | solution.py:214
  137.8 1.4 collective-permute-start.24
  139.1 1.3 collective-permute-start.25
  140.5 1.2 collective-permute-done.21.refs_10_.b_ref
  141.7 1.0 copy-done.9
  142.7 9.9 %weight_grad.1 = (bf16[96,3072]{1,0:T(8,128)(2,1)}, bf16[96,3072]{1,0:T(8,128)(2,1)}, bf16[96,3072]{1,0:T(8,128)(2,1)}, bf16[96,3072]{1,0:T(8,128)(2,1)}) custom-call(s32[44]{0:T(128)} %concatenate.3.info.place.spots, bf16[384,384]{1,0:T(8,128)(2,1)} %bitcast.60, bf16[384,384]{1,0:T(8,128)(2,1)} %copy-done.13, bf16[384,384]{1,0:T(8,128)(2,1)} %copy-done.21, ...), custom_call_target="tpu_custom_call" | custom-call | flops 1000 | bytes 1000 | tf_op jit(solution)/shard_map/weight_grad/pallas_call | solution.py:418
  152.6 2.1 collective-permute-start.26
  154.7 1.2 collective-permute-start.27
  155.9 2.1 collective-permute-start.28
  158.0 9.4 %project.1 = (bf16[384,3072]{1,0:T(8,128)(2,1)}, bf16[384,1536]{1,0:T(8,128)(2,1)}, bf16[384,1536]{1,0:T(8,128)(2,1)}) custom-call(s32[44]{0:T(128)} %concatenate.3.info.place.spots, bf16[384,384]{1,0:T(8,128)(2,1)} %bitcast.61, bf16[384,384]{1,0:T(8,128)(2,1)} %bitcast.63, bf16[384,384]{1,0:T(8,128)(2,1)} %copy-done.13, bf16[384,384]{1,0:T(8,128)(2,1)} %copy-done.14, ...), custom_call_target="tpu_custom_call" | custom-call | flops 1000 | bytes 1000 | tf_op jit(solution)/shard_map/project/pallas_call | solution.py:366
  167.5 1.2 collective-permute-done.25.b_ref
  168.7 3.6 %join.2 = (bf16[384,1536]{1,0:T(8,128)(2,1)}, bf16[384,1536]{1,0:T(8,128)(2,1)}) custom-call(s32[44]{0:T(128)} %concatenate.3.info.place.spots, bf16[2,384,768]{2,1,0:T(8,128)(2,1)} %get-tuple-element.41.refs_6_.own_ref, bf16[2,384,768]{2,1,0:T(8,128)(2,1)} %copy-done.8, bf16[2,384,768]{2,1,0:T(8,128)(2,1)} %copy-done.9), custom_call_target="tpu_custom_call" | custom-call | flops 1000 | bytes 1000 | tf_op jit(solution)/shard_map/join/pallas_call | solution.py:251
  172.3 3.6 %join.3 = (bf16[384,1536]{1,0:T(8,128)(2,1)}, bf16[384,1536]{1,0:T(8,128)(2,1)}) custom-call(s32[44]{0:T(128)} %concatenate.3.info.place.spots, bf16[2,384,768]{2,1,0:T(8,128)(2,1)} %get-tuple-element.46.refs_8_.own_ref, bf16[2,384,768]{2,1,0:T(8,128)(2,1)} %copy-done.18, ...), custom_call_target="tpu_custom_call", output_to_operand_aliasing={{0}: (4, {}), {1}: (5, {})} | custom-call | flops 1000 | bytes 1000 | tf_op jit(solution)/shard_map/join/pallas_call | solution.py:251
  176.0 6.3 %collective-permute-done.28.refs_3_ = bf16[96,3072]{1,0:T(8,128)(2,1)} collective-permute-done((bf16[96,3072]{1,0:T(8,128)(2,1)}, bf16[96,3072]{1,0:T(8,128)(2,1)}, u32[]{:S(2)}, u32[]{:S(2)}) %collective-permute-start.28) | collective-permute-done | bytes 589856 | tf_op jit(solution)/shard_map/ppermute | solution.py:42
  182.3 2.6 %sum_columns.1 = (f32[96,768]{1,0:T(8,128)}, bf16[96,768]{1,0:T(8,128)(2,1)}, bf16[96,768]{1,0:T(8,128)(2,1)}, bf16[96,768]{1,0:T(8,128)(2,1)}) custom-call(s32[44]{0:T(128)} %concatenate.3.info.place.spots, bf16[96,3072]{1,0:T(8,128)(2,1)} %get-tuple-element.49.refs_12_.refs_0_, bf16[96,3072]{1,0:T(8,128)(2,1)} %copy-done.19, ...), custom_call_target="tpu_custom_call" | custom-call | flops 1000 | bytes 1000 | tf_op jit(solution)/shard_map/sum_columns/pallas_call | solution.py:447
  184.9 4.7 %collective-permute-start.29 = (bf16[96,768]{1,0:T(8,128)(2,1)}, bf16[96,768]{1,0:T(8,128)(2,1)S(1)}, u32[]{:S(2)}, u32[]{:S(2)}) collective-permute-start(bf16[96,768]{1,0:T(8,128)(2,1)} %get-tuple-element.64), channel_id=1, source_target_pairs={{0,1},{1,2},{2,3},{3,0},{4,5},{5,6},{6,7},{7,4},{8,9},{9,10},{10,1... | collective-permute-start | bytes 442376 | tf_op jit(solution)/shard_map/ppermute | solution.py:42
  189.6 6.7 %collective-permute-start.30 = (bf16[96,768]{1,0:T(8,128)(2,1)}, bf16[96,768]{1,0:T(8,128)(2,1)S(1)}, u32[]{:S(2)}, u32[]{:S(2)}) collective-permute-start(bf16[96,768]{1,0:T(8,128)(2,1)} %get-tuple-element.65), channel_id=1, source_target_pairs={{0,3},{1,0},{2,1},{3,2},{4,7},{5,4},{6,5},{7,6},{8,11},{9,8},{10,9... | collective-permute-start | bytes 442376 | tf_op jit(solution)/shard_map/ppermute | solution.py:42
  196.3 1.4 collective-permute-start.31
  197.8 3.2 %collective-permute-done.29 = bf16[96,768]{1,0:T(8,128)(2,1)S(1)} collective-permute-done((bf16[96,768]{1,0:T(8,128)(2,1)}, bf16[96,768]{1,0:T(8,128)(2,1)S(1)}, u32[]{:S(2)}, u32[]{:S(2)}) %collective-permute-start.29) | collective-permute-done | bytes 147488 | tf_op jit(solution)/shard_map/ppermute | solution.py:42
  201.0 2.2 %collective-permute-done.31 = bf16[96,768]{1,0:T(8,128)(2,1)S(1)} collective-permute-done((bf16[96,768]{1,0:T(8,128)(2,1)}, bf16[96,768]{1,0:T(8,128)(2,1)S(1)}, u32[]{:S(2)}, u32[]{:S(2)}) %collective-permute-start.31) | collective-permute-done | bytes 147488 | tf_op jit(solution)/shard_map/ppermute | solution.py:42
  203.2 1.0 add_convert_fusion.1
  204.5 5.0 %collective-permute-done.32 = bf16[96,768]{1,0:T(8,128)(2,1)S(1)} collective-permute-done((bf16[96,768]{1,0:T(8,128)(2,1)S(1)}, bf16[96,768]{1,0:T(8,128)(2,1)S(1)}, u32[]{:S(2)}, u32[]{:S(2)}) %collective-permute-start.32) | collective-permute-done | bytes 147488 | tf_op jit(solution)/shard_map/ppermute | solution.py:42
  209.5 1.5 collective-permute-start.35
  211.0 2.1 collective-permute-start.34
  213.2 1.0 copy-done.15
  214.2 0.4 copy-done.16
  214.6 4.6 %meet.1.refs_4_ = bf16[384,3072]{1,0:T(8,128)(2,1)} custom-call(bf16[384,3072]{1,0:T(8,128)(2,1)} %get-tuple-element.50.near_ref, bf16[384,1536]{1,0:T(8,128)(2,1)} %copy-done.15, bf16[384,1536]{1,0:T(8,128)(2,1)} %copy-done.16), custom_call_target="tpu_custom_call" | custom-call | flops 1000 | bytes 1000 | tf_op jit(solution)/shard_map/meet/pallas_call | solution.py:392
  219.9 0.6 copy-done.27
  220.5 2.2 place_columns.1
  (92 shorter events, 2.4 us)
Async XLA Ops:
  0.6 24.3 %collective-permute-start.3 = (bf16[384,3072]{1,0:T(8,128)(2,1)}, bf16[384,3072]{1,0:T(8,128)(2,1)}, u32[]{:S(2)}, u32[]{:S(2)}) collective-permute-start(bf16[384,3072]{1,0:T(8,128)(2,1)} %bitcast.46), channel_id=1, source_target_pairs={{0,8},{1,9},{2,10},{3,11},{4,12},{5,13},{6,14},{7,15},{8,0},{9,1},... | collective-permute-start | bytes 7077896 | tf_op jit(solution)/shard_map/ppermute | solution.py:42
  0.7 17.8 %collective-permute-start.8 = (bf16[96,3072]{1,0:T(8,128)(2,1)}, bf16[96,3072]{1,0:T(8,128)(2,1)}, u32[]{:S(2)}, u32[]{:S(2)}) collective-permute-start(bf16[96,3072]{1,0:T(8,128)(2,1)} %refs_4_.1), channel_id=1, source_target_pairs={{0,68},{1,69},{2,70},{3,71},{4,64},{5,65},{6,66},{7,67},{8,76},{9,... | collective-permute-start | bytes 1769480 | tf_op jit(solution)/shard_map/ppermute | solution.py:42
  3.6 17.9 %collective-permute-start.2 = (bf16[96,3072]{1,0:T(8,128)(2,1)}, bf16[96,3072]{1,0:T(8,128)(2,1)S(1)}, u32[]{:S(2)}, u32[]{:S(2)}) collective-permute-start(bf16[96,3072]{1,0:T(8,128)(2,1)} %refs_4_.1), channel_id=1, source_target_pairs={{0,16},{1,17},{2,18},{3,19},{4,20},{5,21},{6,22},{7,23},{8,24},{9,... | collective-permute-start | bytes 1769480 | tf_op jit(solution)/shard_map/ppermute | solution.py:42
  7.1 10.0 %copy-start = (bf16[1,384,3072]{2,1,0:T(8,128)(2,1)S(1)}, bf16[1,384,3072]{2,1,0:T(8,128)(2,1)}, u32[]{:S(2)}) copy-start(bf16[1,384,3072]{2,1,0:T(8,128)(2,1)} %param.10) | copy-start | bytes 7077892
  10.1 29.8 %collective-permute-start.1 = (bf16[2,384,768]{2,1,0:T(8,128)(2,1)}, bf16[2,384,768]{2,1,0:T(8,128)(2,1)S(1)}, u32[]{:S(2)}, u32[]{:S(2)}) collective-permute-start(bf16[2,384,768]{2,1,0:T(8,128)(2,1)} %window.2), channel_id=1, source_target_pairs={{1,0},{2,1},{3,2},{4,3},{5,4},{6,5},{7,6},{9,8},{10,9},{11,10},{12... | collective-permute-start | bytes 3538952 | tf_op jit(solution)/shard_map/ppermute | solution.py:82
  11.4 29.8 %collective-permute-start = (bf16[2,384,768]{2,1,0:T(8,128)(2,1)}, bf16[2,384,768]{2,1,0:T(8,128)(2,1)}, u32[]{:S(2)}, u32[]{:S(2)}) collective-permute-start(bf16[2,384,768]{2,1,0:T(8,128)(2,1)} %window.2), channel_id=1, source_target_pairs={{0,1},{1,2},{2,3},{3,4},{4,5},{5,6},{6,7},{8,9},{9,10},{10,11},{11... | collective-permute-start | bytes 3538952 | tf_op jit(solution)/shard_map/ppermute | solution.py:78
  18.5 3.1 %copy-start.12 = (bf16[96,3072]{1,0:T(8,128)(2,1)S(1)}, bf16[96,3072]{1,0:T(8,128)(2,1)}, u32[]{:S(2)}) copy-start(bf16[96,3072]{1,0:T(8,128)(2,1)} %refs_4_.1) | copy-start | bytes 1769476
  18.5 61.6 %collective-permute-start.16 = (bf16[384,3072]{1,0:T(8,128)(2,1)}, bf16[384,3072]{1,0:T(8,128)(2,1)}, u32[]{:S(2)}, u32[]{:S(2)}) collective-permute-start(bf16[384,3072]{1,0:T(8,128)(2,1)} %hold.8), channel_id=1, source_target_pairs={{0,68},{1,69},{2,70},{3,71},{4,64},{5,65},{6,66},{7,67},{8,76},{9,... | collective-permute-start | bytes 7077896 | tf_op jit(solution)/shard_map/ppermute | solution.py:42
  21.6 3.4 %copy-start.1 = (bf16[96,3072]{1,0:T(8,128)(2,1)}, bf16[96,3072]{1,0:T(8,128)(2,1)S(1)}, u32[]{:S(2)}) copy-start(bf16[96,3072]{1,0:T(8,128)(2,1)S(1)} %collective-permute-done.2.x_ref) | copy-start | bytes 1769476
  21.6 15.5 %collective-permute-start.4 = (bf16[96,3072]{1,0:T(8,128)(2,1)S(1)}, bf16[96,3072]{1,0:T(8,128)(2,1)S(1)}, u32[]{:S(2)}, u32[]{:S(2)}) collective-permute-start(bf16[96,3072]{1,0:T(8,128)(2,1)S(1)} %copy-done.12), channel_id=1, source_target_pairs={{0,48},{1,49},{2,50},{3,51},{4,52},{5,53},{6,54},{7,55},{8,56},{9,... | collective-permute-start | bytes 1769480 | tf_op jit(solution)/shard_map/ppermute | solution.py:42
  25.0 26.1 %collective-permute-start.7 = (bf16[96,3072]{1,0:T(8,128)(2,1)}, bf16[96,3072]{1,0:T(8,128)(2,1)}, u32[]{:S(2)}, u32[]{:S(2)}) collective-permute-start(bf16[96,3072]{1,0:T(8,128)(2,1)} %hold.5.rest_0_.rest_2_.refs_1_.refs_5_), channel_id=1, source_target_pairs={{0,16},{1,17},{2,18},{3,19},{4,20},{5,21},{6,22},{7,23},{8,24},{9,... | collective-permute-start | bytes 1769480 | tf_op jit(solution)/shard_map/ppermute | solution.py:42
  37.1 4.2 %copy-start.6 = (bf16[96,3072]{1,0:T(8,128)(2,1)}, bf16[96,3072]{1,0:T(8,128)(2,1)S(1)}, u32[]{:S(2)}) copy-start(bf16[96,3072]{1,0:T(8,128)(2,1)S(1)} %collective-permute-done.4.rest_3_.refs_2_.refs_6_) | copy-start | bytes 1769476
  40.0 1.3 copy-start.2
  41.3 29.4 %collective-permute-start.6 = (bf16[2,384,768]{2,1,0:T(8,128)(2,1)}, bf16[2,384,768]{2,1,0:T(8,128)(2,1)S(1)}, u32[]{:S(2)}, u32[]{:S(2)}) collective-permute-start(bf16[2,384,768]{2,1,0:T(8,128)(2,1)} %hold.6.rest_0_), channel_id=1, source_target_pairs={{1,0},{2,1},{3,2},{4,3},{5,4},{6,5},{7,6},{9,8},{10,9},{11,10},{12... | collective-permute-start | bytes 3538952 | tf_op jit(solution)/shard_map/ppermute | solution.py:82
  42.6 29.4 %collective-permute-start.5 = (bf16[2,384,768]{2,1,0:T(8,128)(2,1)}, bf16[2,384,768]{2,1,0:T(8,128)(2,1)}, u32[]{:S(2)}, u32[]{:S(2)}) collective-permute-start(bf16[2,384,768]{2,1,0:T(8,128)(2,1)} %hold.6.rest_0_), channel_id=1, source_target_pairs={{0,1},{1,2},{2,3},{3,4},{4,5},{5,6},{6,7},{8,9},{9,10},{10,11},{11... | collective-permute-start | bytes 3538952 | tf_op jit(solution)/shard_map/ppermute | solution.py:78
  48.6 17.2 %collective-permute-start.10 = (bf16[96,3072]{1,0:T(8,128)(2,1)}, bf16[96,3072]{1,0:T(8,128)(2,1)S(1)}, u32[]{:S(2)}, u32[]{:S(2)}) collective-permute-start(bf16[96,3072]{1,0:T(8,128)(2,1)} %hold.7.refs_0_.refs_8_), channel_id=1, source_target_pairs={{0,48},{1,49},{2,50},{3,51},{4,52},{5,53},{6,54},{7,55},{8,56},{9,... | collective-permute-start | bytes 1769480 | tf_op jit(solution)/shard_map/ppermute | solution.py:42
  51.0 15.1 %collective-permute-start.9 = (bf16[96,3072]{1,0:T(8,128)(2,1)}, bf16[96,3072]{1,0:T(8,128)(2,1)S(1)}, u32[]{:S(2)}, u32[]{:S(2)}) collective-permute-start(bf16[96,3072]{1,0:T(8,128)(2,1)} %hold.7.refs_0_.refs_8_), channel_id=1, source_target_pairs={{0,16},{1,17},{2,18},{3,19},{4,20},{5,21},{6,22},{7,23},{8,24},{9,... | collective-permute-start | bytes 1769480 | tf_op jit(solution)/shard_map/ppermute | solution.py:42
  65.8 6.2 %copy-start.4 = (bf16[96,3072]{1,0:T(8,128)(2,1)}, bf16[96,3072]{1,0:T(8,128)(2,1)S(1)}, u32[]{:S(2)}) copy-start(bf16[96,3072]{1,0:T(8,128)(2,1)S(1)} %collective-permute-done.10.rest_2_.refs_2_.refs_10_) | copy-start | bytes 1769476
  66.1 5.8 %copy-start.5 = (bf16[96,3072]{1,0:T(8,128)(2,1)}, bf16[96,3072]{1,0:T(8,128)(2,1)S(1)}, u32[]{:S(2)}) copy-start(bf16[96,3072]{1,0:T(8,128)(2,1)S(1)} %collective-permute-done.9.rest_1_.refs_1_.refs_9_) | copy-start | bytes 1769476
  70.7 1.3 copy-start.10
  80.2 3.9 %copy-start.7 = (bf16[768,384]{1,0:T(8,128)(2,1)S(1)}, bf16[768,384]{1,0:T(8,128)(2,1)}, u32[]{:S(2)}) copy-start(bf16[768,384]{1,0:T(8,128)(2,1)} %get-tuple-element.36.refs_6_.attn_ref) | copy-start | bytes 1769476
  80.2 5.1 %copy-start.3 = (bf16[768,384]{1,0:T(8,128)(2,1)S(1)}, bf16[768,384]{1,0:T(8,128)(2,1)}, u32[]{:S(2)}) copy-start(bf16[768,384]{1,0:T(8,128)(2,1)} %get-tuple-element.38.rest_0_.attn_ref) | copy-start | bytes 1769476
  80.2 61.5 %collective-permute-start.17 = (bf16[384,3072]{1,0:T(8,128)(2,1)}, bf16[384,3072]{1,0:T(8,128)(2,1)}, u32[]{:S(2)}, u32[]{:S(2)}) collective-permute-start(bf16[384,3072]{1,0:T(8,128)(2,1)} %hold.9.refs_6_), channel_id=1, source_target_pairs={{0,8},{1,9},{2,10},{3,11},{4,12},{5,13},{6,14},{7,15},{8,0},{9,1},... | collective-permute-start | bytes 7077896 | tf_op jit(solution)/shard_map/ppermute | solution.py:42
  80.3 19.3 %collective-permute-start.13 = (bf16[96,3072]{1,0:T(8,128)(2,1)}, bf16[96,3072]{1,0:T(8,128)(2,1)S(1)}, u32[]{:S(2)}, u32[]{:S(2)}) collective-permute-start(bf16[96,3072]{1,0:T(8,128)(2,1)} %hold.7.refs_0_.refs_8_), channel_id=1, source_target_pairs={{0,32},{1,33},{2,34},{3,35},{4,36},{5,37},{6,38},{7,39},{8,40},{9,... | collective-permute-start | bytes 1769480 | tf_op jit(solution)/shard_map/ppermute | solution.py:42
  83.9 1.8 collective-permute-start.18
  84.9 26.9 %collective-permute-start.11 = (bf16[384,384]{1,0:T(8,128)(2,1)S(1)}, bf16[384,384]{1,0:T(8,128)(2,1)S(1)}, u32[]{:S(2)}, u32[]{:S(2)}) collective-permute-start(bf16[384,384]{1,0:T(8,128)(2,1)S(1)} %bitcast.67), channel_id=1, source_target_pairs={{0,8},{1,9},{2,10},{3,11},{4,12},{5,13},{6,14},{7,15},{8,0},{9,1},... | collective-permute-start | bytes 884744 | tf_op jit(solution)/shard_map/ppermute | solution.py:42
  85.4 14.2 %copy-start.24 = (bf16[4,1,96,384]{3,2,1,0:T(8,128)(2,1)}, bf16[4,1,96,384]{3,2,1,0:T(8,128)(2,1)S(1)}, u32[]{:S(2)}) copy-start(bf16[4,1,96,384]{3,2,1,0:T(8,128)(2,1)S(1)} %get-tuple-element.67) | copy-start | bytes 884740
  85.4 27.8 %copy-start.17 = (bf16[4,1,96,384]{3,2,1,0:T(8,128)(2,1)}, bf16[4,1,96,384]{3,2,1,0:T(8,128)(2,1)S(1)}, u32[]{:S(2)}) copy-start(bf16[4,1,96,384]{3,2,1,0:T(8,128)(2,1)S(1)} %get-tuple-element.68) | copy-start | bytes 884740
  85.4 27.8 %collective-permute-start.12 = (bf16[384,384]{1,0:T(8,128)(2,1)S(1)}, bf16[384,384]{1,0:T(8,128)(2,1)S(1)}, u32[]{:S(2)}, u32[]{:S(2)}) collective-permute-start(bf16[384,384]{1,0:T(8,128)(2,1)S(1)} %bitcast.65), channel_id=1, source_target_pairs={{0,8},{1,9},{2,10},{3,11},{4,12},{5,13},{6,14},{7,15},{8,0},{9,1},... | collective-permute-start | bytes 884744 | tf_op jit(solution)/shard_map/ppermute | solution.py:42
  85.8 0.7 copy-start.22
  99.6 0.8 copy-start.11
  107.0 16.9 %collective-permute-start.19 = (bf16[384,384]{1,0:T(8,128)(2,1)}, bf16[384,384]{1,0:T(8,128)(2,1)S(1)}, u32[]{:S(2)}, u32[]{:S(2)}) collective-permute-start(bf16[384,384]{1,0:T(8,128)(2,1)} %get-tuple-element.43), channel_id=1, source_target_pairs={{0,8},{1,9},{2,10},{3,11},{4,12},{5,13},{6,14},{7,15},{8,0},{9,1},... | collective-permute-start | bytes 884744 | tf_op jit(solution)/shard_map/ppermute | solution.py:42
  107.4 33.1 %collective-permute-start.20 = (bf16[2,384,768]{2,1,0:T(8,128)(2,1)}, bf16[2,384,768]{2,1,0:T(8,128)(2,1)S(1)}, u32[]{:S(2)}, u32[]{:S(2)}) collective-permute-start(bf16[2,384,768]{2,1,0:T(8,128)(2,1)} %get-tuple-element.47), channel_id=1, source_target_pairs={{0,1},{1,2},{2,3},{3,4},{4,5},{5,6},{6,7},{8,9},{9,10},{10,11},{11... | collective-permute-start | bytes 3538952 | tf_op jit(solution)/shard_map/ppermute | solution.py:78
  111.8 25.9 %copy-start.13 = (bf16[384,384]{1,0:T(8,128)(2,1)}, bf16[384,384]{1,0:T(8,128)(2,1)S(1)}, u32[]{:S(2)}) copy-start(bf16[384,384]{1,0:T(8,128)(2,1)S(1)} %collective-permute-done.11.refs_1_.refs_2_) | copy-start | bytes 884740
  111.8 29.8 %collective-permute-start.21 = (bf16[2,384,768]{2,1,0:T(8,128)(2,1)}, bf16[2,384,768]{2,1,0:T(8,128)(2,1)S(1)}, u32[]{:S(2)}, u32[]{:S(2)}) collective-permute-start(bf16[2,384,768]{2,1,0:T(8,128)(2,1)} %get-tuple-element.48), channel_id=1, source_target_pairs={{1,0},{2,1},{3,2},{4,3},{5,4},{6,5},{7,6},{9,8},{10,9},{11,10},{12... | collective-permute-start | bytes 3538952 | tf_op jit(solution)/shard_map/ppermute | solution.py:82
  113.1 10.8 %copy-start.14 = (bf16[384,384]{1,0:T(8,128)(2,1)}, bf16[384,384]{1,0:T(8,128)(2,1)S(1)}, u32[]{:S(2)}) copy-start(bf16[384,384]{1,0:T(8,128)(2,1)S(1)} %collective-permute-done.12.rest_1_.refs_3_) | copy-start | bytes 884740
  113.2 24.6 %collective-permute-start.14 = (bf16[384,384]{1,0:T(8,128)(2,1)S(1)}, bf16[384,384]{1,0:T(8,128)(2,1)S(1)}, u32[]{:S(2)}, u32[]{:S(2)}) collective-permute-start(bf16[384,384]{1,0:T(8,128)(2,1)S(1)} %bitcast.62), channel_id=1, source_target_pairs={{0,68},{1,69},{2,70},{3,71},{4,64},{5,65},{6,66},{7,67},{8,76},{9,... | collective-permute-start | bytes 884744 | tf_op jit(solution)/shard_map/ppermute | solution.py:42
  123.9 0.7 copy-start.23
  123.9 15.2 %collective-permute-start.15 = (bf16[384,384]{1,0:T(8,128)(2,1)}, bf16[384,384]{1,0:T(8,128)(2,1)}, u32[]{:S(2)}, u32[]{:S(2)}) collective-permute-start(bf16[384,384]{1,0:T(8,128)(2,1)} %bitcast.66), channel_id=1, source_target_pairs={{0,76},{1,77},{2,78},{3,79},{4,72},{5,73},{6,74},{7,75},{8,68},{9,... | collective-permute-start | bytes 884744 | tf_op jit(solution)/shard_map/ppermute | solution.py:42
  137.7 3.9 %copy-start.21 = (bf16[384,384]{1,0:T(8,128)(2,1)}, bf16[384,384]{1,0:T(8,128)(2,1)S(1)}, u32[]{:S(2)}) copy-start(bf16[384,384]{1,0:T(8,128)(2,1)S(1)} %collective-permute-done.14.refs_2_) | copy-start | bytes 884740
  137.8 29.6 %collective-permute-start.24 = (bf16[2,384,768]{2,1,0:T(8,128)(2,1)}, bf16[2,384,768]{2,1,0:T(8,128)(2,1)S(1)}, u32[]{:S(2)}, u32[]{:S(2)}) collective-permute-start(bf16[2,384,768]{2,1,0:T(8,128)(2,1)} %get-tuple-element.54), channel_id=1, source_target_pairs={{0,1},{1,2},{2,3},{3,4},{4,5},{5,6},{6,7},{8,9},{9,10},{10,11},{11... | collective-permute-start | bytes 3538952 | tf_op jit(solution)/shard_map/ppermute | solution.py:78
  139.1 29.6 %collective-permute-start.25 = (bf16[2,384,768]{2,1,0:T(8,128)(2,1)}, bf16[2,384,768]{2,1,0:T(8,128)(2,1)}, u32[]{:S(2)}, u32[]{:S(2)}) collective-permute-start(bf16[2,384,768]{2,1,0:T(8,128)(2,1)} %get-tuple-element.55), channel_id=1, source_target_pairs={{1,0},{2,1},{3,2},{4,3},{5,4},{6,5},{7,6},{9,8},{10,9},{11,10},{12... | collective-permute-start | bytes 3538952 | tf_op jit(solution)/shard_map/ppermute | solution.py:82
  140.4 1.2 copy-start.8
  141.7 1.1 copy-start.9
  152.6 23.4 %collective-permute-start.26 = (bf16[96,3072]{1,0:T(8,128)(2,1)}, bf16[96,3072]{1,0:T(8,128)(2,1)S(1)}, u32[]{:S(2)}, u32[]{:S(2)}) collective-permute-start(bf16[96,3072]{1,0:T(8,128)(2,1)} %get-tuple-element.60), channel_id=1, source_target_pairs={{0,16},{1,17},{2,18},{3,19},{4,20},{5,21},{6,22},{7,23},{8,24},{9,... | collective-permute-start | bytes 1769480 | tf_op jit(solution)/shard_map/ppermute | solution.py:42
  154.7 21.3 %collective-permute-start.27 = (bf16[96,3072]{1,0:T(8,128)(2,1)}, bf16[96,3072]{1,0:T(8,128)(2,1)}, u32[]{:S(2)}, u32[]{:S(2)}) collective-permute-start(bf16[96,3072]{1,0:T(8,128)(2,1)} %get-tuple-element.61), channel_id=1, source_target_pairs={{0,48},{1,49},{2,50},{3,51},{4,52},{5,53},{6,54},{7,55},{8,56},{9,... | collective-permute-start | bytes 1769480 | tf_op jit(solution)/shard_map/ppermute | solution.py:42
  155.9 26.4 %collective-permute-start.28 = (bf16[96,3072]{1,0:T(8,128)(2,1)}, bf16[96,3072]{1,0:T(8,128)(2,1)}, u32[]{:S(2)}, u32[]{:S(2)}) collective-permute-start(bf16[96,3072]{1,0:T(8,128)(2,1)} %get-tuple-element.62), channel_id=1, source_target_pairs={{0,32},{1,33},{2,34},{3,35},{4,36},{5,37},{6,38},{7,39},{8,40},{9,... | collective-permute-start | bytes 1769480 | tf_op jit(solution)/shard_map/ppermute | solution.py:42
  167.4 5.0 %copy-start.18 = (bf16[2,384,768]{2,1,0:T(8,128)(2,1)}, bf16[2,384,768]{2,1,0:T(8,128)(2,1)S(1)}, u32[]{:S(2)}) copy-start(bf16[2,384,768]{2,1,0:T(8,128)(2,1)S(1)} %collective-permute-done.24.a_ref) | copy-start | bytes 3538948
  167.4 45.8 %collective-permute-start.22 = (bf16[384,1536]{1,0:T(8,128)(2,1)}, bf16[384,1536]{1,0:T(8,128)(2,1)S(1)}, u32[]{:S(2)}, u32[]{:S(2)}) collective-permute-start(bf16[384,1536]{1,0:T(8,128)(2,1)} %get-tuple-element.51), channel_id=1, source_target_pairs={{0,8},{1,9},{2,10},{3,11},{4,12},{5,13},{6,14},{7,15},{8,0},{9,1},... | collective-permute-start | bytes 3538952 | tf_op jit(solution)/shard_map/ppermute | solution.py:42
  168.7 44.5 %collective-permute-start.23 = (bf16[384,1536]{1,0:T(8,128)(2,1)}, bf16[384,1536]{1,0:T(8,128)(2,1)S(1)}, u32[]{:S(2)}, u32[]{:S(2)}) collective-permute-start(bf16[384,1536]{1,0:T(8,128)(2,1)} %get-tuple-element.52), channel_id=1, source_target_pairs={{0,8},{1,9},{2,10},{3,11},{4,12},{5,13},{6,14},{7,15},{8,0},{9,1},... | collective-permute-start | bytes 3538952 | tf_op jit(solution)/shard_map/ppermute | solution.py:42
  176.0 6.3 %copy-start.19 = (bf16[96,3072]{1,0:T(8,128)(2,1)}, bf16[96,3072]{1,0:T(8,128)(2,1)S(1)}, u32[]{:S(2)}) copy-start(bf16[96,3072]{1,0:T(8,128)(2,1)S(1)} %collective-permute-done.26.refs_1_) | copy-start | bytes 1769476
  184.9 16.0 %collective-permute-start.29 = (bf16[96,768]{1,0:T(8,128)(2,1)}, bf16[96,768]{1,0:T(8,128)(2,1)S(1)}, u32[]{:S(2)}, u32[]{:S(2)}) collective-permute-start(bf16[96,768]{1,0:T(8,128)(2,1)} %get-tuple-element.64), channel_id=1, source_target_pairs={{0,1},{1,2},{2,3},{3,0},{4,5},{5,6},{6,7},{7,4},{8,9},{9,10},{10,1... | collective-permute-start | bytes 442376 | tf_op jit(solution)/shard_map/ppermute | solution.py:42
  189.6 11.4 %collective-permute-start.30 = (bf16[96,768]{1,0:T(8,128)(2,1)}, bf16[96,768]{1,0:T(8,128)(2,1)S(1)}, u32[]{:S(2)}, u32[]{:S(2)}) collective-permute-start(bf16[96,768]{1,0:T(8,128)(2,1)} %get-tuple-element.65), channel_id=1, source_target_pairs={{0,3},{1,0},{2,1},{3,2},{4,7},{5,4},{6,5},{7,6},{8,11},{9,8},{10,9... | collective-permute-start | bytes 442376 | tf_op jit(solution)/shard_map/ppermute | solution.py:42
  196.3 6.9 %collective-permute-start.31 = (bf16[96,768]{1,0:T(8,128)(2,1)}, bf16[96,768]{1,0:T(8,128)(2,1)S(1)}, u32[]{:S(2)}, u32[]{:S(2)}) collective-permute-start(bf16[96,768]{1,0:T(8,128)(2,1)} %get-tuple-element.66), channel_id=1, source_target_pairs={{0,2},{1,3},{2,0},{3,1},{4,6},{5,7},{6,4},{7,5},{8,10},{9,11},{10,... | collective-permute-start | bytes 442376 | tf_op jit(solution)/shard_map/ppermute | solution.py:42
  204.2 5.2 %collective-permute-start.32 = (bf16[96,768]{1,0:T(8,128)(2,1)S(1)}, bf16[96,768]{1,0:T(8,128)(2,1)S(1)}, u32[]{:S(2)}, u32[]{:S(2)}) collective-permute-start(bf16[96,768]{1,0:T(8,128)(2,1)S(1)} %add_convert_fusion.1), channel_id=1, source_target_pairs={{0,4},{1,5},{2,6},{3,7},{4,0},{5,1},{6,2},{7,3},{8,12},{9,13},{10,... | collective-permute-start | bytes 442376 | tf_op jit(solution)/shard_map/ppermute | solution.py:42
  209.5 9.7 %copy-start.20 = (bf16[96,768]{1,0:T(8,128)(2,1)}, bf16[96,768]{1,0:T(8,128)(2,1)S(1)}, u32[]{:S(2)}) copy-start(bf16[96,768]{1,0:T(8,128)(2,1)S(1)} %add_convert_fusion.refs_0_) | copy-start | bytes 442372
  209.5 9.7 %collective-permute-start.35 = (bf16[96,768]{1,0:T(8,128)(2,1)S(1)}, bf16[96,768]{1,0:T(8,128)(2,1)S(1)}, u32[]{:S(2)}, u32[]{:S(2)}) collective-permute-start(bf16[96,768]{1,0:T(8,128)(2,1)S(1)} %add_convert_fusion.refs_0_), channel_id=1, source_target_pairs={{0,2},{1,3},{2,0},{3,1},{4,6},{5,7},{6,4},{7,5},{8,10},{9,11},{10,... | collective-permute-start | bytes 442376 | tf_op jit(solution)/shard_map/ppermute | solution.py:42
  211.0 8.2 %collective-permute-start.34 = (bf16[96,768]{1,0:T(8,128)(2,1)S(1)}, bf16[96,768]{1,0:T(8,128)(2,1)S(1)}, u32[]{:S(2)}, u32[]{:S(2)}) collective-permute-start(bf16[96,768]{1,0:T(8,128)(2,1)S(1)} %add_convert_fusion.refs_0_), channel_id=1, source_target_pairs={{0,3},{1,0},{2,1},{3,2},{4,7},{5,4},{6,5},{7,6},{8,11},{9,8},{10,9... | collective-permute-start | bytes 442376 | tf_op jit(solution)/shard_map/ppermute | solution.py:42
  213.2 6.4 %collective-permute-start.33 = (bf16[96,768]{1,0:T(8,128)(2,1)S(1)}, bf16[96,768]{1,0:T(8,128)(2,1)S(1)}, u32[]{:S(2)}, u32[]{:S(2)}) collective-permute-start(bf16[96,768]{1,0:T(8,128)(2,1)S(1)} %add_convert_fusion.refs_0_), channel_id=1, source_target_pairs={{0,1},{1,2},{2,3},{3,0},{4,5},{5,6},{6,7},{7,4},{8,9},{9,10},{10,1... | collective-permute-start | bytes 442376 | tf_op jit(solution)/shard_map/ppermute | solution.py:42
  213.2 1.0 copy-start.15
  213.2 1.4 copy-start.16
  219.2 0.7 copy-start.25
  219.2 0.7 copy-start.26
  219.9 0.6 copy-start.27

commit v4 on v3

--- a/solution.py
+++ b/solution.py
@@ -18,7 +18,7 @@
 BF = jnp.bfloat16
 F32 = jnp.float32
 VMEM_LIMIT = 60 * 1024 * 1024
-WG_STEPS = 4
+WG_STEPS = 3
 
 NX, NZ, NC, NL, NY = 2, 4, 2, 2, 4
 NS = NL * NY
@@ -404,7 +404,9 @@
 def weight_grad_kernel(place, *refs):
     a_refs, u_refs = refs[:4], refs[4:8]
     out_refs, total = refs[-1 - NZ:-1], refs[-1]
-    total[...] = sum(nn(a[...], u[...]) for a, u in zip(a_refs, u_refs)).astype(BF)
+    left = jnp.concatenate([a[...] for a in a_refs], axis=1)
+    right = jnp.concatenate([u[...] for u in u_refs], axis=0)
+    total[...] = nn(left, right).astype(BF)
     rows = out_refs[0].shape[0]
     for i, out in enumerate(out_refs):
         out[...] = total[pl.ds(pl.multiple_of(place[TO_Z + i] * rows, rows), rows), :]
@@ -523,12 +525,12 @@
     attn0, total0 = attend(0, info, q, k, v, *near0, heads)
     grad0 = back(w0, (attn0,))
     w1 = around(hold(cross, pair))
-    attn1, total1 = attend(1, info, q, k, v, *near1, heads, (grad0[0], w1[1], w1[2]))
-    w1.append(move_z(w1[0], 2))
+    dq, own0, to_left, to_right = attend_back(
+        0, info, q, k, v, *near0, grad0, attn0, total0, heads, (w1[1], w1[2]), False
+    )
+    w1.append(move_z(hold(w1[0], grad0[0]), 2))
+    attn1, total1 = attend(1, info, q, k, v, *near1, heads, (own0, w1[3]))
     up_cross = hold(up_cross, attn1)
-    dq, own0, to_left, to_right = attend_back(
-        0, info, q, k, v, *near0, grad0, attn0, total0, heads, (attn1,), False
-    )
     sent0 = (to_next(to_right), to_previous(to_left))
 
     def pick(attn, core):
@@ -545,16 +547,16 @@
         move_cross(own_part),
         move_cross_core(core_part),
     ]
-    grad1 = back(w1, (own0,))
+    grad1 = back(w1, (attn1,))
     core_far = move_core(core_part)
     dq, own1, to_left, to_right = attend_back(
         1, info, q, k, v, *near1, grad1, attn1, total1, heads, (dq, core_far), True
     )
     sent1 = (to_next(to_right), to_previous(to_left))
     u_list = [upstream, up_core, up_cross, move_core(up_cross)]
-    pieces = weight_grad(info, a_list, u_list, (own1,) + sent0)
+    pieces = weight_grad(info, a_list, u_list, (own1,))
     turned = [a_list[0], own_part, a_list[1], core_far]
-    near, *far = project(info, turned, w0 + w1, pieces[:1])
+    near, *far = project(info, turned, w0 + w1, pieces[:1] + sent0)
     mixed = meet(near, *[move_core(t) for t in far])
     done = join(0, info, own0, *sent0, heads, cols, None)
     done = join(1, info, own1, *sent1, heads, cols, done)

time: 224 us -> 213 us (0.951)
  starting transfers between devices: 73.7 us -> 64.8 us
  waiting for transfers between devices: 39.8 us -> 35.7 us
  local copies, waits for them, and re-layouts: 9.55 us -> 12.6 us
    ppermute x28, starting transfers between devices: 51 us -> 43.3 us  [move(): return lax.ppermute(x, ('dp', 'space'), moves(change))]
    ppermute x4, waiting for transfers between devices: 9.94 us -> 6.53 us  [to_previous(): return lax.ppermute(x, 'space', [(i + 1, i) for i in range(NS - 1)])]
    unnamed x58 -> x57, local copies, waits for them, and re-layouts: 7.94 us -> 10.9 us
  transfers between devices with their start and end apart: 36 -> 36, of which waited for: 14 -> 13; matrix products, arithmetic and copies ran while one was open for 2% -> 3% of each run, Pallas kernels for 43% -> 45%
where the time goes in v4:
time: 213 us; the launch traced here: 212 us
  Pallas kernels  96.9 us (45%)
  starting transfers between devices  64.8 us (30%)
  waiting for transfers between devices  35.7 us (17%)
  local copies, waits for them, and re-layouts  12.6 us (6%)
    ppermute x28, starting transfers between devices, move(): return lax.ppermute(x, ('dp', 'space'), moves(change))  43.3 us
    ppermute x28, waiting for transfers between devices, move(): return lax.ppermute(x, ('dp', 'space'), moves(change))  26.3 us
    pallas_call x2, Pallas kernels, attend_back(): pl.pallas_call(functools.partial(backward_kernel, per, part), out_shape=(...  26.1 us
    pallas_call x2, Pallas kernels, attend(): pl.pallas_call(functools.partial(forward_kernel, per, part), out_shape=(j...  16.5 us
    ppermute x4, starting transfers between devices, to_next(): return lax.ppermute(x, 'space', [(i, i + 1) for i in range(NS - 1)])  16.3 us
    pallas_call x2, Pallas kernels, project_back(): pl.pallas_call(project_back_kernel, out_shape=(jax.ShapeDtypeStruct((NZ *...  13.1 us
    unnamed x57, local copies, waits for them, and re-layouts  10.9 us
    pallas_call x1, Pallas kernels, project(): pl.pallas_call(project_kernel, out_shape=(jax.ShapeDtypeStruct((tokens, w...  9.43 us
  transfers between devices with their start and end apart: 36, of which 13 were waited for; matrix products, arithmetic and copies ran while one was open for 3% of the time, Pallas kernels for 45%

profile of v4, /device:TPU:0, one launch (start us, length us, event | category | flops | bytes accessed | tf_op | source)
XLA Modules:
  0.0 212.1 jit_solution(3000625419960283952)
XLA Ops:
  0.7 2.9 %collective-permute-start.9 = (bf16[96,3072]{1,0:T(8,128)(2,1)}, bf16[96,3072]{1,0:T(8,128)(2,1)S(1)}, u32[]{:S(2)}, u32[]{:S(2)}) collective-permute-start(bf16[96,3072]{1,0:T(8,128)(2,1)} %refs_4_.1), channel_id=1, source_target_pairs={{0,68},{1,69},{2,70},{3,71},{4,64},{5,65},{6,66},{7,67},{8,76},{9,... | collective-permute-start | bytes 1769480 | tf_op jit(solution)/shard_map/ppermute | solution.py:42
  3.6 1.9 collective-permute-start.2
  5.6 0.8 copy.25
  6.4 0.7 concatenate.3.info.place.spots
  7.1 3.1 %window.2 = bf16[2,384,768]{2,1,0:T(8,128)(2,1)} custom-call(s32[44]{0:T(128)} %concatenate.3.info.place.spots, bf16[384,1536]{1,0:T(8,128)(2,1)} %bitcast.34, bf16[384,1536]{1,0:T(8,128)(2,1)} %bitcast.40), custom_call_target="tpu_custom_call" | custom-call | flops 1000 | bytes 1000 | tf_op jit(solution)/shard_map/window/pallas_call | solution.py:300
  10.2 1.3 collective-permute-start.1
  11.5 5.6 %collective-permute-start = (bf16[2,384,768]{2,1,0:T(8,128)(2,1)}, bf16[2,384,768]{2,1,0:T(8,128)(2,1)}, u32[]{:S(2)}, u32[]{:S(2)}) collective-permute-start(bf16[2,384,768]{2,1,0:T(8,128)(2,1)} %window.2), channel_id=1, source_target_pairs={{0,1},{1,2},{2,3},{3,4},{4,5},{5,6},{6,7},{8,9},{9,10},{10,11},{11... | collective-permute-start | bytes 3538952 | tf_op jit(solution)/shard_map/ppermute | solution.py:78
  17.0 1.4 copy.38.x_ref
  18.4 0.8 copy-done.2
  19.3 2.3 %collective-permute-start.17 = (bf16[384,3072]{1,0:T(8,128)(2,1)}, bf16[384,3072]{1,0:T(8,128)(2,1)S(1)}, u32[]{:S(2)}, u32[]{:S(2)}) collective-permute-start(bf16[384,3072]{1,0:T(8,128)(2,1)} %hold.10), channel_id=1, source_target_pairs={{0,68},{1,69},{2,70},{3,71},{4,64},{5,65},{6,66},{7,67},{8,76},{9,... | collective-permute-start | bytes 7077896 | tf_op jit(solution)/shard_map/ppermute | solution.py:42
  21.6 4.0 %collective-permute-start.4 = (bf16[96,3072]{1,0:T(8,128)(2,1)}, bf16[96,3072]{1,0:T(8,128)(2,1)S(1)}, u32[]{:S(2)}, u32[]{:S(2)}) collective-permute-start(bf16[96,3072]{1,0:T(8,128)(2,1)} %refs_4_.1), channel_id=1, source_target_pairs={{0,48},{1,49},{2,50},{3,51},{4,52},{5,53},{6,54},{7,55},{8,56},{9,... | collective-permute-start | bytes 1769480 | tf_op jit(solution)/shard_map/ppermute | solution.py:42
  25.6 2.9 %window.3.x_ref = bf16[2,384,768]{2,1,0:T(8,128)(2,1)} custom-call(s32[44]{0:T(128)} %concatenate.3.info.place.spots, bf16[384,1536]{1,0:T(8,128)(2,1)} %bitcast.35, bf16[384,1536]{1,0:T(8,128)(2,1)} %bitcast.41, bf16[96,3072]{1,0:T(8,128)(2,1)} %hold.6.rest_0_.rest_2_.refs_1_.refs_5_), custom_call_target="tpu_custom_call" | custom-call | flops 1000 | bytes 1000 | tf_op jit(solution)/shard_map/window/pallas_call | solution.py:300
  28.6 9.5 %collective-permute-done.4.rest_3_.refs_2_.refs_6_ = bf16[96,3072]{1,0:T(8,128)(2,1)S(1)} collective-permute-done((bf16[96,3072]{1,0:T(8,128)(2,1)}, bf16[96,3072]{1,0:T(8,128)(2,1)S(1)}, u32[]{:S(2)}, u32[]{:S(2)}) %collective-permute-start.4) | collective-permute-done | bytes 589856 | tf_op jit(solution)/shard_map/ppermute | solution.py:42
  38.0 2.1 collective-permute-done.1.right_ref.rest_1_
  40.1 1.2 collective-permute-done.left_ref.rest_0_
  41.3 2.4 %collective-permute-start.11 = (bf16[96,3072]{1,0:T(8,128)(2,1)}, bf16[96,3072]{1,0:T(8,128)(2,1)}, u32[]{:S(2)}, u32[]{:S(2)}) collective-permute-start(bf16[96,3072]{1,0:T(8,128)(2,1)} %hold.8.refs_0_.refs_8_), channel_id=1, source_target_pairs={{0,48},{1,49},{2,50},{3,51},{4,52},{5,53},{6,54},{7,55},{8,56},{9,... | collective-permute-start | bytes 1769480 | tf_op jit(solution)/shard_map/ppermute | solution.py:42
  43.7 1.3 collective-permute-start.6
  45.0 6.0 %collective-permute-start.5 = (bf16[2,384,768]{2,1,0:T(8,128)(2,1)S(1)}, bf16[2,384,768]{2,1,0:T(8,128)(2,1)}, u32[]{:S(2)}, u32[]{:S(2)}) collective-permute-start(bf16[2,384,768]{2,1,0:T(8,128)(2,1)S(1)} %copy-done.4), channel_id=1, source_target_pairs={{0,1},{1,2},{2,3},{3,4},{4,5},{5,6},{6,7},{8,9},{9,10},{10,11},{11... | collective-permute-start | bytes 3538952 | tf_op jit(solution)/shard_map/ppermute | solution.py:78
  51.0 0.8 collective-permute-start.10
  51.8 8.3 %attend.2 = (bf16[768,384]{1,0:T(8,128)(2,1)}, f32[6,1,384]{2,1,0:T(1,128)}) custom-call(s32[44]{0:T(128)} %concatenate.3.info.place.spots, bf16[384,1536]{1,0:T(8,128)(2,1)} %bitcast.51, bf16[384,1536]{1,0:T(8,128)(2,1)} %bitcast.36, bf16[384,1536]{1,0:T(8,128)(2,1)} %bitcast.42, bf16[2,384,768]{2,1,0:T(8,128)(2,1)} %collective-permute-done.left_ref.rest_0_, ...), custom_call_target="tpu_custom_call" | custom-call | flops 1000 | bytes 1000 | tf_op jit(solution)/shard_map/attend/pallas_call | solution.py:151
  60.1 0.8 copy.37.x_ref
  60.9 6.6 %project_back.2 = (bf16[384,384]{1,0:T(8,128)(2,1)}, bf16[384,384]{1,0:T(8,128)(2,1)}) custom-call(s32[44]{0:T(128)} %concatenate.3.info.place.spots, bf16[96,3072]{1,0:T(8,128)(2,1)} %refs_4_.1, bf16[96,3072]{1,0:T(8,128)(2,1)} %hold.6.rest_0_.rest_2_.refs_1_.refs_5_, bf16[96,3072]{1,0:T(8,128)(2,1)} %copy-done.7, ...), custom_call_target="tpu_custom_call" | custom-call | flops 1000 | bytes 1000 | tf_op jit(solution)/shard_map/project_back/pallas_call | solution.py:327
  67.5 2.4 %collective-permute-start.12 = (bf16[96,3072]{1,0:T(8,128)(2,1)}, bf16[96,3072]{1,0:T(8,128)(2,1)S(1)}, u32[]{:S(2)}, u32[]{:S(2)}) collective-permute-start(bf16[96,3072]{1,0:T(8,128)(2,1)} %hold.9), channel_id=1, source_target_pairs={{0,32},{1,33},{2,34},{3,35},{4,36},{5,37},{6,38},{7,39},{8,40},{9,... | collective-permute-start | bytes 1769480 | tf_op jit(solution)/shard_map/ppermute | solution.py:42
  70.0 1.9 collective-permute-done.8.theirs_ref
  71.9 13.1 %attend_back.2 = (bf16[384,1536]{1,0:T(8,128)(2,1)}, bf16[2,384,768]{2,1,0:T(8,128)(2,1)}, bf16[2,384,768]{2,1,0:T(8,128)(2,1)}, bf16[2,384,768]{2,1,0:T(8,128)(2,1)}) custom-call(s32[44]{0:T(128)} %concatenate.3.info.place.spots, bf16[384,1536]{1,0:T(8,128)(2,1)} %bitcast.52, bf16[384,1536]{1,0:T(8,128)(2,1)} %bitcast.37, bf16[384,1536]{1,0:T(8,128)(2,1)} %bitcast.43, ...), custom_call_target="tpu_custom_call" | custom-call | flops 1000 | bytes 1000 | tf_op jit(solution)/shard_map/attend_back/pallas_call | solution.py:214
  85.0 0.8 copy-done.8
  85.8 8.2 %attend.3 = (bf16[768,384]{1,0:T(8,128)(2,1)}, f32[6,1,384]{2,1,0:T(1,128)}) custom-call(s32[44]{0:T(128)} %concatenate.3.info.place.spots, bf16[384,1536]{1,0:T(8,128)(2,1)} %bitcast.53, bf16[384,1536]{1,0:T(8,128)(2,1)} %bitcast.38, bf16[384,1536]{1,0:T(8,128)(2,1)} %bitcast.44, bf16[2,384,768]{2,1,0:T(8,128)(2,1)} %collective-permute-done.5.left_ref, ...), custom_call_target="tpu_custom_call" | custom-call | flops 1000 | bytes 1000 | tf_op jit(solution)/shard_map/attend/pallas_call | solution.py:151
  94.0 1.4 copy-done.5
  95.5 0.9 copy-done.9
  96.4 0.8 constant_dynamic-slice_fusion.1
  97.9 6.6 %project_back.3 = (bf16[384,384]{1,0:T(8,128)(2,1)}, bf16[384,384]{1,0:T(8,128)(2,1)}) custom-call(s32[44]{0:T(128)} %concatenate.3.info.place.spots, bf16[96,3072]{1,0:T(8,128)(2,1)} %hold.8.refs_0_.refs_8_, bf16[96,3072]{1,0:T(8,128)(2,1)} %collective-permute-done.10.rest_0_.refs_1_.refs_9_, ...), custom_call_target="tpu_custom_call" | custom-call | flops 1000 | bytes 1000 | tf_op jit(solution)/shard_map/project_back/pallas_call | solution.py:327
  104.6 3.1 %collective-permute-start.20 = (bf16[2,384,768]{2,1,0:T(8,128)(2,1)}, bf16[2,384,768]{2,1,0:T(8,128)(2,1)S(1)}, u32[]{:S(2)}, u32[]{:S(2)}) collective-permute-start(bf16[2,384,768]{2,1,0:T(8,128)(2,1)} %get-tuple-element.48), channel_id=1, source_target_pairs={{0,1},{1,2},{2,3},{3,4},{4,5},{5,6},{6,7},{8,9},{9,10},{10,11},{11... | collective-permute-start | bytes 3538952 | tf_op jit(solution)/shard_map/ppermute | solution.py:78
  107.8 1.3 collective-permute-start.21
  109.1 8.7 %collective-permute-start.15 = (bf16[384,384]{1,0:T(8,128)(2,1)S(1)}, bf16[384,384]{1,0:T(8,128)(2,1)S(1)}, u32[]{:S(2)}, u32[]{:S(2)}) collective-permute-start(bf16[384,384]{1,0:T(8,128)(2,1)S(1)} %bitcast.62), channel_id=1, source_target_pairs={{0,68},{1,69},{2,70},{3,71},{4,64},{5,65},{6,66},{7,67},{8,76},{9,... | collective-permute-start | bytes 884744 | tf_op jit(solution)/shard_map/ppermute | solution.py:42
  117.8 0.7 copy-done.22
  118.5 13.1 %attend_back.3 = (bf16[384,1536]{1,0:T(8,128)(2,1)}, bf16[2,384,768]{2,1,0:T(8,128)(2,1)}, bf16[2,384,768]{2,1,0:T(8,128)(2,1)}, bf16[2,384,768]{2,1,0:T(8,128)(2,1)}) custom-call(s32[44]{0:T(128)} %concatenate.3.info.place.spots, bf16[384,1536]{1,0:T(8,128)(2,1)} %bitcast.54, bf16[384,1536]{1,0:T(8,128)(2,1)} %bitcast.39, ...), custom_call_target="tpu_custom_call", output_to_operand_aliasing={{0}: (10, {})} | custom-call | flops 1000 | bytes 1000 | tf_op jit(solution)/shard_map/attend_back/pallas_call | solution.py:214
  131.6 1.6 collective-permute-start.24
  133.2 1.3 collective-permute-start.25
  134.5 9.0 %weight_grad.1 = (bf16[96,3072]{1,0:T(8,128)(2,1)}, bf16[96,3072]{1,0:T(8,128)(2,1)}, bf16[96,3072]{1,0:T(8,128)(2,1)}, bf16[96,3072]{1,0:T(8,128)(2,1)}) custom-call(s32[44]{0:T(128)} %concatenate.3.info.place.spots, bf16[384,384]{1,0:T(8,128)(2,1)} %bitcast.60, bf16[384,384]{1,0:T(8,128)(2,1)} %copy-done.12, bf16[384,384]{1,0:T(8,128)(2,1)} %copy-done.20, ...), custom_call_target="tpu_custom_call" | custom-call | flops 1000 | bytes 1000 | tf_op jit(solution)/shard_map/weight_grad/pallas_call | solution.py:420
  143.5 0.9 collective-permute-start.26
  144.4 2.4 %collective-permute-start.27 = (bf16[96,3072]{1,0:T(8,128)(2,1)}, bf16[96,3072]{1,0:T(8,128)(2,1)}, u32[]{:S(2)}, u32[]{:S(2)}) collective-permute-start(bf16[96,3072]{1,0:T(8,128)(2,1)} %get-tuple-element.61), channel_id=1, source_target_pairs={{0,48},{1,49},{2,50},{3,51},{4,52},{5,53},{6,54},{7,55},{8,56},{9,... | collective-permute-start | bytes 1769480 | tf_op jit(solution)/shard_map/ppermute | solution.py:42
  147.0 0.8 copy-done.11
  147.8 9.4 %project.1 = (bf16[384,3072]{1,0:T(8,128)(2,1)}, bf16[384,1536]{1,0:T(8,128)(2,1)}, bf16[384,1536]{1,0:T(8,128)(2,1)}) custom-call(s32[44]{0:T(128)} %concatenate.3.info.place.spots, bf16[384,384]{1,0:T(8,128)(2,1)} %bitcast.61, bf16[384,384]{1,0:T(8,128)(2,1)} %bitcast.63, bf16[384,384]{1,0:T(8,128)(2,1)} %copy-done.12, bf16[384,384]{1,0:T(8,128)(2,1)} %copy-done.13, ...), custom_call_target="tpu_custom_call" | custom-call | flops 1000 | bytes 1000 | tf_op jit(solution)/shard_map/project/pallas_call | solution.py:366
  157.3 1.7 collective-permute-done.24.a_ref
  159.0 4.4 %collective-permute-done.25.b_ref = bf16[2,384,768]{2,1,0:T(8,128)(2,1)} collective-permute-done((bf16[2,384,768]{2,1,0:T(8,128)(2,1)}, bf16[2,384,768]{2,1,0:T(8,128)(2,1)}, u32[]{:S(2)}, u32[]{:S(2)}) %collective-permute-start.25) | collective-permute-done | bytes 1179680 | tf_op jit(solution)/shard_map/ppermute | solution.py:82
  163.4 3.6 %join.2 = (bf16[384,1536]{1,0:T(8,128)(2,1)}, bf16[384,1536]{1,0:T(8,128)(2,1)}) custom-call(s32[44]{0:T(128)} %concatenate.3.info.place.spots, bf16[2,384,768]{2,1,0:T(8,128)(2,1)} %get-tuple-element.40.rest_0_.own_ref, bf16[2,384,768]{2,1,0:T(8,128)(2,1)} %copy-done.10, bf16[2,384,768]{2,1,0:T(8,128)(2,1)} %copy-done.11), custom_call_target="tpu_custom_call" | custom-call | flops 1000 | bytes 1000 | tf_op jit(solution)/shard_map/join/pallas_call | solution.py:251
  167.0 3.6 %join.3 = (bf16[384,1536]{1,0:T(8,128)(2,1)}, bf16[384,1536]{1,0:T(8,128)(2,1)}) custom-call(s32[44]{0:T(128)} %concatenate.3.info.place.spots, bf16[2,384,768]{2,1,0:T(8,128)(2,1)} %get-tuple-element.46.refs_8_.own_ref, bf16[2,384,768]{2,1,0:T(8,128)(2,1)} %copy-done.17, ...), custom_call_target="tpu_custom_call", output_to_operand_aliasing={{0}: (4, {}), {1}: (5, {})} | custom-call | flops 1000 | bytes 1000 | tf_op jit(solution)/shard_map/join/pallas_call | solution.py:251
  170.7 1.1 collective-permute-done.27.refs_2_
  171.8 0.8 collective-permute-done.28.refs_3_
  172.6 2.6 %sum_columns.1 = (f32[96,768]{1,0:T(8,128)}, bf16[96,768]{1,0:T(8,128)(2,1)}, bf16[96,768]{1,0:T(8,128)(2,1)}, bf16[96,768]{1,0:T(8,128)(2,1)}) custom-call(s32[44]{0:T(128)} %concatenate.3.info.place.spots, bf16[96,3072]{1,0:T(8,128)(2,1)} %get-tuple-element.47.refs_12_.refs_0_, bf16[96,3072]{1,0:T(8,128)(2,1)} %copy-done.18, ...), custom_call_target="tpu_custom_call" | custom-call | flops 1000 | bytes 1000 | tf_op jit(solution)/shard_map/sum_columns/pallas_call | solution.py:449
  175.2 3.5 %collective-permute-start.29 = (bf16[96,768]{1,0:T(8,128)(2,1)}, bf16[96,768]{1,0:T(8,128)(2,1)S(1)}, u32[]{:S(2)}, u32[]{:S(2)}) collective-permute-start(bf16[96,768]{1,0:T(8,128)(2,1)} %get-tuple-element.64), channel_id=1, source_target_pairs={{0,1},{1,2},{2,3},{3,0},{4,5},{5,6},{6,7},{7,4},{8,9},{9,10},{10,1... | collective-permute-start | bytes 442376 | tf_op jit(solution)/shard_map/ppermute | solution.py:42
  178.7 4.5 %collective-permute-start.30 = (bf16[96,768]{1,0:T(8,128)(2,1)}, bf16[96,768]{1,0:T(8,128)(2,1)S(1)}, u32[]{:S(2)}, u32[]{:S(2)}) collective-permute-start(bf16[96,768]{1,0:T(8,128)(2,1)} %get-tuple-element.65), channel_id=1, source_target_pairs={{0,3},{1,0},{2,1},{3,2},{4,7},{5,4},{6,5},{7,6},{8,11},{9,8},{10,9... | collective-permute-start | bytes 442376 | tf_op jit(solution)/shard_map/ppermute | solution.py:42
  183.2 1.5 collective-permute-start.31
  184.6 3.3 %collective-permute-done.29 = bf16[96,768]{1,0:T(8,128)(2,1)S(1)} collective-permute-done((bf16[96,768]{1,0:T(8,128)(2,1)}, bf16[96,768]{1,0:T(8,128)(2,1)S(1)}, u32[]{:S(2)}, u32[]{:S(2)}) %collective-permute-start.29) | collective-permute-done | bytes 147488 | tf_op jit(solution)/shard_map/ppermute | solution.py:42
  187.9 2.5 %collective-permute-done.30 = bf16[96,768]{1,0:T(8,128)(2,1)S(1)} collective-permute-done((bf16[96,768]{1,0:T(8,128)(2,1)}, bf16[96,768]{1,0:T(8,128)(2,1)S(1)}, u32[]{:S(2)}, u32[]{:S(2)}) %collective-permute-start.30) | collective-permute-done | bytes 147488 | tf_op jit(solution)/shard_map/ppermute | solution.py:42
  190.4 1.8 collective-permute-done.31
  192.2 1.0 add_convert_fusion.1
  193.3 0.5 collective-permute-start.32
  193.7 5.1 %collective-permute-done.32 = bf16[96,768]{1,0:T(8,128)(2,1)S(1)} collective-permute-done((bf16[96,768]{1,0:T(8,128)(2,1)S(1)}, bf16[96,768]{1,0:T(8,128)(2,1)S(1)}, u32[]{:S(2)}, u32[]{:S(2)}) %collective-permute-start.32) | collective-permute-done | bytes 147488 | tf_op jit(solution)/shard_map/ppermute | solution.py:42
  199.0 3.5 %collective-permute-start.34 = (bf16[96,768]{1,0:T(8,128)(2,1)S(1)}, bf16[96,768]{1,0:T(8,128)(2,1)S(1)}, u32[]{:S(2)}, u32[]{:S(2)}) collective-permute-start(bf16[96,768]{1,0:T(8,128)(2,1)S(1)} %add_convert_fusion.refs_0_), channel_id=1, source_target_pairs={{0,3},{1,0},{2,1},{3,2},{4,7},{5,4},{6,5},{7,6},{8,11},{9,8},{10,9... | collective-permute-start | bytes 442376 | tf_op jit(solution)/shard_map/ppermute | solution.py:42
  202.5 1.0 copy-done.14
  203.8 4.6 %meet.1.refs_4_ = bf16[384,3072]{1,0:T(8,128)(2,1)} custom-call(bf16[384,3072]{1,0:T(8,128)(2,1)} %get-tuple-element.50.near_ref, bf16[384,1536]{1,0:T(8,128)(2,1)} %copy-done.14, bf16[384,1536]{1,0:T(8,128)(2,1)} %copy-done.15), custom_call_target="tpu_custom_call" | custom-call | flops 1000 | bytes 1000 | tf_op jit(solution)/shard_map/meet/pallas_call | solution.py:392
  209.2 0.6 copy-done.26
  209.8 2.2 %place_columns.1 = f32[96,3072]{1,0:T(8,128)} custom-call(s32[44]{0:T(128)} %concatenate.3.info.place.spots, bf16[96,768]{1,0:T(8,128)(2,1)} %copy-done.19, bf16[96,768]{1,0:T(8,128)(2,1)} %copy-done.26, bf16[96,768]{1,0:T(8,128)(2,1)} %copy-done.25, bf16[96,768]{1,0:T(8,128)(2,1)} %copy-done.24, bf16[384,3072]{1,0:T(8,128)(2,1)} %meet.1.refs_4_), custom_call_target="tpu_custom_call" | custom-call | flops 1000 | bytes 1000 | tf_op jit(solution)/shard_map/place_columns/pallas_call | solution.py:473
  (92 shorter events, 2.7 us)
Async XLA Ops:
  0.6 25.0 %collective-permute-start.3 = (bf16[384,3072]{1,0:T(8,128)(2,1)}, bf16[384,3072]{1,0:T(8,128)(2,1)}, u32[]{:S(2)}, u32[]{:S(2)}) collective-permute-start(bf16[384,3072]{1,0:T(8,128)(2,1)} %bitcast.46), channel_id=1, source_target_pairs={{0,8},{1,9},{2,10},{3,11},{4,12},{5,13},{6,14},{7,15},{8,0},{9,1},... | collective-permute-start | bytes 7077896 | tf_op jit(solution)/shard_map/ppermute | solution.py:42
  0.7 17.7 %collective-permute-start.9 = (bf16[96,3072]{1,0:T(8,128)(2,1)}, bf16[96,3072]{1,0:T(8,128)(2,1)S(1)}, u32[]{:S(2)}, u32[]{:S(2)}) collective-permute-start(bf16[96,3072]{1,0:T(8,128)(2,1)} %refs_4_.1), channel_id=1, source_target_pairs={{0,68},{1,69},{2,70},{3,71},{4,64},{5,65},{6,66},{7,67},{8,76},{9,... | collective-permute-start | bytes 1769480 | tf_op jit(solution)/shard_map/ppermute | solution.py:42
  3.6 17.9 %collective-permute-start.2 = (bf16[96,3072]{1,0:T(8,128)(2,1)}, bf16[96,3072]{1,0:T(8,128)(2,1)S(1)}, u32[]{:S(2)}, u32[]{:S(2)}) collective-permute-start(bf16[96,3072]{1,0:T(8,128)(2,1)} %refs_4_.1), channel_id=1, source_target_pairs={{0,16},{1,17},{2,18},{3,19},{4,20},{5,21},{6,22},{7,23},{8,24},{9,... | collective-permute-start | bytes 1769480 | tf_op jit(solution)/shard_map/ppermute | solution.py:42
  7.1 10.0 %copy-start = (bf16[1,384,3072]{2,1,0:T(8,128)(2,1)S(1)}, bf16[1,384,3072]{2,1,0:T(8,128)(2,1)}, u32[]{:S(2)}) copy-start(bf16[1,384,3072]{2,1,0:T(8,128)(2,1)} %param.10) | copy-start | bytes 7077892
  10.2 30.0 %collective-permute-start.1 = (bf16[2,384,768]{2,1,0:T(8,128)(2,1)}, bf16[2,384,768]{2,1,0:T(8,128)(2,1)}, u32[]{:S(2)}, u32[]{:S(2)}) collective-permute-start(bf16[2,384,768]{2,1,0:T(8,128)(2,1)} %window.2), channel_id=1, source_target_pairs={{1,0},{2,1},{3,2},{4,3},{5,4},{6,5},{7,6},{9,8},{10,9},{11,10},{12... | collective-permute-start | bytes 3538952 | tf_op jit(solution)/shard_map/ppermute | solution.py:82
  11.5 29.8 %collective-permute-start = (bf16[2,384,768]{2,1,0:T(8,128)(2,1)}, bf16[2,384,768]{2,1,0:T(8,128)(2,1)}, u32[]{:S(2)}, u32[]{:S(2)}) collective-permute-start(bf16[2,384,768]{2,1,0:T(8,128)(2,1)} %window.2), channel_id=1, source_target_pairs={{0,1},{1,2},{2,3},{3,4},{4,5},{5,6},{6,7},{8,9},{9,10},{10,11},{11... | collective-permute-start | bytes 3538952 | tf_op jit(solution)/shard_map/ppermute | solution.py:78
  18.4 0.8 copy-start.2
  19.3 74.7 %collective-permute-start.17 = (bf16[384,3072]{1,0:T(8,128)(2,1)}, bf16[384,3072]{1,0:T(8,128)(2,1)S(1)}, u32[]{:S(2)}, u32[]{:S(2)}) collective-permute-start(bf16[384,3072]{1,0:T(8,128)(2,1)} %hold.10), channel_id=1, source_target_pairs={{0,68},{1,69},{2,70},{3,71},{4,64},{5,65},{6,66},{7,67},{8,76},{9,... | collective-permute-start | bytes 7077896 | tf_op jit(solution)/shard_map/ppermute | solution.py:42
  21.6 4.0 %copy-start.1 = (bf16[96,3072]{1,0:T(8,128)(2,1)}, bf16[96,3072]{1,0:T(8,128)(2,1)S(1)}, u32[]{:S(2)}) copy-start(bf16[96,3072]{1,0:T(8,128)(2,1)S(1)} %collective-permute-done.2.x_ref) | copy-start | bytes 1769476
  21.6 16.5 %collective-permute-start.4 = (bf16[96,3072]{1,0:T(8,128)(2,1)}, bf16[96,3072]{1,0:T(8,128)(2,1)S(1)}, u32[]{:S(2)}, u32[]{:S(2)}) collective-permute-start(bf16[96,3072]{1,0:T(8,128)(2,1)} %refs_4_.1), channel_id=1, source_target_pairs={{0,48},{1,49},{2,50},{3,51},{4,52},{5,53},{6,54},{7,55},{8,56},{9,... | collective-permute-start | bytes 1769480 | tf_op jit(solution)/shard_map/ppermute | solution.py:42
  25.6 25.4 %collective-permute-start.7 = (bf16[96,3072]{1,0:T(8,128)(2,1)}, bf16[96,3072]{1,0:T(8,128)(2,1)}, u32[]{:S(2)}, u32[]{:S(2)}) collective-permute-start(bf16[96,3072]{1,0:T(8,128)(2,1)} %hold.6.rest_0_.rest_2_.refs_1_.refs_5_), channel_id=1, source_target_pairs={{0,16},{1,17},{2,18},{3,19},{4,20},{5,21},{6,22},{7,23},{8,24},{9,... | collective-permute-start | bytes 1769480 | tf_op jit(solution)/shard_map/ppermute | solution.py:42
  38.0 3.3 %copy-start.7 = (bf16[96,3072]{1,0:T(8,128)(2,1)}, bf16[96,3072]{1,0:T(8,128)(2,1)S(1)}, u32[]{:S(2)}) copy-start(bf16[96,3072]{1,0:T(8,128)(2,1)S(1)} %collective-permute-done.4.rest_3_.refs_2_.refs_6_) | copy-start | bytes 1769476
  41.3 2.4 %copy-start.4 = (bf16[2,384,768]{2,1,0:T(8,128)(2,1)S(1)}, bf16[2,384,768]{2,1,0:T(8,128)(2,1)}, u32[]{:S(2)}) copy-start(bf16[2,384,768]{2,1,0:T(8,128)(2,1)} %hold.7.rest_0_) | copy-start | bytes 3538948
  41.3 26.2 %collective-permute-start.11 = (bf16[96,3072]{1,0:T(8,128)(2,1)}, bf16[96,3072]{1,0:T(8,128)(2,1)}, u32[]{:S(2)}, u32[]{:S(2)}) collective-permute-start(bf16[96,3072]{1,0:T(8,128)(2,1)} %hold.8.refs_0_.refs_8_), channel_id=1, source_target_pairs={{0,48},{1,49},{2,50},{3,51},{4,52},{5,53},{6,54},{7,55},{8,56},{9,... | collective-permute-start | bytes 1769480 | tf_op jit(solution)/shard_map/ppermute | solution.py:42
  43.7 41.3 %collective-permute-start.6 = (bf16[2,384,768]{2,1,0:T(8,128)(2,1)S(1)}, bf16[2,384,768]{2,1,0:T(8,128)(2,1)}, u32[]{:S(2)}, u32[]{:S(2)}) collective-permute-start(bf16[2,384,768]{2,1,0:T(8,128)(2,1)S(1)} %copy-done.4), channel_id=1, source_target_pairs={{1,0},{2,1},{3,2},{4,3},{5,4},{6,5},{7,6},{9,8},{10,9},{11,10},{12... | collective-permute-start | bytes 3538952 | tf_op jit(solution)/shard_map/ppermute | solution.py:82
  45.0 40.0 %collective-permute-start.5 = (bf16[2,384,768]{2,1,0:T(8,128)(2,1)S(1)}, bf16[2,384,768]{2,1,0:T(8,128)(2,1)}, u32[]{:S(2)}, u32[]{:S(2)}) collective-permute-start(bf16[2,384,768]{2,1,0:T(8,128)(2,1)S(1)} %copy-done.4), channel_id=1, source_target_pairs={{0,1},{1,2},{2,3},{3,4},{4,5},{5,6},{6,7},{8,9},{9,10},{10,11},{11... | collective-permute-start | bytes 3538952 | tf_op jit(solution)/shard_map/ppermute | solution.py:78
  51.0 18.9 %collective-permute-start.10 = (bf16[96,3072]{1,0:T(8,128)(2,1)}, bf16[96,3072]{1,0:T(8,128)(2,1)}, u32[]{:S(2)}, u32[]{:S(2)}) collective-permute-start(bf16[96,3072]{1,0:T(8,128)(2,1)} %hold.8.refs_0_.refs_8_), channel_id=1, source_target_pairs={{0,16},{1,17},{2,18},{3,19},{4,20},{5,21},{6,22},{7,23},{8,24},{9,... | collective-permute-start | bytes 1769480 | tf_op jit(solution)/shard_map/ppermute | solution.py:42
  51.8 8.3 %copy-start.3 = (bf16[96,3072]{1,0:T(8,128)(2,1)S(1)}, bf16[96,3072]{1,0:T(8,128)(2,1)}, u32[]{:S(2)}) copy-start(bf16[96,3072]{1,0:T(8,128)(2,1)} %hold.8.refs_0_.refs_8_) | copy-start | bytes 1769476
  67.5 17.4 %collective-permute-start.12 = (bf16[96,3072]{1,0:T(8,128)(2,1)}, bf16[96,3072]{1,0:T(8,128)(2,1)S(1)}, u32[]{:S(2)}, u32[]{:S(2)}) collective-permute-start(bf16[96,3072]{1,0:T(8,128)(2,1)} %hold.9), channel_id=1, source_target_pairs={{0,32},{1,33},{2,34},{3,35},{4,36},{5,37},{6,38},{7,39},{8,40},{9,... | collective-permute-start | bytes 1769480 | tf_op jit(solution)/shard_map/ppermute | solution.py:42
  70.0 1.9 collective-permute-start.8
  84.9 0.8 copy-start.8
  93.9 1.4 copy-start.5
  95.4 1.1 copy-start.9
  95.4 2.0 copy-start.6
  95.4 39.1 %collective-permute-start.18 = (bf16[384,3072]{1,0:T(8,128)(2,1)}, bf16[384,3072]{1,0:T(8,128)(2,1)}, u32[]{:S(2)}, u32[]{:S(2)}) collective-permute-start(bf16[384,3072]{1,0:T(8,128)(2,1)} %hold.11.refs_6_), channel_id=1, source_target_pairs={{0,8},{1,9},{2,10},{3,11},{4,12},{5,13},{6,14},{7,15},{8,0},{9,1},... | collective-permute-start | bytes 7077896 | tf_op jit(solution)/shard_map/ppermute | solution.py:42
  97.2 10.5 %collective-permute-start.13 = (bf16[384,384]{1,0:T(8,128)(2,1)S(1)}, bf16[384,384]{1,0:T(8,128)(2,1)S(1)}, u32[]{:S(2)}, u32[]{:S(2)}) collective-permute-start(bf16[384,384]{1,0:T(8,128)(2,1)S(1)} %bitcast.67), channel_id=1, source_target_pairs={{0,8},{1,9},{2,10},{3,11},{4,12},{5,13},{6,14},{7,15},{8,0},{9,1},... | collective-permute-start | bytes 884744 | tf_op jit(solution)/shard_map/ppermute | solution.py:42
  97.4 7.0 %copy-start.23 = (bf16[4,1,96,384]{3,2,1,0:T(8,128)(2,1)}, bf16[4,1,96,384]{3,2,1,0:T(8,128)(2,1)S(1)}, u32[]{:S(2)}) copy-start(bf16[4,1,96,384]{3,2,1,0:T(8,128)(2,1)S(1)} %get-tuple-element.67) | copy-start | bytes 884740
  97.5 11.6 %copy-start.16 = (bf16[4,1,96,384]{3,2,1,0:T(8,128)(2,1)}, bf16[4,1,96,384]{3,2,1,0:T(8,128)(2,1)S(1)}, u32[]{:S(2)}) copy-start(bf16[4,1,96,384]{3,2,1,0:T(8,128)(2,1)S(1)} %get-tuple-element.68) | copy-start | bytes 884740
  97.5 11.6 %collective-permute-start.14 = (bf16[384,384]{1,0:T(8,128)(2,1)S(1)}, bf16[384,384]{1,0:T(8,128)(2,1)S(1)}, u32[]{:S(2)}, u32[]{:S(2)}) collective-permute-start(bf16[384,384]{1,0:T(8,128)(2,1)S(1)} %bitcast.65), channel_id=1, source_target_pairs={{0,8},{1,9},{2,10},{3,11},{4,12},{5,13},{6,14},{7,15},{8,0},{9,1},... | collective-permute-start | bytes 884744 | tf_op jit(solution)/shard_map/ppermute | solution.py:42
  104.5 13.2 %collective-permute-start.19 = (bf16[384,384]{1,0:T(8,128)(2,1)}, bf16[384,384]{1,0:T(8,128)(2,1)S(1)}, u32[]{:S(2)}, u32[]{:S(2)}) collective-permute-start(bf16[384,384]{1,0:T(8,128)(2,1)} %get-tuple-element.43), channel_id=1, source_target_pairs={{0,8},{1,9},{2,10},{3,11},{4,12},{5,13},{6,14},{7,15},{8,0},{9,1},... | collective-permute-start | bytes 884744 | tf_op jit(solution)/shard_map/ppermute | solution.py:42
  104.6 39.8 %collective-permute-start.20 = (bf16[2,384,768]{2,1,0:T(8,128)(2,1)}, bf16[2,384,768]{2,1,0:T(8,128)(2,1)S(1)}, u32[]{:S(2)}, u32[]{:S(2)}) collective-permute-start(bf16[2,384,768]{2,1,0:T(8,128)(2,1)} %get-tuple-element.48), channel_id=1, source_target_pairs={{0,1},{1,2},{2,3},{3,4},{4,5},{5,6},{6,7},{8,9},{9,10},{10,11},{11... | collective-permute-start | bytes 3538952 | tf_op jit(solution)/shard_map/ppermute | solution.py:78
  107.7 23.8 %copy-start.12 = (bf16[384,384]{1,0:T(8,128)(2,1)}, bf16[384,384]{1,0:T(8,128)(2,1)S(1)}, u32[]{:S(2)}) copy-start(bf16[384,384]{1,0:T(8,128)(2,1)S(1)} %collective-permute-done.13.refs_1_.refs_2_) | copy-start | bytes 884740
  107.8 39.0 %collective-permute-start.21 = (bf16[2,384,768]{2,1,0:T(8,128)(2,1)}, bf16[2,384,768]{2,1,0:T(8,128)(2,1)S(1)}, u32[]{:S(2)}, u32[]{:S(2)}) collective-permute-start(bf16[2,384,768]{2,1,0:T(8,128)(2,1)} %get-tuple-element.49), channel_id=1, source_target_pairs={{1,0},{2,1},{3,2},{4,3},{5,4},{6,5},{7,6},{9,8},{10,9},{11,10},{12... | collective-permute-start | bytes 3538952 | tf_op jit(solution)/shard_map/ppermute | solution.py:82
  109.1 8.7 %copy-start.13 = (bf16[384,384]{1,0:T(8,128)(2,1)}, bf16[384,384]{1,0:T(8,128)(2,1)S(1)}, u32[]{:S(2)}) copy-start(bf16[384,384]{1,0:T(8,128)(2,1)S(1)} %collective-permute-done.14.rest_1_.refs_3_) | copy-start | bytes 884740
  109.1 22.5 %collective-permute-start.15 = (bf16[384,384]{1,0:T(8,128)(2,1)S(1)}, bf16[384,384]{1,0:T(8,128)(2,1)S(1)}, u32[]{:S(2)}, u32[]{:S(2)}) collective-permute-start(bf16[384,384]{1,0:T(8,128)(2,1)S(1)} %bitcast.62), channel_id=1, source_target_pairs={{0,68},{1,69},{2,70},{3,71},{4,64},{5,65},{6,66},{7,67},{8,76},{9,... | collective-permute-start | bytes 884744 | tf_op jit(solution)/shard_map/ppermute | solution.py:42
  117.7 0.7 copy-start.22
  117.7 15.4 %collective-permute-start.16 = (bf16[384,384]{1,0:T(8,128)(2,1)}, bf16[384,384]{1,0:T(8,128)(2,1)S(1)}, u32[]{:S(2)}, u32[]{:S(2)}) collective-permute-start(bf16[384,384]{1,0:T(8,128)(2,1)} %bitcast.66), channel_id=1, source_target_pairs={{0,76},{1,77},{2,78},{3,79},{4,72},{5,73},{6,74},{7,75},{8,68},{9,... | collective-permute-start | bytes 884744 | tf_op jit(solution)/shard_map/ppermute | solution.py:42
  131.5 2.9 %copy-start.20 = (bf16[384,384]{1,0:T(8,128)(2,1)}, bf16[384,384]{1,0:T(8,128)(2,1)S(1)}, u32[]{:S(2)}) copy-start(bf16[384,384]{1,0:T(8,128)(2,1)S(1)} %collective-permute-done.15.refs_2_) | copy-start | bytes 884740
  131.6 27.4 %collective-permute-start.24 = (bf16[2,384,768]{2,1,0:T(8,128)(2,1)}, bf16[2,384,768]{2,1,0:T(8,128)(2,1)S(1)}, u32[]{:S(2)}, u32[]{:S(2)}) collective-permute-start(bf16[2,384,768]{2,1,0:T(8,128)(2,1)} %get-tuple-element.54), channel_id=1, source_target_pairs={{0,1},{1,2},{2,3},{3,4},{4,5},{5,6},{6,7},{8,9},{9,10},{10,11},{11... | collective-permute-start | bytes 3538952 | tf_op jit(solution)/shard_map/ppermute | solution.py:78
  133.2 1.3 copy-start.21
  133.2 30.3 %collective-permute-start.25 = (bf16[2,384,768]{2,1,0:T(8,128)(2,1)}, bf16[2,384,768]{2,1,0:T(8,128)(2,1)}, u32[]{:S(2)}, u32[]{:S(2)}) collective-permute-start(bf16[2,384,768]{2,1,0:T(8,128)(2,1)} %get-tuple-element.55), channel_id=1, source_target_pairs={{1,0},{2,1},{3,2},{4,3},{5,4},{6,5},{7,6},{9,8},{10,9},{11,10},{12... | collective-permute-start | bytes 3538952 | tf_op jit(solution)/shard_map/ppermute | solution.py:82
  143.5 27.2 %collective-permute-start.26 = (bf16[96,3072]{1,0:T(8,128)(2,1)}, bf16[96,3072]{1,0:T(8,128)(2,1)S(1)}, u32[]{:S(2)}, u32[]{:S(2)}) collective-permute-start(bf16[96,3072]{1,0:T(8,128)(2,1)} %get-tuple-element.60), channel_id=1, source_target_pairs={{0,16},{1,17},{2,18},{3,19},{4,20},{5,21},{6,22},{7,23},{8,24},{9,... | collective-permute-start | bytes 1769480 | tf_op jit(solution)/shard_map/ppermute | solution.py:42
  144.4 2.6 %copy-start.10 = (bf16[2,384,768]{2,1,0:T(8,128)(2,1)}, bf16[2,384,768]{2,1,0:T(8,128)(2,1)S(1)}, u32[]{:S(2)}) copy-start(bf16[2,384,768]{2,1,0:T(8,128)(2,1)S(1)} %collective-permute-done.20.refs_13_.a_ref) | copy-start | bytes 3538948
  144.4 27.4 %collective-permute-start.27 = (bf16[96,3072]{1,0:T(8,128)(2,1)}, bf16[96,3072]{1,0:T(8,128)(2,1)}, u32[]{:S(2)}, u32[]{:S(2)}) collective-permute-start(bf16[96,3072]{1,0:T(8,128)(2,1)} %get-tuple-element.61), channel_id=1, source_target_pairs={{0,48},{1,49},{2,50},{3,51},{4,52},{5,53},{6,54},{7,55},{8,56},{9,... | collective-permute-start | bytes 1769480 | tf_op jit(solution)/shard_map/ppermute | solution.py:42
  146.8 1.0 copy-start.11
  146.8 25.8 %collective-permute-start.28 = (bf16[96,3072]{1,0:T(8,128)(2,1)}, bf16[96,3072]{1,0:T(8,128)(2,1)}, u32[]{:S(2)}, u32[]{:S(2)}) collective-permute-start(bf16[96,3072]{1,0:T(8,128)(2,1)} %get-tuple-element.62), channel_id=1, source_target_pairs={{0,32},{1,33},{2,34},{3,35},{4,36},{5,37},{6,38},{7,39},{8,40},{9,... | collective-permute-start | bytes 1769480 | tf_op jit(solution)/shard_map/ppermute | solution.py:42
  159.0 8.1 %copy-start.17 = (bf16[2,384,768]{2,1,0:T(8,128)(2,1)}, bf16[2,384,768]{2,1,0:T(8,128)(2,1)S(1)}, u32[]{:S(2)}) copy-start(bf16[2,384,768]{2,1,0:T(8,128)(2,1)S(1)} %collective-permute-done.24.a_ref) | copy-start | bytes 3538948
  159.0 43.5 %collective-permute-start.22 = (bf16[384,1536]{1,0:T(8,128)(2,1)}, bf16[384,1536]{1,0:T(8,128)(2,1)S(1)}, u32[]{:S(2)}, u32[]{:S(2)}) collective-permute-start(bf16[384,1536]{1,0:T(8,128)(2,1)} %get-tuple-element.51), channel_id=1, source_target_pairs={{0,8},{1,9},{2,10},{3,11},{4,12},{5,13},{6,14},{7,15},{8,0},{9,1},... | collective-permute-start | bytes 3538952 | tf_op jit(solution)/shard_map/ppermute | solution.py:42
  163.4 39.0 %collective-permute-start.23 = (bf16[384,1536]{1,0:T(8,128)(2,1)}, bf16[384,1536]{1,0:T(8,128)(2,1)S(1)}, u32[]{:S(2)}, u32[]{:S(2)}) collective-permute-start(bf16[384,1536]{1,0:T(8,128)(2,1)} %get-tuple-element.52), channel_id=1, source_target_pairs={{0,8},{1,9},{2,10},{3,11},{4,12},{5,13},{6,14},{7,15},{8,0},{9,1},... | collective-permute-start | bytes 3538952 | tf_op jit(solution)/shard_map/ppermute | solution.py:42
  170.7 1.9 copy-start.18
  175.2 12.7 %collective-permute-start.29 = (bf16[96,768]{1,0:T(8,128)(2,1)}, bf16[96,768]{1,0:T(8,128)(2,1)S(1)}, u32[]{:S(2)}, u32[]{:S(2)}) collective-permute-start(bf16[96,768]{1,0:T(8,128)(2,1)} %get-tuple-element.64), channel_id=1, source_target_pairs={{0,1},{1,2},{2,3},{3,0},{4,5},{5,6},{6,7},{7,4},{8,9},{9,10},{10,1... | collective-permute-start | bytes 442376 | tf_op jit(solution)/shard_map/ppermute | solution.py:42
  178.7 11.7 %collective-permute-start.30 = (bf16[96,768]{1,0:T(8,128)(2,1)}, bf16[96,768]{1,0:T(8,128)(2,1)S(1)}, u32[]{:S(2)}, u32[]{:S(2)}) collective-permute-start(bf16[96,768]{1,0:T(8,128)(2,1)} %get-tuple-element.65), channel_id=1, source_target_pairs={{0,3},{1,0},{2,1},{3,2},{4,7},{5,4},{6,5},{7,6},{8,11},{9,8},{10,9... | collective-permute-start | bytes 442376 | tf_op jit(solution)/shard_map/ppermute | solution.py:42
  183.2 9.1 %collective-permute-start.31 = (bf16[96,768]{1,0:T(8,128)(2,1)}, bf16[96,768]{1,0:T(8,128)(2,1)S(1)}, u32[]{:S(2)}, u32[]{:S(2)}) collective-permute-start(bf16[96,768]{1,0:T(8,128)(2,1)} %get-tuple-element.66), channel_id=1, source_target_pairs={{0,2},{1,3},{2,0},{3,1},{4,6},{5,7},{6,4},{7,5},{8,10},{9,11},{10,... | collective-permute-start | bytes 442376 | tf_op jit(solution)/shard_map/ppermute | solution.py:42
  193.3 5.6 %collective-permute-start.32 = (bf16[96,768]{1,0:T(8,128)(2,1)S(1)}, bf16[96,768]{1,0:T(8,128)(2,1)S(1)}, u32[]{:S(2)}, u32[]{:S(2)}) collective-permute-start(bf16[96,768]{1,0:T(8,128)(2,1)S(1)} %add_convert_fusion.1), channel_id=1, source_target_pairs={{0,4},{1,5},{2,6},{3,7},{4,0},{5,1},{6,2},{7,3},{8,12},{9,13},{10,... | collective-permute-start | bytes 442376 | tf_op jit(solution)/shard_map/ppermute | solution.py:42
  198.9 9.6 %copy-start.19 = (bf16[96,768]{1,0:T(8,128)(2,1)}, bf16[96,768]{1,0:T(8,128)(2,1)S(1)}, u32[]{:S(2)}) copy-start(bf16[96,768]{1,0:T(8,128)(2,1)S(1)} %add_convert_fusion.refs_0_) | copy-start | bytes 442372
  198.9 9.6 %collective-permute-start.35 = (bf16[96,768]{1,0:T(8,128)(2,1)S(1)}, bf16[96,768]{1,0:T(8,128)(2,1)S(1)}, u32[]{:S(2)}, u32[]{:S(2)}) collective-permute-start(bf16[96,768]{1,0:T(8,128)(2,1)S(1)} %add_convert_fusion.refs_0_), channel_id=1, source_target_pairs={{0,2},{1,3},{2,0},{3,1},{4,6},{5,7},{6,4},{7,5},{8,10},{9,11},{10,... | collective-permute-start | bytes 442376 | tf_op jit(solution)/shard_map/ppermute | solution.py:42
  199.0 9.5 %collective-permute-start.34 = (bf16[96,768]{1,0:T(8,128)(2,1)S(1)}, bf16[96,768]{1,0:T(8,128)(2,1)S(1)}, u32[]{:S(2)}, u32[]{:S(2)}) collective-permute-start(bf16[96,768]{1,0:T(8,128)(2,1)S(1)} %add_convert_fusion.refs_0_), channel_id=1, source_target_pairs={{0,3},{1,0},{2,1},{3,2},{4,7},{5,4},{6,5},{7,6},{8,11},{9,8},{10,9... | collective-permute-start | bytes 442376 | tf_op jit(solution)/shard_map/ppermute | solution.py:42
  202.4 6.4 %collective-permute-start.33 = (bf16[96,768]{1,0:T(8,128)(2,1)S(1)}, bf16[96,768]{1,0:T(8,128)(2,1)S(1)}, u32[]{:S(2)}, u32[]{:S(2)}) collective-permute-start(bf16[96,768]{1,0:T(8,128)(2,1)S(1)} %add_convert_fusion.refs_0_), channel_id=1, source_target_pairs={{0,1},{1,2},{2,3},{3,0},{4,5},{5,6},{6,7},{7,4},{8,9},{9,10},{10,1... | collective-permute-start | bytes 442376 | tf_op jit(solution)/shard_map/ppermute | solution.py:42
  202.4 1.0 copy-start.14
  202.5 1.4 copy-start.15
  208.5 0.7 copy-start.24
  208.5 0.7 copy-start.25
  209.2 0.7 copy-start.26

commit v5 on v4

--- a/solution.py
+++ b/solution.py
@@ -561,7 +561,7 @@
     done = join(0, info, own0, *sent0, heads, cols, None)
     done = join(1, info, own1, *sent1, heads, cols, done)
 
-    columns = sum_columns(info, (pieces[0],) + tuple(move_z(pieces[i], i) for i in (1, 3, 2)), done)
+    columns = sum_columns(info, (pieces[0],) + tuple(move_z(pieces[i], i) for i in (1, 3, 2)), sent1)
     mine = add(columns[0], *[move_y(columns[i], i) for i in (1, 3, 2)]).astype(BF)
     mine = add(mine, move_lo(mine)).astype(BF)
     gathered = [mine] + [move_y(mine, i) for i in (1, 3, 2)]

time: 213 us -> 220 us (1.033)
  waiting for transfers between devices: 35.7 us -> 44.3 us
  starting transfers between devices: 64.8 us -> 60.1 us
  local copies, waits for them, and re-layouts: 12.6 us -> 14.8 us
    ppermute x28, waiting for transfers between devices: 26.3 us -> 29.6 us  [move(): return lax.ppermute(x, ('dp', 'space'), moves(change))]
    ppermute x4, waiting for transfers between devices: 6.53 us -> 9.41 us  [to_previous(): return lax.ppermute(x, 'space', [(i + 1, i) for i in range(NS - 1)])]
    ppermute x28, starting transfers between devices: 43.3 us -> 40.8 us  [move(): return lax.ppermute(x, ('dp', 'space'), moves(change))]
    ppermute x4, waiting for transfers between devices: 2.9 us -> 5.26 us  [to_next(): return lax.ppermute(x, 'space', [(i, i + 1) for i in range(NS - 1)])]
    unnamed x57 -> x53, local copies, waits for them, and re-layouts: 10.9 us -> 12.6 us
  transfers between devices with their start and end apart: 36 -> 36, of which waited for: 13 -> 12; matrix products, arithmetic and copies ran while one was open for 3% -> 3% of each run, Pallas kernels for 45% -> 43%
where the time goes in v5:
time: 220 us; the launch traced here: 218 us
  Pallas kernels  97 us (44%)
  starting transfers between devices  60.1 us (27%)
  waiting for transfers between devices  44.3 us (20%)
  local copies, waits for them, and re-layouts  14.8 us (7%)
    ppermute x28, starting transfers between devices, move(): return lax.ppermute(x, ('dp', 'space'), moves(change))  40.8 us
    ppermute x28, waiting for transfers between devices, move(): return lax.ppermute(x, ('dp', 'space'), moves(change))  29.6 us
    pallas_call x2, Pallas kernels, attend_back(): pl.pallas_call(functools.partial(backward_kernel, per, part), out_shape=(...  26.2 us
    pallas_call x2, Pallas kernels, attend(): pl.pallas_call(functools.partial(forward_kernel, per, part), out_shape=(j...  16.5 us
    ppermute x4, starting transfers between devices, to_next(): return lax.ppermute(x, 'space', [(i, i + 1) for i in range(NS - 1)])  14.2 us
    pallas_call x2, Pallas kernels, project_back(): pl.pallas_call(project_back_kernel, out_shape=(jax.ShapeDtypeStruct((NZ *...  13.2 us
    unnamed x53, local copies, waits for them, and re-layouts  12.6 us
    pallas_call x1, Pallas kernels, project(): pl.pallas_call(project_kernel, out_shape=(jax.ShapeDtypeStruct((tokens, w...  9.44 us
  transfers between devices with their start and end apart: 36, of which 12 were waited for; matrix products, arithmetic and copies ran while one was open for 3% of the time, Pallas kernels for 43%

profile of v5, /device:TPU:0, one launch (start us, length us, event | category | flops | bytes accessed | tf_op | source)
XLA Modules:
  0.0 218.3 jit_solution(17066186847257858697)
XLA Ops:
  0.7 2.9 %collective-permute-start.9 = (bf16[96,3072]{1,0:T(8,128)(2,1)}, bf16[96,3072]{1,0:T(8,128)(2,1)S(1)}, u32[]{:S(2)}, u32[]{:S(2)}) collective-permute-start(bf16[96,3072]{1,0:T(8,128)(2,1)} %refs_4_.1), channel_id=1, source_target_pairs={{0,68},{1,69},{2,70},{3,71},{4,64},{5,65},{6,66},{7,67},{8,76},{9,... | collective-permute-start | bytes 1769480 | tf_op jit(solution)/shard_map/ppermute | solution.py:42
  3.6 1.9 collective-permute-start.2
  5.6 0.8 copy.25
  7.0 3.1 %window.2 = bf16[2,384,768]{2,1,0:T(8,128)(2,1)} custom-call(s32[44]{0:T(128)} %concatenate.3.info.place.spots, bf16[384,1536]{1,0:T(8,128)(2,1)} %bitcast.34, bf16[384,1536]{1,0:T(8,128)(2,1)} %bitcast.40), custom_call_target="tpu_custom_call" | custom-call | flops 1000 | bytes 1000 | tf_op jit(solution)/shard_map/window/pallas_call | solution.py:300
  10.1 4.6 %collective-permute-start = (bf16[2,384,768]{2,1,0:T(8,128)(2,1)}, bf16[2,384,768]{2,1,0:T(8,128)(2,1)}, u32[]{:S(2)}, u32[]{:S(2)}) collective-permute-start(bf16[2,384,768]{2,1,0:T(8,128)(2,1)} %window.2), channel_id=1, source_target_pairs={{0,1},{1,2},{2,3},{3,4},{4,5},{5,6},{6,7},{8,9},{9,10},{10,11},{11... | collective-permute-start | bytes 3538952 | tf_op jit(solution)/shard_map/ppermute | solution.py:78
  14.7 1.3 collective-permute-start.1
  16.0 1.4 copy.38.x_ref
  17.9 0.8 copy-done.2
  18.7 2.8 %collective-permute-start.17 = (bf16[384,3072]{1,0:T(8,128)(2,1)}, bf16[384,3072]{1,0:T(8,128)(2,1)S(1)}, u32[]{:S(2)}, u32[]{:S(2)}) collective-permute-start(bf16[384,3072]{1,0:T(8,128)(2,1)} %hold.10), channel_id=1, source_target_pairs={{0,68},{1,69},{2,70},{3,71},{4,64},{5,65},{6,66},{7,67},{8,76},{9,... | collective-permute-start | bytes 7077896 | tf_op jit(solution)/shard_map/ppermute | solution.py:42
  21.6 4.0 %collective-permute-start.4 = (bf16[96,3072]{1,0:T(8,128)(2,1)}, bf16[96,3072]{1,0:T(8,128)(2,1)S(1)}, u32[]{:S(2)}, u32[]{:S(2)}) collective-permute-start(bf16[96,3072]{1,0:T(8,128)(2,1)} %refs_4_.1), channel_id=1, source_target_pairs={{0,48},{1,49},{2,50},{3,51},{4,52},{5,53},{6,54},{7,55},{8,56},{9,... | collective-permute-start | bytes 1769480 | tf_op jit(solution)/shard_map/ppermute | solution.py:42
  25.6 2.9 %window.3.x_ref = bf16[2,384,768]{2,1,0:T(8,128)(2,1)} custom-call(s32[44]{0:T(128)} %concatenate.3.info.place.spots, bf16[384,1536]{1,0:T(8,128)(2,1)} %bitcast.35, bf16[384,1536]{1,0:T(8,128)(2,1)} %bitcast.41, bf16[96,3072]{1,0:T(8,128)(2,1)} %hold.6.rest_0_.rest_2_.refs_1_.refs_5_), custom_call_target="tpu_custom_call" | custom-call | flops 1000 | bytes 1000 | tf_op jit(solution)/shard_map/window/pallas_call | solution.py:300
  28.6 9.6 %collective-permute-done.4.rest_3_.refs_2_.refs_6_ = bf16[96,3072]{1,0:T(8,128)(2,1)S(1)} collective-permute-done((bf16[96,3072]{1,0:T(8,128)(2,1)}, bf16[96,3072]{1,0:T(8,128)(2,1)S(1)}, u32[]{:S(2)}, u32[]{:S(2)}) %collective-permute-start.4) | collective-permute-done | bytes 589856 | tf_op jit(solution)/shard_map/ppermute | solution.py:42
  38.1 1.0 collective-permute-done.left_ref.rest_0_
  39.1 5.2 %collective-permute-done.1.right_ref.rest_1_ = bf16[2,384,768]{2,1,0:T(8,128)(2,1)} collective-permute-done((bf16[2,384,768]{2,1,0:T(8,128)(2,1)}, bf16[2,384,768]{2,1,0:T(8,128)(2,1)}, u32[]{:S(2)}, u32[]{:S(2)}) %collective-permute-start.1) | collective-permute-done | bytes 1179680 | tf_op jit(solution)/shard_map/ppermute | solution.py:82
  44.4 1.9 collective-permute-start.10
  46.3 3.4 %collective-permute-start.5 = (bf16[2,384,768]{2,1,0:T(8,128)(2,1)S(1)}, bf16[2,384,768]{2,1,0:T(8,128)(2,1)}, u32[]{:S(2)}, u32[]{:S(2)}) collective-permute-start(bf16[2,384,768]{2,1,0:T(8,128)(2,1)S(1)} %copy-done.4), channel_id=1, source_target_pairs={{0,1},{1,2},{2,3},{3,4},{4,5},{5,6},{6,7},{8,9},{9,10},{10,11},{11... | collective-permute-start | bytes 3538952 | tf_op jit(solution)/shard_map/ppermute | solution.py:78
  49.7 1.3 collective-permute-start.6
  51.0 1.8 collective-permute-start.11
  52.8 8.3 %attend.2 = (bf16[768,384]{1,0:T(8,128)(2,1)}, f32[6,1,384]{2,1,0:T(1,128)}) custom-call(s32[44]{0:T(128)} %concatenate.3.info.place.spots, bf16[384,1536]{1,0:T(8,128)(2,1)} %bitcast.51, bf16[384,1536]{1,0:T(8,128)(2,1)} %bitcast.36, bf16[384,1536]{1,0:T(8,128)(2,1)} %bitcast.42, bf16[2,384,768]{2,1,0:T(8,128)(2,1)} %collective-permute-done.left_ref.rest_0_, ...), custom_call_target="tpu_custom_call" | custom-call | flops 1000 | bytes 1000 | tf_op jit(solution)/shard_map/attend/pallas_call | solution.py:151
  61.1 0.8 copy.37.x_ref
  62.0 6.6 %project_back.2 = (bf16[384,384]{1,0:T(8,128)(2,1)}, bf16[384,384]{1,0:T(8,128)(2,1)}) custom-call(s32[44]{0:T(128)} %concatenate.3.info.place.spots, bf16[96,3072]{1,0:T(8,128)(2,1)} %refs_4_.1, bf16[96,3072]{1,0:T(8,128)(2,1)} %hold.6.rest_0_.rest_2_.refs_1_.refs_5_, bf16[96,3072]{1,0:T(8,128)(2,1)} %copy-done.7, ...), custom_call_target="tpu_custom_call" | custom-call | flops 1000 | bytes 1000 | tf_op jit(solution)/shard_map/project_back/pallas_call | solution.py:327
  68.5 1.9 collective-permute-start.12
  70.5 1.9 collective-permute-done.8.theirs_ref
  72.4 13.1 %attend_back.2 = (bf16[384,1536]{1,0:T(8,128)(2,1)}, bf16[2,384,768]{2,1,0:T(8,128)(2,1)}, bf16[2,384,768]{2,1,0:T(8,128)(2,1)}, bf16[2,384,768]{2,1,0:T(8,128)(2,1)}) custom-call(s32[44]{0:T(128)} %concatenate.3.info.place.spots, bf16[384,1536]{1,0:T(8,128)(2,1)} %bitcast.52, bf16[384,1536]{1,0:T(8,128)(2,1)} %bitcast.37, bf16[384,1536]{1,0:T(8,128)(2,1)} %bitcast.43, ...), custom_call_target="tpu_custom_call" | custom-call | flops 1000 | bytes 1000 | tf_op jit(solution)/shard_map/attend_back/pallas_call | solution.py:214
  85.5 0.8 copy-done.8
  86.3 8.2 %attend.3 = (bf16[768,384]{1,0:T(8,128)(2,1)}, f32[6,1,384]{2,1,0:T(1,128)}) custom-call(s32[44]{0:T(128)} %concatenate.3.info.place.spots, bf16[384,1536]{1,0:T(8,128)(2,1)} %bitcast.53, bf16[384,1536]{1,0:T(8,128)(2,1)} %bitcast.38, bf16[384,1536]{1,0:T(8,128)(2,1)} %bitcast.44, bf16[2,384,768]{2,1,0:T(8,128)(2,1)} %collective-permute-done.5.left_ref, ...), custom_call_target="tpu_custom_call" | custom-call | flops 1000 | bytes 1000 | tf_op jit(solution)/shard_map/attend/pallas_call | solution.py:151
  94.5 1.4 copy-done.5
  96.0 0.9 copy-done.9
  96.9 0.8 constant_dynamic-slice_fusion.1
  97.9 6.6 %project_back.3 = (bf16[384,384]{1,0:T(8,128)(2,1)}, bf16[384,384]{1,0:T(8,128)(2,1)}) custom-call(s32[44]{0:T(128)} %concatenate.3.info.place.spots, bf16[96,3072]{1,0:T(8,128)(2,1)} %hold.8.refs_0_.refs_8_, bf16[96,3072]{1,0:T(8,128)(2,1)} %collective-permute-done.10.rest_0_.refs_1_.refs_9_, ...), custom_call_target="tpu_custom_call" | custom-call | flops 1000 | bytes 1000 | tf_op jit(solution)/shard_map/project_back/pallas_call | solution.py:327
  104.8 0.8 constant_dynamic-slice_fusion
  105.8 4.6 %collective-permute-start.20 = (bf16[2,384,768]{2,1,0:T(8,128)(2,1)}, bf16[2,384,768]{2,1,0:T(8,128)(2,1)S(1)}, u32[]{:S(2)}, u32[]{:S(2)}) collective-permute-start(bf16[2,384,768]{2,1,0:T(8,128)(2,1)} %get-tuple-element.48), channel_id=1, source_target_pairs={{0,1},{1,2},{2,3},{3,4},{4,5},{5,6},{6,7},{8,9},{9,10},{10,11},{11... | collective-permute-start | bytes 3538952 | tf_op jit(solution)/shard_map/ppermute | solution.py:78
  110.4 1.3 collective-permute-start.21
  111.8 5.3 %collective-permute-start.15 = (bf16[384,384]{1,0:T(8,128)(2,1)S(1)}, bf16[384,384]{1,0:T(8,128)(2,1)S(1)}, u32[]{:S(2)}, u32[]{:S(2)}) collective-permute-start(bf16[384,384]{1,0:T(8,128)(2,1)S(1)} %bitcast.60), channel_id=1, source_target_pairs={{0,68},{1,69},{2,70},{3,71},{4,64},{5,65},{6,66},{7,67},{8,76},{9,... | collective-permute-start | bytes 884744 | tf_op jit(solution)/shard_map/ppermute | solution.py:42
  117.1 0.7 copy-done.14
  117.8 13.1 %attend_back.3 = (bf16[384,1536]{1,0:T(8,128)(2,1)}, bf16[2,384,768]{2,1,0:T(8,128)(2,1)}, bf16[2,384,768]{2,1,0:T(8,128)(2,1)}, bf16[2,384,768]{2,1,0:T(8,128)(2,1)}) custom-call(s32[44]{0:T(128)} %concatenate.3.info.place.spots, bf16[384,1536]{1,0:T(8,128)(2,1)} %bitcast.54, bf16[384,1536]{1,0:T(8,128)(2,1)} %bitcast.39, ...), custom_call_target="tpu_custom_call", output_to_operand_aliasing={{0}: (10, {})} | custom-call | flops 1000 | bytes 1000 | tf_op jit(solution)/shard_map/attend_back/pallas_call | solution.py:214
  131.7 1.6 collective-permute-start.24
  133.3 1.3 collective-permute-start.25
  134.6 9.1 %weight_grad.1 = (bf16[96,3072]{1,0:T(8,128)(2,1)}, bf16[96,3072]{1,0:T(8,128)(2,1)}, bf16[96,3072]{1,0:T(8,128)(2,1)}, bf16[96,3072]{1,0:T(8,128)(2,1)}) custom-call(s32[44]{0:T(128)} %concatenate.3.info.place.spots, bf16[384,384]{1,0:T(8,128)(2,1)} %bitcast.58, bf16[384,384]{1,0:T(8,128)(2,1)} %copy-done.13, bf16[384,384]{1,0:T(8,128)(2,1)} %copy-done.21, ...), custom_call_target="tpu_custom_call" | custom-call | flops 1000 | bytes 1000 | tf_op jit(solution)/shard_map/weight_grad/pallas_call | solution.py:420
  143.6 0.7 collective-permute-start.26
  144.3 2.6 %collective-permute-start.27 = (bf16[96,3072]{1,0:T(8,128)(2,1)}, bf16[96,3072]{1,0:T(8,128)(2,1)}, u32[]{:S(2)}, u32[]{:S(2)}) collective-permute-start(bf16[96,3072]{1,0:T(8,128)(2,1)} %get-tuple-element.61), channel_id=1, source_target_pairs={{0,48},{1,49},{2,50},{3,51},{4,52},{5,53},{6,54},{7,55},{8,56},{9,... | collective-permute-start | bytes 1769480 | tf_op jit(solution)/shard_map/ppermute | solution.py:42
  148.0 9.4 %project.1 = (bf16[384,3072]{1,0:T(8,128)(2,1)}, bf16[384,1536]{1,0:T(8,128)(2,1)}, bf16[384,1536]{1,0:T(8,128)(2,1)}) custom-call(s32[44]{0:T(128)} %concatenate.3.info.place.spots, bf16[384,384]{1,0:T(8,128)(2,1)} %bitcast.59, bf16[384,384]{1,0:T(8,128)(2,1)} %bitcast.61, bf16[384,384]{1,0:T(8,128)(2,1)} %copy-done.13, bf16[384,384]{1,0:T(8,128)(2,1)} %copy-done.14, ...), custom_call_target="tpu_custom_call" | custom-call | flops 1000 | bytes 1000 | tf_op jit(solution)/shard_map/project/pallas_call | solution.py:366
  157.4 4.3 %collective-permute-done.24.a_ref.refs_4_ = bf16[2,384,768]{2,1,0:T(8,128)(2,1)S(1)} collective-permute-done((bf16[2,384,768]{2,1,0:T(8,128)(2,1)}, bf16[2,384,768]{2,1,0:T(8,128)(2,1)S(1)}, u32[]{:S(2)}, u32[]{:S(2)}) %collective-permute-start.24) | collective-permute-done | bytes 1179680 | tf_op jit(solution)/shard_map/ppermute | solution.py:78
  161.7 4.2 %collective-permute-done.25.b_ref.refs_5_ = bf16[2,384,768]{2,1,0:T(8,128)(2,1)} collective-permute-done((bf16[2,384,768]{2,1,0:T(8,128)(2,1)}, bf16[2,384,768]{2,1,0:T(8,128)(2,1)}, u32[]{:S(2)}, u32[]{:S(2)}) %collective-permute-start.25) | collective-permute-done | bytes 1179680 | tf_op jit(solution)/shard_map/ppermute | solution.py:82
  165.9 7.5 %collective-permute-done.26.refs_1_ = bf16[96,3072]{1,0:T(8,128)(2,1)S(1)} collective-permute-done((bf16[96,3072]{1,0:T(8,128)(2,1)}, bf16[96,3072]{1,0:T(8,128)(2,1)S(1)}, u32[]{:S(2)}, u32[]{:S(2)}) %collective-permute-start.26) | collective-permute-done | bytes 589856 | tf_op jit(solution)/shard_map/ppermute | solution.py:42
  173.3 0.8 copy-done.18
  174.1 2.6 %sum_columns.1 = (f32[96,768]{1,0:T(8,128)}, bf16[96,768]{1,0:T(8,128)(2,1)}, bf16[96,768]{1,0:T(8,128)(2,1)}, bf16[96,768]{1,0:T(8,128)(2,1)}) custom-call(s32[44]{0:T(128)} %concatenate.3.info.place.spots, bf16[96,3072]{1,0:T(8,128)(2,1)} %get-tuple-element.47.refs_12_.refs_0_, bf16[96,3072]{1,0:T(8,128)(2,1)} %copy-done.18, ...), custom_call_target="tpu_custom_call" | custom-call | flops 1000 | bytes 1000 | tf_op jit(solution)/shard_map/sum_columns/pallas_call | solution.py:449
  176.8 2.4 %collective-permute-start.29 = (bf16[96,768]{1,0:T(8,128)(2,1)}, bf16[96,768]{1,0:T(8,128)(2,1)S(1)}, u32[]{:S(2)}, u32[]{:S(2)}) collective-permute-start(bf16[96,768]{1,0:T(8,128)(2,1)} %get-tuple-element.64), channel_id=1, source_target_pairs={{0,1},{1,2},{2,3},{3,0},{4,5},{5,6},{6,7},{7,4},{8,9},{9,10},{10,1... | collective-permute-start | bytes 442376 | tf_op jit(solution)/shard_map/ppermute | solution.py:42
  179.1 2.4 %collective-permute-start.30 = (bf16[96,768]{1,0:T(8,128)(2,1)}, bf16[96,768]{1,0:T(8,128)(2,1)S(1)}, u32[]{:S(2)}, u32[]{:S(2)}) collective-permute-start(bf16[96,768]{1,0:T(8,128)(2,1)} %get-tuple-element.65), channel_id=1, source_target_pairs={{0,3},{1,0},{2,1},{3,2},{4,7},{5,4},{6,5},{7,6},{8,11},{9,8},{10,9... | collective-permute-start | bytes 442376 | tf_op jit(solution)/shard_map/ppermute | solution.py:42
  181.6 1.4 collective-permute-start.31
  183.0 2.6 %collective-permute-done.29 = bf16[96,768]{1,0:T(8,128)(2,1)S(1)} collective-permute-done((bf16[96,768]{1,0:T(8,128)(2,1)}, bf16[96,768]{1,0:T(8,128)(2,1)S(1)}, u32[]{:S(2)}, u32[]{:S(2)}) %collective-permute-start.29) | collective-permute-done | bytes 147488 | tf_op jit(solution)/shard_map/ppermute | solution.py:42
  185.6 2.6 %collective-permute-done.30 = bf16[96,768]{1,0:T(8,128)(2,1)S(1)} collective-permute-done((bf16[96,768]{1,0:T(8,128)(2,1)}, bf16[96,768]{1,0:T(8,128)(2,1)S(1)}, u32[]{:S(2)}, u32[]{:S(2)}) %collective-permute-start.30) | collective-permute-done | bytes 147488 | tf_op jit(solution)/shard_map/ppermute | solution.py:42
  188.2 1.8 collective-permute-done.31
  190.0 1.0 add_convert_fusion.1
  191.0 2.9 %collective-permute-start.32 = (bf16[96,768]{1,0:T(8,128)(2,1)S(1)}, bf16[96,768]{1,0:T(8,128)(2,1)S(1)}, u32[]{:S(2)}, u32[]{:S(2)}) collective-permute-start(bf16[96,768]{1,0:T(8,128)(2,1)S(1)} %add_convert_fusion.1), channel_id=1, source_target_pairs={{0,4},{1,5},{2,6},{3,7},{4,0},{5,1},{6,2},{7,3},{8,12},{9,13},{10,... | collective-permute-start | bytes 442376 | tf_op jit(solution)/shard_map/ppermute | solution.py:42
  193.9 3.1 %collective-permute-done.32 = bf16[96,768]{1,0:T(8,128)(2,1)S(1)} collective-permute-done((bf16[96,768]{1,0:T(8,128)(2,1)S(1)}, bf16[96,768]{1,0:T(8,128)(2,1)S(1)}, u32[]{:S(2)}, u32[]{:S(2)}) %collective-permute-start.32) | collective-permute-done | bytes 147488 | tf_op jit(solution)/shard_map/ppermute | solution.py:42
  197.1 0.8 collective-permute-start.33
  197.9 2.5 %collective-permute-start.34 = (bf16[96,768]{1,0:T(8,128)(2,1)S(1)}, bf16[96,768]{1,0:T(8,128)(2,1)S(1)}, u32[]{:S(2)}, u32[]{:S(2)}) collective-permute-start(bf16[96,768]{1,0:T(8,128)(2,1)S(1)} %add_convert_fusion.refs_0_), channel_id=1, source_target_pairs={{0,3},{1,0},{2,1},{3,2},{4,7},{5,4},{6,5},{7,6},{8,11},{9,8},{10,9... | collective-permute-start | bytes 442376 | tf_op jit(solution)/shard_map/ppermute | solution.py:42
  200.4 1.1 collective-permute-start.35
  201.5 3.6 %join.2 = (bf16[384,1536]{1,0:T(8,128)(2,1)}, bf16[384,1536]{1,0:T(8,128)(2,1)}) custom-call(s32[44]{0:T(128)} %concatenate.3.info.place.spots, bf16[2,384,768]{2,1,0:T(8,128)(2,1)} %get-tuple-element.40.rest_0_.own_ref, bf16[2,384,768]{2,1,0:T(8,128)(2,1)} %copy-done.10, bf16[2,384,768]{2,1,0:T(8,128)(2,1)} %copy-done.11), custom_call_target="tpu_custom_call" | custom-call | flops 1000 | bytes 1000 | tf_op jit(solution)/shard_map/join/pallas_call | solution.py:251
  205.1 3.6 %join.3 = (bf16[384,1536]{1,0:T(8,128)(2,1)}, bf16[384,1536]{1,0:T(8,128)(2,1)}) custom-call(s32[44]{0:T(128)} %concatenate.3.info.place.spots, bf16[2,384,768]{2,1,0:T(8,128)(2,1)} %get-tuple-element.46.refs_8_.own_ref, bf16[2,384,768]{2,1,0:T(8,128)(2,1)} %copy-done.12, ...), custom_call_target="tpu_custom_call", output_to_operand_aliasing={{0}: (4, {}), {1}: (5, {})} | custom-call | flops 1000 | bytes 1000 | tf_op jit(solution)/shard_map/join/pallas_call | solution.py:251
  208.8 1.0 copy-done.15
  210.1 4.6 %meet.1.refs_4_ = bf16[384,3072]{1,0:T(8,128)(2,1)} custom-call(bf16[384,3072]{1,0:T(8,128)(2,1)} %get-tuple-element.50.near_ref, bf16[384,1536]{1,0:T(8,128)(2,1)} %copy-done.15, bf16[384,1536]{1,0:T(8,128)(2,1)} %copy-done.16), custom_call_target="tpu_custom_call" | custom-call | flops 1000 | bytes 1000 | tf_op jit(solution)/shard_map/meet/pallas_call | solution.py:392
  216.1 2.2 %place_columns.1 = f32[96,3072]{1,0:T(8,128)} custom-call(s32[44]{0:T(128)} %concatenate.3.info.place.spots, bf16[96,768]{1,0:T(8,128)(2,1)} %copy-done.19, bf16[96,768]{1,0:T(8,128)(2,1)} %copy-done.22, bf16[96,768]{1,0:T(8,128)(2,1)} %copy-done.23, bf16[96,768]{1,0:T(8,128)(2,1)} %copy-done.24, bf16[384,3072]{1,0:T(8,128)(2,1)} %meet.1.refs_4_), custom_call_target="tpu_custom_call" | custom-call | flops 1000 | bytes 1000 | tf_op jit(solution)/shard_map/place_columns/pallas_call | solution.py:473
  (88 shorter events, 5.7 us)
Async XLA Ops:
  0.6 25.0 %collective-permute-start.3 = (bf16[384,3072]{1,0:T(8,128)(2,1)}, bf16[384,3072]{1,0:T(8,128)(2,1)}, u32[]{:S(2)}, u32[]{:S(2)}) collective-permute-start(bf16[384,3072]{1,0:T(8,128)(2,1)} %bitcast.46), channel_id=1, source_target_pairs={{0,8},{1,9},{2,10},{3,11},{4,12},{5,13},{6,14},{7,15},{8,0},{9,1},... | collective-permute-start | bytes 7077896 | tf_op jit(solution)/shard_map/ppermute | solution.py:42
  0.7 17.2 %collective-permute-start.9 = (bf16[96,3072]{1,0:T(8,128)(2,1)}, bf16[96,3072]{1,0:T(8,128)(2,1)S(1)}, u32[]{:S(2)}, u32[]{:S(2)}) collective-permute-start(bf16[96,3072]{1,0:T(8,128)(2,1)} %refs_4_.1), channel_id=1, source_target_pairs={{0,68},{1,69},{2,70},{3,71},{4,64},{5,65},{6,66},{7,67},{8,76},{9,... | collective-permute-start | bytes 1769480 | tf_op jit(solution)/shard_map/ppermute | solution.py:42
  3.6 17.9 %collective-permute-start.2 = (bf16[96,3072]{1,0:T(8,128)(2,1)}, bf16[96,3072]{1,0:T(8,128)(2,1)S(1)}, u32[]{:S(2)}, u32[]{:S(2)}) collective-permute-start(bf16[96,3072]{1,0:T(8,128)(2,1)} %refs_4_.1), channel_id=1, source_target_pairs={{0,16},{1,17},{2,18},{3,19},{4,20},{5,21},{6,22},{7,23},{8,24},{9,... | collective-permute-start | bytes 1769480 | tf_op jit(solution)/shard_map/ppermute | solution.py:42
  7.0 9.0 %copy-start = (bf16[1,384,3072]{2,1,0:T(8,128)(2,1)S(1)}, bf16[1,384,3072]{2,1,0:T(8,128)(2,1)}, u32[]{:S(2)}) copy-start(bf16[1,384,3072]{2,1,0:T(8,128)(2,1)} %param.10) | copy-start | bytes 7077892
  10.1 29.0 %collective-permute-start = (bf16[2,384,768]{2,1,0:T(8,128)(2,1)}, bf16[2,384,768]{2,1,0:T(8,128)(2,1)}, u32[]{:S(2)}, u32[]{:S(2)}) collective-permute-start(bf16[2,384,768]{2,1,0:T(8,128)(2,1)} %window.2), channel_id=1, source_target_pairs={{0,1},{1,2},{2,3},{3,4},{4,5},{5,6},{6,7},{8,9},{9,10},{10,11},{11... | collective-permute-start | bytes 3538952 | tf_op jit(solution)/shard_map/ppermute | solution.py:78
  14.7 29.7 %collective-permute-start.1 = (bf16[2,384,768]{2,1,0:T(8,128)(2,1)}, bf16[2,384,768]{2,1,0:T(8,128)(2,1)}, u32[]{:S(2)}, u32[]{:S(2)}) collective-permute-start(bf16[2,384,768]{2,1,0:T(8,128)(2,1)} %window.2), channel_id=1, source_target_pairs={{1,0},{2,1},{3,2},{4,3},{5,4},{6,5},{7,6},{9,8},{10,9},{11,10},{12... | collective-permute-start | bytes 3538952 | tf_op jit(solution)/shard_map/ppermute | solution.py:82
  17.9 0.8 copy-start.2
  18.7 75.7 %collective-permute-start.17 = (bf16[384,3072]{1,0:T(8,128)(2,1)}, bf16[384,3072]{1,0:T(8,128)(2,1)S(1)}, u32[]{:S(2)}, u32[]{:S(2)}) collective-permute-start(bf16[384,3072]{1,0:T(8,128)(2,1)} %hold.10), channel_id=1, source_target_pairs={{0,68},{1,69},{2,70},{3,71},{4,64},{5,65},{6,66},{7,67},{8,76},{9,... | collective-permute-start | bytes 7077896 | tf_op jit(solution)/shard_map/ppermute | solution.py:42
  21.6 4.0 %copy-start.1 = (bf16[96,3072]{1,0:T(8,128)(2,1)}, bf16[96,3072]{1,0:T(8,128)(2,1)S(1)}, u32[]{:S(2)}) copy-start(bf16[96,3072]{1,0:T(8,128)(2,1)S(1)} %collective-permute-done.2.x_ref) | copy-start | bytes 1769476
  21.6 16.6 %collective-permute-start.4 = (bf16[96,3072]{1,0:T(8,128)(2,1)}, bf16[96,3072]{1,0:T(8,128)(2,1)S(1)}, u32[]{:S(2)}, u32[]{:S(2)}) collective-permute-start(bf16[96,3072]{1,0:T(8,128)(2,1)} %refs_4_.1), channel_id=1, source_target_pairs={{0,48},{1,49},{2,50},{3,51},{4,52},{5,53},{6,54},{7,55},{8,56},{9,... | collective-permute-start | bytes 1769480 | tf_op jit(solution)/shard_map/ppermute | solution.py:42
  25.6 25.4 %collective-permute-start.7 = (bf16[96,3072]{1,0:T(8,128)(2,1)}, bf16[96,3072]{1,0:T(8,128)(2,1)}, u32[]{:S(2)}, u32[]{:S(2)}) collective-permute-start(bf16[96,3072]{1,0:T(8,128)(2,1)} %hold.6.rest_0_.rest_2_.refs_1_.refs_5_), channel_id=1, source_target_pairs={{0,16},{1,17},{2,18},{3,19},{4,20},{5,21},{6,22},{7,23},{8,24},{9,... | collective-permute-start | bytes 1769480 | tf_op jit(solution)/shard_map/ppermute | solution.py:42
  38.1 6.2 %copy-start.7 = (bf16[96,3072]{1,0:T(8,128)(2,1)}, bf16[96,3072]{1,0:T(8,128)(2,1)S(1)}, u32[]{:S(2)}) copy-start(bf16[96,3072]{1,0:T(8,128)(2,1)S(1)} %collective-permute-done.4.rest_3_.refs_2_.refs_6_) | copy-start | bytes 1769476
  44.4 1.9 copy-start.4
  44.4 24.2 %collective-permute-start.10 = (bf16[96,3072]{1,0:T(8,128)(2,1)}, bf16[96,3072]{1,0:T(8,128)(2,1)}, u32[]{:S(2)}, u32[]{:S(2)}) collective-permute-start(bf16[96,3072]{1,0:T(8,128)(2,1)} %hold.8.refs_0_.refs_8_), channel_id=1, source_target_pairs={{0,16},{1,17},{2,18},{3,19},{4,20},{5,21},{6,22},{7,23},{8,24},{9,... | collective-permute-start | bytes 1769480 | tf_op jit(solution)/shard_map/ppermute | solution.py:42
  46.3 39.2 %collective-permute-start.5 = (bf16[2,384,768]{2,1,0:T(8,128)(2,1)S(1)}, bf16[2,384,768]{2,1,0:T(8,128)(2,1)}, u32[]{:S(2)}, u32[]{:S(2)}) collective-permute-start(bf16[2,384,768]{2,1,0:T(8,128)(2,1)S(1)} %copy-done.4), channel_id=1, source_target_pairs={{0,1},{1,2},{2,3},{3,4},{4,5},{5,6},{6,7},{8,9},{9,10},{10,11},{11... | collective-permute-start | bytes 3538952 | tf_op jit(solution)/shard_map/ppermute | solution.py:78
  49.7 35.8 %collective-permute-start.6 = (bf16[2,384,768]{2,1,0:T(8,128)(2,1)S(1)}, bf16[2,384,768]{2,1,0:T(8,128)(2,1)}, u32[]{:S(2)}, u32[]{:S(2)}) collective-permute-start(bf16[2,384,768]{2,1,0:T(8,128)(2,1)S(1)} %copy-done.4), channel_id=1, source_target_pairs={{1,0},{2,1},{3,2},{4,3},{5,4},{6,5},{7,6},{9,8},{10,9},{11,10},{12... | collective-permute-start | bytes 3538952 | tf_op jit(solution)/shard_map/ppermute | solution.py:82
  51.0 19.5 %collective-permute-start.11 = (bf16[96,3072]{1,0:T(8,128)(2,1)}, bf16[96,3072]{1,0:T(8,128)(2,1)}, u32[]{:S(2)}, u32[]{:S(2)}) collective-permute-start(bf16[96,3072]{1,0:T(8,128)(2,1)} %hold.8.refs_0_.refs_8_), channel_id=1, source_target_pairs={{0,48},{1,49},{2,50},{3,51},{4,52},{5,53},{6,54},{7,55},{8,56},{9,... | collective-permute-start | bytes 1769480 | tf_op jit(solution)/shard_map/ppermute | solution.py:42
  52.8 8.3 %copy-start.3 = (bf16[96,3072]{1,0:T(8,128)(2,1)S(1)}, bf16[96,3072]{1,0:T(8,128)(2,1)}, u32[]{:S(2)}) copy-start(bf16[96,3072]{1,0:T(8,128)(2,1)} %hold.8.refs_0_.refs_8_) | copy-start | bytes 1769476
  68.5 16.9 %collective-permute-start.12 = (bf16[96,3072]{1,0:T(8,128)(2,1)}, bf16[96,3072]{1,0:T(8,128)(2,1)S(1)}, u32[]{:S(2)}, u32[]{:S(2)}) collective-permute-start(bf16[96,3072]{1,0:T(8,128)(2,1)} %hold.9), channel_id=1, source_target_pairs={{0,32},{1,33},{2,34},{3,35},{4,36},{5,37},{6,38},{7,39},{8,40},{9,... | collective-permute-start | bytes 1769480 | tf_op jit(solution)/shard_map/ppermute | solution.py:42
  70.5 1.9 collective-permute-start.8
  85.5 0.8 copy-start.8
  94.5 1.4 copy-start.5
  95.9 1.1 copy-start.9
  95.9 38.7 %collective-permute-start.18 = (bf16[384,3072]{1,0:T(8,128)(2,1)}, bf16[384,3072]{1,0:T(8,128)(2,1)}, u32[]{:S(2)}, u32[]{:S(2)}) collective-permute-start(bf16[384,3072]{1,0:T(8,128)(2,1)} %hold.11.refs_6_), channel_id=1, source_target_pairs={{0,8},{1,9},{2,10},{3,11},{4,12},{5,13},{6,14},{7,15},{8,0},{9,1},... | collective-permute-start | bytes 7077896 | tf_op jit(solution)/shard_map/ppermute | solution.py:42
  97.7 7.1 %copy-start.6 = (bf16[768,384]{1,0:T(8,128)(2,1)S(1)}, bf16[768,384]{1,0:T(8,128)(2,1)}, u32[]{:S(2)}) copy-start(bf16[768,384]{1,0:T(8,128)(2,1)} %get-tuple-element.41.rest_0_.refs_6_.attn_ref) | copy-start | bytes 1769476
  97.7 12.7 %collective-permute-start.13 = (bf16[384,384]{1,0:T(8,128)(2,1)S(1)}, bf16[384,384]{1,0:T(8,128)(2,1)S(1)}, u32[]{:S(2)}, u32[]{:S(2)}) collective-permute-start(bf16[384,384]{1,0:T(8,128)(2,1)S(1)} %bitcast.65), channel_id=1, source_target_pairs={{0,8},{1,9},{2,10},{3,11},{4,12},{5,13},{6,14},{7,15},{8,0},{9,1},... | collective-permute-start | bytes 884744 | tf_op jit(solution)/shard_map/ppermute | solution.py:42
  104.5 7.3 %collective-permute-start.19 = (bf16[384,384]{1,0:T(8,128)(2,1)}, bf16[384,384]{1,0:T(8,128)(2,1)S(1)}, u32[]{:S(2)}, u32[]{:S(2)}) collective-permute-start(bf16[384,384]{1,0:T(8,128)(2,1)} %get-tuple-element.43), channel_id=1, source_target_pairs={{0,8},{1,9},{2,10},{3,11},{4,12},{5,13},{6,14},{7,15},{8,0},{9,1},... | collective-permute-start | bytes 884744 | tf_op jit(solution)/shard_map/ppermute | solution.py:42
  105.6 25.3 %copy-start.17 = (bf16[4,1,96,384]{3,2,1,0:T(8,128)(2,1)}, bf16[4,1,96,384]{3,2,1,0:T(8,128)(2,1)S(1)}, u32[]{:S(2)}) copy-start(bf16[4,1,96,384]{3,2,1,0:T(8,128)(2,1)S(1)} %get-tuple-element.68) | copy-start | bytes 884740
  105.6 11.5 %collective-permute-start.14 = (bf16[384,384]{1,0:T(8,128)(2,1)}, bf16[384,384]{1,0:T(8,128)(2,1)S(1)}, u32[]{:S(2)}, u32[]{:S(2)}) collective-permute-start(bf16[384,384]{1,0:T(8,128)(2,1)} %bitcast.21), channel_id=1, source_target_pairs={{0,8},{1,9},{2,10},{3,11},{4,12},{5,13},{6,14},{7,15},{8,0},{9,1},... | collective-permute-start | bytes 884744 | tf_op jit(solution)/shard_map/ppermute | solution.py:42
  105.8 38.5 %collective-permute-start.20 = (bf16[2,384,768]{2,1,0:T(8,128)(2,1)}, bf16[2,384,768]{2,1,0:T(8,128)(2,1)S(1)}, u32[]{:S(2)}, u32[]{:S(2)}) collective-permute-start(bf16[2,384,768]{2,1,0:T(8,128)(2,1)} %get-tuple-element.48), channel_id=1, source_target_pairs={{0,1},{1,2},{2,3},{3,4},{4,5},{5,6},{6,7},{8,9},{9,10},{10,11},{11... | collective-permute-start | bytes 3538952 | tf_op jit(solution)/shard_map/ppermute | solution.py:78
  110.4 20.5 %copy-start.13 = (bf16[384,384]{1,0:T(8,128)(2,1)}, bf16[384,384]{1,0:T(8,128)(2,1)S(1)}, u32[]{:S(2)}) copy-start(bf16[384,384]{1,0:T(8,128)(2,1)S(1)} %collective-permute-done.13.refs_1_.refs_2_) | copy-start | bytes 884740
  110.4 36.5 %collective-permute-start.21 = (bf16[2,384,768]{2,1,0:T(8,128)(2,1)}, bf16[2,384,768]{2,1,0:T(8,128)(2,1)S(1)}, u32[]{:S(2)}, u32[]{:S(2)}) collective-permute-start(bf16[2,384,768]{2,1,0:T(8,128)(2,1)} %get-tuple-element.49), channel_id=1, source_target_pairs={{1,0},{2,1},{3,2},{4,3},{5,4},{6,5},{7,6},{9,8},{10,9},{11,10},{12... | collective-permute-start | bytes 3538952 | tf_op jit(solution)/shard_map/ppermute | solution.py:82
  111.8 5.3 %copy-start.20 = (bf16[384,384]{1,0:T(8,128)(2,1)}, bf16[384,384]{1,0:T(8,128)(2,1)S(1)}, u32[]{:S(2)}) copy-start(bf16[384,384]{1,0:T(8,128)(2,1)S(1)} %collective-permute-done.19.theirs_ref) | copy-start | bytes 884740
  111.8 19.2 %collective-permute-start.15 = (bf16[384,384]{1,0:T(8,128)(2,1)S(1)}, bf16[384,384]{1,0:T(8,128)(2,1)S(1)}, u32[]{:S(2)}, u32[]{:S(2)}) collective-permute-start(bf16[384,384]{1,0:T(8,128)(2,1)S(1)} %bitcast.60), channel_id=1, source_target_pairs={{0,68},{1,69},{2,70},{3,71},{4,64},{5,65},{6,66},{7,67},{8,76},{9,... | collective-permute-start | bytes 884744 | tf_op jit(solution)/shard_map/ppermute | solution.py:42
  117.1 0.7 copy-start.14
  117.1 16.2 %collective-permute-start.16 = (bf16[384,384]{1,0:T(8,128)(2,1)}, bf16[384,384]{1,0:T(8,128)(2,1)}, u32[]{:S(2)}, u32[]{:S(2)}) collective-permute-start(bf16[384,384]{1,0:T(8,128)(2,1)} %bitcast.21), channel_id=1, source_target_pairs={{0,76},{1,77},{2,78},{3,79},{4,72},{5,73},{6,74},{7,75},{8,68},{9,... | collective-permute-start | bytes 884744 | tf_op jit(solution)/shard_map/ppermute | solution.py:42
  131.0 0.7 copy-start.21
  131.7 30.0 %collective-permute-start.24 = (bf16[2,384,768]{2,1,0:T(8,128)(2,1)}, bf16[2,384,768]{2,1,0:T(8,128)(2,1)S(1)}, u32[]{:S(2)}, u32[]{:S(2)}) collective-permute-start(bf16[2,384,768]{2,1,0:T(8,128)(2,1)} %get-tuple-element.54), channel_id=1, source_target_pairs={{0,1},{1,2},{2,3},{3,4},{4,5},{5,6},{6,7},{8,9},{9,10},{10,11},{11... | collective-permute-start | bytes 3538952 | tf_op jit(solution)/shard_map/ppermute | solution.py:78
  133.3 32.6 %collective-permute-start.25 = (bf16[2,384,768]{2,1,0:T(8,128)(2,1)}, bf16[2,384,768]{2,1,0:T(8,128)(2,1)}, u32[]{:S(2)}, u32[]{:S(2)}) collective-permute-start(bf16[2,384,768]{2,1,0:T(8,128)(2,1)} %get-tuple-element.55), channel_id=1, source_target_pairs={{1,0},{2,1},{3,2},{4,3},{5,4},{6,5},{7,6},{9,8},{10,9},{11,10},{12... | collective-permute-start | bytes 3538952 | tf_op jit(solution)/shard_map/ppermute | solution.py:82
  143.6 29.7 %collective-permute-start.26 = (bf16[96,3072]{1,0:T(8,128)(2,1)}, bf16[96,3072]{1,0:T(8,128)(2,1)S(1)}, u32[]{:S(2)}, u32[]{:S(2)}) collective-permute-start(bf16[96,3072]{1,0:T(8,128)(2,1)} %get-tuple-element.60), channel_id=1, source_target_pairs={{0,16},{1,17},{2,18},{3,19},{4,20},{5,21},{6,22},{7,23},{8,24},{9,... | collective-permute-start | bytes 1769480 | tf_op jit(solution)/shard_map/ppermute | solution.py:42
  144.3 3.0 %copy-start.10 = (bf16[2,384,768]{2,1,0:T(8,128)(2,1)}, bf16[2,384,768]{2,1,0:T(8,128)(2,1)S(1)}, u32[]{:S(2)}) copy-start(bf16[2,384,768]{2,1,0:T(8,128)(2,1)S(1)} %collective-permute-done.20.refs_13_.a_ref) | copy-start | bytes 3538948
  144.3 29.0 %collective-permute-start.27 = (bf16[96,3072]{1,0:T(8,128)(2,1)}, bf16[96,3072]{1,0:T(8,128)(2,1)}, u32[]{:S(2)}, u32[]{:S(2)}) collective-permute-start(bf16[96,3072]{1,0:T(8,128)(2,1)} %get-tuple-element.61), channel_id=1, source_target_pairs={{0,48},{1,49},{2,50},{3,51},{4,52},{5,53},{6,54},{7,55},{8,56},{9,... | collective-permute-start | bytes 1769480 | tf_op jit(solution)/shard_map/ppermute | solution.py:42
  146.9 1.0 copy-start.11
  146.9 26.4 %collective-permute-start.28 = (bf16[96,3072]{1,0:T(8,128)(2,1)}, bf16[96,3072]{1,0:T(8,128)(2,1)}, u32[]{:S(2)}, u32[]{:S(2)}) collective-permute-start(bf16[96,3072]{1,0:T(8,128)(2,1)} %get-tuple-element.62), channel_id=1, source_target_pairs={{0,32},{1,33},{2,34},{3,35},{4,36},{5,37},{6,38},{7,39},{8,40},{9,... | collective-permute-start | bytes 1769480 | tf_op jit(solution)/shard_map/ppermute | solution.py:42
  161.7 11.7 %copy-start.12 = (bf16[2,384,768]{2,1,0:T(8,128)(2,1)}, bf16[2,384,768]{2,1,0:T(8,128)(2,1)S(1)}, u32[]{:S(2)}) copy-start(bf16[2,384,768]{2,1,0:T(8,128)(2,1)S(1)} %collective-permute-done.24.a_ref.refs_4_) | copy-start | bytes 3538948
  161.7 47.1 %collective-permute-start.22 = (bf16[384,1536]{1,0:T(8,128)(2,1)}, bf16[384,1536]{1,0:T(8,128)(2,1)S(1)}, u32[]{:S(2)}, u32[]{:S(2)}) collective-permute-start(bf16[384,1536]{1,0:T(8,128)(2,1)} %get-tuple-element.51), channel_id=1, source_target_pairs={{0,8},{1,9},{2,10},{3,11},{4,12},{5,13},{6,14},{7,15},{8,0},{9,1},... | collective-permute-start | bytes 3538952 | tf_op jit(solution)/shard_map/ppermute | solution.py:42
  165.9 42.9 %collective-permute-start.23 = (bf16[384,1536]{1,0:T(8,128)(2,1)}, bf16[384,1536]{1,0:T(8,128)(2,1)S(1)}, u32[]{:S(2)}, u32[]{:S(2)}) collective-permute-start(bf16[384,1536]{1,0:T(8,128)(2,1)} %get-tuple-element.52), channel_id=1, source_target_pairs={{0,8},{1,9},{2,10},{3,11},{4,12},{5,13},{6,14},{7,15},{8,0},{9,1},... | collective-permute-start | bytes 3538952 | tf_op jit(solution)/shard_map/ppermute | solution.py:42
  173.3 0.8 copy-start.18
  176.8 8.9 %collective-permute-start.29 = (bf16[96,768]{1,0:T(8,128)(2,1)}, bf16[96,768]{1,0:T(8,128)(2,1)S(1)}, u32[]{:S(2)}, u32[]{:S(2)}) collective-permute-start(bf16[96,768]{1,0:T(8,128)(2,1)} %get-tuple-element.64), channel_id=1, source_target_pairs={{0,1},{1,2},{2,3},{3,0},{4,5},{5,6},{6,7},{7,4},{8,9},{9,10},{10,1... | collective-permute-start | bytes 442376 | tf_op jit(solution)/shard_map/ppermute | solution.py:42
  179.1 9.0 %collective-permute-start.30 = (bf16[96,768]{1,0:T(8,128)(2,1)}, bf16[96,768]{1,0:T(8,128)(2,1)S(1)}, u32[]{:S(2)}, u32[]{:S(2)}) collective-permute-start(bf16[96,768]{1,0:T(8,128)(2,1)} %get-tuple-element.65), channel_id=1, source_target_pairs={{0,3},{1,0},{2,1},{3,2},{4,7},{5,4},{6,5},{7,6},{8,11},{9,8},{10,9... | collective-permute-start | bytes 442376 | tf_op jit(solution)/shard_map/ppermute | solution.py:42
  181.6 8.4 %collective-permute-start.31 = (bf16[96,768]{1,0:T(8,128)(2,1)}, bf16[96,768]{1,0:T(8,128)(2,1)S(1)}, u32[]{:S(2)}, u32[]{:S(2)}) collective-permute-start(bf16[96,768]{1,0:T(8,128)(2,1)} %get-tuple-element.66), channel_id=1, source_target_pairs={{0,2},{1,3},{2,0},{3,1},{4,6},{5,7},{6,4},{7,5},{8,10},{9,11},{10,... | collective-permute-start | bytes 442376 | tf_op jit(solution)/shard_map/ppermute | solution.py:42
  191.0 6.0 %collective-permute-start.32 = (bf16[96,768]{1,0:T(8,128)(2,1)S(1)}, bf16[96,768]{1,0:T(8,128)(2,1)S(1)}, u32[]{:S(2)}, u32[]{:S(2)}) collective-permute-start(bf16[96,768]{1,0:T(8,128)(2,1)S(1)} %add_convert_fusion.1), channel_id=1, source_target_pairs={{0,4},{1,5},{2,6},{3,7},{4,0},{5,1},{6,2},{7,3},{8,12},{9,13},{10,... | collective-permute-start | bytes 442376 | tf_op jit(solution)/shard_map/ppermute | solution.py:42
  197.1 8.0 %copy-start.19 = (bf16[96,768]{1,0:T(8,128)(2,1)}, bf16[96,768]{1,0:T(8,128)(2,1)S(1)}, u32[]{:S(2)}) copy-start(bf16[96,768]{1,0:T(8,128)(2,1)S(1)} %add_convert_fusion.refs_0_) | copy-start | bytes 442372
  197.1 17.6 %collective-permute-start.33 = (bf16[96,768]{1,0:T(8,128)(2,1)S(1)}, bf16[96,768]{1,0:T(8,128)(2,1)S(1)}, u32[]{:S(2)}, u32[]{:S(2)}) collective-permute-start(bf16[96,768]{1,0:T(8,128)(2,1)S(1)} %add_convert_fusion.refs_0_), channel_id=1, source_target_pairs={{0,1},{1,2},{2,3},{3,0},{4,5},{5,6},{6,7},{7,4},{8,9},{9,10},{10,1... | collective-permute-start | bytes 442376 | tf_op jit(solution)/shard_map/ppermute | solution.py:42
  197.9 16.8 %collective-permute-start.34 = (bf16[96,768]{1,0:T(8,128)(2,1)S(1)}, bf16[96,768]{1,0:T(8,128)(2,1)S(1)}, u32[]{:S(2)}, u32[]{:S(2)}) collective-permute-start(bf16[96,768]{1,0:T(8,128)(2,1)S(1)} %add_convert_fusion.refs_0_), channel_id=1, source_target_pairs={{0,3},{1,0},{2,1},{3,2},{4,7},{5,4},{6,5},{7,6},{8,11},{9,8},{10,9... | collective-permute-start | bytes 442376 | tf_op jit(solution)/shard_map/ppermute | solution.py:42
  200.4 14.3 %collective-permute-start.35 = (bf16[96,768]{1,0:T(8,128)(2,1)S(1)}, bf16[96,768]{1,0:T(8,128)(2,1)S(1)}, u32[]{:S(2)}, u32[]{:S(2)}) collective-permute-start(bf16[96,768]{1,0:T(8,128)(2,1)S(1)} %add_convert_fusion.refs_0_), channel_id=1, source_target_pairs={{0,2},{1,3},{2,0},{3,1},{4,6},{5,7},{6,4},{7,5},{8,10},{9,11},{10,... | collective-permute-start | bytes 442376 | tf_op jit(solution)/shard_map/ppermute | solution.py:42
  208.7 1.0 copy-start.15
  208.7 1.4 copy-start.16
  214.7 0.7 copy-start.22
  214.7 0.7 copy-start.23
  215.5 0.6 copy-start.24
